TPU v7x, 128 devices: a whole 4x4x4 slice. The times are simulated.
128 devices in a mesh: section: 2 (over core), seq: 16 (over y, x), fsdp: 4 (over z).
Axes of the slice: x: 4, y: 4, z: 4, core: 2. Of those that a mesh axis runs over, the one named last changes fastest.
Arguments:
- hidden_in: bfloat16 [3, 4, 2048, 640], P(None, 'fsdp', 'seq'), may hold values from -6 to 6
- positions: int32 [3, 4, 2048], P(None, 'fsdp', 'seq'), may hold values from 0 to 4093, as said below
- segments: int32 [3, 4, 2048], P(None, 'fsdp'), may hold values from 0 to 4, as said below
- cotangent: bfloat16 [3, 4, 2048, 640], P(None, 'fsdp', 'seq'), may hold values from -6 to 6
- query_weight: bfloat16 [2, 640, 1024], P('section', 'fsdp'), may hold values from -0.25 to 0.25
- key_weight: bfloat16 [2, 640, 256], P('section', 'fsdp'), may hold values from -0.25 to 0.25
- value_weight: bfloat16 [2, 640, 256], P('section', 'fsdp'), may hold values from -0.25 to 0.25
- output_weight: bfloat16 [2, 1024, 640], P('section', 'fsdp'), may hold values from -0.1875 to 0.1875
- gate_weight: bfloat16 [2, 640, 2048], P('section', 'fsdp'), may hold values from -0.25 to 0.25
- up_weight: bfloat16 [2, 640, 2048], P('section', 'fsdp'), may hold values from -0.25 to 0.25
- down_weight: bfloat16 [2, 2048, 640], P('section', 'fsdp'), may hold values from -0.125 to 0.125
- pre_gain: bfloat16 [2, 640], P('section', 'fsdp'), may hold values from 0.5 to 1.5
- query_gain: bfloat16 [2, 256], P('section', 'fsdp'), may hold values from 0.5 to 1.5
- key_gain: bfloat16 [2, 256], P('section', 'fsdp'), may hold values from 0.5 to 1.5
- mix_gain: bfloat16 [2, 640], P('section', 'fsdp'), may hold values from 0.5 to 1.5
- ffn_gain: bfloat16 [2, 640], P('section', 'fsdp'), may hold values from 0.5 to 1.5
- out_gain: bfloat16 [2, 640], P('section', 'fsdp'), may hold values from 0.5 to 1.5
Outputs:
- section_outputs: bfloat16 [2, 3, 4, 2048, 640], P('section', None, 'fsdp', 'seq')
- input_grads: float32 [2, 3, 4, 2048, 640], P('section', None, 'fsdp', 'seq')
- query_grad: float32 [2, 640, 1024], P('section', 'fsdp')
- key_grad: float32 [2, 640, 256], P('section', 'fsdp')
- value_grad: float32 [2, 640, 256], P('section', 'fsdp')
- output_grad: float32 [2, 1024, 640], P('section', 'fsdp')
- gate_grad: float32 [2, 640, 2048], P('section', 'fsdp')
- up_grad: float32 [2, 640, 2048], P('section', 'fsdp')
- down_grad: float32 [2, 2048, 640], P('section', 'fsdp')
- pre_gain_grad: float32 [2, 640], P('section', 'fsdp')
- query_gain_grad: float32 [2, 256], P('section', 'fsdp')
- key_gain_grad: float32 [2, 256], P('section', 'fsdp')
- mix_gain_grad: float32 [2, 640], P('section', 'fsdp')
- ffn_gain_grad: float32 [2, 640], P('section', 'fsdp')
- out_gain_grad: float32 [2, 640], P('section', 'fsdp')
Inputs may be any that keep to these rules, and one draw needn't show every extreme that they name: `segments`: segment numbers never fall along a sequence; in every sequence one segment begins within its first 128 tokens and ends within its last 128. `positions`: within a segment the position rises by one from token to token.
All inputs are finite; a program needn't handle non-finite values.
Results may differ from a plain program's by a relative error of at most 0.029.
Values may be sent and summed in bfloat16 or wider, within the bound.
No kernel may reach another device: no remote copies, remote signals or barrier semaphores. Data moves between devices by JAX's collectives and lax.ppermute only.
A program may use at most 256 MiB of HBM per device.

v0:
```python
import jax
import jax.numpy as jnp
from jax import lax
from jax.sharding import PartitionSpec as P

WINDOW = 512


EPSILON = 1e-06
ROPE_BASE = 10000.0


def shifted(x, axis, by):
    count = lax.axis_size(axis)
    pairs = [(i, i + by) for i in range(count) if 0 <= i + by < count]
    return lax.ppermute(x, axis, pairs)


def shortened(x):

    def short(part):
        return part.astype(jnp.bfloat16) if part.dtype == jnp.float32 else part

    return jax.tree.map(short, x)


def normalize(values, gain):
    return values * lax.rsqrt(jnp.mean(values * values, axis=-1, keepdims=True) + EPSILON) * gain


def rotate(values, places):
    half = values.shape[-1] // 2
    exponent = jnp.arange(half).astype(jnp.float32) * (2.0 / values.shape[-1])
    freqs = ROPE_BASE ** (-exponent)
    angle = places.astype(jnp.float32)[:, None] * freqs[None, :]
    cosine = jnp.cos(angle)
    sine = jnp.sin(angle)
    if values.ndim == 3:
        cosine = cosine[:, None, :]
        sine = sine[:, None, :]
    former = values[..., :half]
    latter = values[..., half:]
    return jnp.concatenate(
        [former * cosine - latter * sine, latter * cosine + former * sine], axis=-1
    )


def product(left, right):
    return jnp.dot(left, right, preferred_element_type=jnp.float32)


def inner_rows(left, right):
    return lax.dot_general(
        left, right, (((0,), (0,)), ((), ())), preferred_element_type=jnp.float32
    )


def against(left, right):
    return lax.dot_general(
        left, right, (((1,), (1,)), ((), ())), preferred_element_type=jnp.float32
    )


def window_mask(segment_row, seq_index, shard, hops):
    anchor = seq_index * shard
    padded = jnp.concatenate([jnp.full((hops * shard,), -1, jnp.int32), segment_row])
    query_seg = lax.dynamic_slice_in_dim(segment_row, anchor, shard, 0)
    key_seg = lax.dynamic_slice_in_dim(padded, anchor, (hops + 1) * shard, 0)
    gap = (jnp.arange(shard, dtype=jnp.int32) + hops * shard)[:, None] - jnp.arange(
        (hops + 1) * shard, dtype=jnp.int32
    )[None, :]
    return (gap >= 0) & (gap < WINDOW) & (query_seg[:, None] == key_seg[None, :])


def scores(query_rot, keys_all, allowed):
    raw = jnp.einsum("qhd,kd->hqk", query_rot, keys_all, preferred_element_type=jnp.float32)
    return jnp.where(allowed[None], raw * query_rot.shape[-1] ** (-0.5), -1e30)


def fetch_halo(stacked, hops):
    pieces = []
    carried = stacked
    for offset in range(hops):
        carried = shifted(carried, "seq", 1)
        pieces.insert(0, carried)
    return pieces


def return_halo(pieces, hops):
    carried = jnp.zeros_like(pieces[0])
    for offset in range(hops):
        carried = shifted(shortened(carried + pieces[offset]), "seq", -1)
    return carried


def forward_layer(inputs, places, segment_row, weights, seq_index, hops):
    (
        query_w,
        key_w,
        value_w,
        output_w,
        gate_w,
        up_w,
        down_w,
        pre_g,
        query_g,
        key_g,
        mix_g,
        ffn_g,
        out_g,
    ) = weights
    shard = inputs.shape[0]
    size = key_w.shape[1]
    heads = query_w.shape[1] // size
    normed = normalize(inputs, pre_g).astype(jnp.bfloat16)
    query_raw = product(normed, query_w).reshape(shard, heads, size)
    key_raw = product(normed, key_w)
    values = product(normed, value_w).astype(jnp.bfloat16)
    query_rot = rotate(normalize(query_raw, query_g), places).astype(jnp.bfloat16)
    key_rot = rotate(normalize(key_raw, key_g), places).astype(jnp.bfloat16)
    stacked = jnp.stack([key_rot, values])
    pieces = fetch_halo(stacked, hops)
    joined = jnp.concatenate(pieces + [stacked], axis=1)
    keys_all = joined[0]
    values_all = joined[1]
    allowed = window_mask(segment_row, seq_index, shard, hops)
    score = scores(query_rot, keys_all, allowed)
    highest = jnp.max(score, axis=-1, keepdims=True)
    expo = jnp.exp(score - highest)
    total = jnp.sum(expo, axis=-1, keepdims=True)
    prob = expo / total
    log_total = highest + jnp.log(total)
    mixed = jnp.einsum(
        "hqk,kd->qhd", prob.astype(jnp.bfloat16), values_all, preferred_element_type=jnp.float32
    )
    mixed = mixed.reshape(shard, heads * size).astype(jnp.bfloat16)
    branch = product(mixed, output_w)
    middle = inputs + normalize(branch, mix_g)
    inner = normalize(middle, ffn_g).astype(jnp.bfloat16)
    gate_act = product(inner, gate_w)
    up_act = product(inner, up_w)
    hidden = (jax.nn.gelu(gate_act) * up_act).astype(jnp.bfloat16)
    down = product(hidden, down_w)
    result = (middle + normalize(down, out_g)).astype(jnp.bfloat16)
    stored = {
        "inputs": inputs,
        "places": places,
        "normed": normed,
        "query_raw": query_raw,
        "key_raw": key_raw,
        "query_rot": query_rot,
        "keys_all": keys_all,
        "values_all": values_all,
        "allowed": allowed,
        "log_total": log_total,
        "mixed": mixed,
        "branch": branch,
        "middle": middle,
        "inner": inner,
        "gate_act": gate_act,
        "up_act": up_act,
        "hidden": hidden,
        "down": down,
    }
    return (result, stored)


def backward_layer(grad_out, stored, weights, hops):
    (
        query_w,
        key_w,
        value_w,
        output_w,
        gate_w,
        up_w,
        down_w,
        pre_g,
        query_g,
        key_g,
        mix_g,
        ffn_g,
        out_g,
    ) = weights
    shard = grad_out.shape[0]
    size = key_w.shape[1]
    heads = query_w.shape[1] // size
    places = stored["places"]
    _, pull = jax.vjp(normalize, stored["down"], out_g)
    d_down, d_out_g = pull(grad_out)
    d_down = d_down.astype(jnp.bfloat16)
    grad_down_w = inner_rows(stored["hidden"], d_down)
    d_hidden = against(d_down, down_w)
    _, pull = jax.vjp(
        lambda gate_in, up_in: jax.nn.gelu(gate_in) * up_in, stored["gate_act"], stored["up_act"]
    )
    d_gate, d_up = pull(d_hidden)
    d_gate = d_gate.astype(jnp.bfloat16)
    d_up = d_up.astype(jnp.bfloat16)
    grad_gate_w = inner_rows(stored["inner"], d_gate)
    grad_up_w = inner_rows(stored["inner"], d_up)
    d_inner = against(d_gate, gate_w) + against(d_up, up_w)
    _, pull = jax.vjp(normalize, stored["middle"], ffn_g)
    d_middle_ffn, d_ffn_g = pull(d_inner)
    d_middle = grad_out + d_middle_ffn
    _, pull = jax.vjp(normalize, stored["branch"], mix_g)
    d_branch, d_mix_g = pull(d_middle)
    d_branch = d_branch.astype(jnp.bfloat16)
    grad_output_w = inner_rows(stored["mixed"], d_branch)
    d_mixed = against(d_branch, output_w).astype(jnp.bfloat16).reshape(shard, heads, size)
    score = scores(stored["query_rot"], stored["keys_all"], stored["allowed"])
    prob = jnp.exp(score - stored["log_total"])
    d_prob = jnp.einsum(
        "qhd,kd->hqk", d_mixed, stored["values_all"], preferred_element_type=jnp.float32
    )
    d_score = (prob * (d_prob - jnp.sum(prob * d_prob, axis=-1, keepdims=True))).astype(
        jnp.bfloat16
    )
    scale = size ** (-0.5)
    d_query_rot = (
        jnp.einsum("hqk,kd->qhd", d_score, stored["keys_all"], preferred_element_type=jnp.float32)
        * scale
    )
    d_keys = (
        jnp.einsum("hqk,qhd->kd", d_score, stored["query_rot"], preferred_element_type=jnp.float32)
        * scale
    )
    d_values_all = jnp.einsum(
        "hqk,qhd->kd", prob.astype(jnp.bfloat16), d_mixed, preferred_element_type=jnp.float32
    )
    d_stacked = jnp.stack([d_keys, d_values_all])
    pieces = [d_stacked[:, offset * shard : (offset + 1) * shard] for offset in range(hops)]
    local = d_stacked[:, hops * shard :] + return_halo(pieces, hops)
    d_key_rot = local[0]
    d_values = local[1].astype(jnp.bfloat16)
    grad_value_w = inner_rows(stored["normed"], d_values)
    _, pull = jax.vjp(
        lambda raw_in, gain_in: rotate(normalize(raw_in, gain_in), places),
        stored["query_raw"],
        query_g,
    )
    d_query_raw, d_query_g = pull(d_query_rot)
    d_query_raw = d_query_raw.reshape(shard, heads * size).astype(jnp.bfloat16)
    _, pull = jax.vjp(
        lambda raw_in, gain_in: rotate(normalize(raw_in, gain_in), places), stored["key_raw"], key_g
    )
    d_key_raw, d_key_g = pull(d_key_rot)
    d_key_raw = d_key_raw.astype(jnp.bfloat16)
    grad_query_w = inner_rows(stored["normed"], d_query_raw)
    grad_key_w = inner_rows(stored["normed"], d_key_raw)
    d_normed = (
        against(d_query_raw, query_w) + against(d_key_raw, key_w) + against(d_values, value_w)
    )
    _, pull = jax.vjp(normalize, stored["inputs"], pre_g)
    d_inputs_pre, d_pre_g = pull(d_normed)
    d_inputs = d_middle + d_inputs_pre
    gradients = (
        grad_query_w,
        grad_key_w,
        grad_value_w,
        grad_output_w,
        grad_gate_w,
        grad_up_w,
        grad_down_w,
        d_pre_g,
        d_query_g,
        d_key_g,
        d_mix_g,
        d_ffn_g,
        d_out_g,
    )
    return (d_inputs, gradients)


def reorder(gradient, seq_count, fsdp_count):
    rows = gradient.shape[0]
    split = gradient.reshape(
        (fsdp_count, seq_count, rows // (fsdp_count * seq_count)) + gradient.shape[1:]
    )
    return jnp.swapaxes(split, 0, 1).reshape(gradient.shape)


def per_device(
    hidden_in,
    positions,
    segments,
    cotangent,
    query_weight,
    key_weight,
    value_weight,
    output_weight,
    gate_weight,
    up_weight,
    down_weight,
    pre_gain,
    query_gain,
    key_gain,
    mix_gain,
    ffn_gain,
    out_gain,
):
    attn_part = (
        lax.all_gather(query_weight, "fsdp", axis=1, tiled=True),
        lax.all_gather(key_weight, "fsdp", axis=1, tiled=True),
        lax.all_gather(value_weight, "fsdp", axis=1, tiled=True),
        lax.all_gather(output_weight, "fsdp", axis=1, tiled=True),
        lax.all_gather(pre_gain, "fsdp", axis=1, tiled=True),
        lax.all_gather(query_gain, "fsdp", axis=1, tiled=True),
        lax.all_gather(key_gain, "fsdp", axis=1, tiled=True),
        lax.all_gather(mix_gain, "fsdp", axis=1, tiled=True),
    )
    ffn_part = (
        lax.all_gather(gate_weight, "fsdp", axis=1, tiled=True),
        lax.all_gather(up_weight, "fsdp", axis=1, tiled=True),
        lax.all_gather(down_weight, "fsdp", axis=1, tiled=True),
        lax.all_gather(ffn_gain, "fsdp", axis=1, tiled=True),
        lax.all_gather(out_gain, "fsdp", axis=1, tiled=True),
    )
    weights = (
        attn_part[0][0],
        attn_part[1][0],
        attn_part[2][0],
        attn_part[3][0],
        ffn_part[0][0],
        ffn_part[1][0],
        ffn_part[2][0],
        attn_part[4][0].astype(jnp.float32),
        attn_part[5][0].astype(jnp.float32),
        attn_part[6][0].astype(jnp.float32),
        attn_part[7][0].astype(jnp.float32),
        ffn_part[3][0].astype(jnp.float32),
        ffn_part[4][0].astype(jnp.float32),
    )
    leading_section = lax.axis_index("section") == 0
    seq_index = lax.axis_index("seq")
    micro = hidden_in.shape[0]
    shard = hidden_in.shape[2]
    hops = WINDOW // shard
    inputs_all = hidden_in[:, 0]
    cot_all = cotangent[:, 0]
    place_rows = positions[:, 0]
    segment_rows = segments[:, 0]
    received = jnp.zeros_like(inputs_all[0])
    stored_ticks = []
    result_ticks = []
    for moment in range(micro + 1):
        own = min(moment, micro - 1)
        later = max(moment - 1, 0)
        batch = jnp.where(leading_section, own, later)
        inputs = jnp.where(leading_section, inputs_all[own], received).astype(jnp.float32)
        places = lax.dynamic_index_in_dim(place_rows, batch, 0, keepdims=False)
        segment_row = lax.dynamic_index_in_dim(segment_rows, batch, 0, keepdims=False)
        result, stored = forward_layer(inputs, places, segment_row, weights, seq_index, hops)
        stored_ticks.append(stored)
        result_ticks.append(result)
        if moment < micro:
            received = shifted(result, "section", 1)
    outputs = jnp.stack(
        [
            jnp.where(leading_section, result_ticks[index], result_ticks[index + 1])
            for index in range(micro)
        ]
    )
    grad_recv = jnp.zeros_like(inputs_all[0])
    totals = None
    input_ticks = []
    for moment in range(micro + 1):
        early = stored_ticks[max(moment - 1, 0)]
        late = stored_ticks[min(moment + 1, micro)]
        stored = jax.tree.map(
            lambda first_val, second_val: jnp.where(leading_section, first_val, second_val),
            early,
            late,
        )
        grad_out = jnp.where(leading_section, grad_recv, cot_all[min(moment, micro - 1)]).astype(
            jnp.float32
        )
        d_inputs, gradients = backward_layer(grad_out, stored, weights, hops)
        valid = jnp.where(leading_section, moment >= 1, moment < micro)
        masked = tuple((jnp.where(valid, item, jnp.zeros_like(item)) for item in gradients))
        totals = (
            masked
            if totals is None
            else tuple((first_val + second_val for first_val, second_val in zip(totals, masked)))
        )
        input_ticks.append(d_inputs)
        if moment < micro:
            grad_recv = shifted(d_inputs.astype(jnp.bfloat16), "section", -1)
    input_grads = jnp.stack(
        [
            jnp.where(leading_section, input_ticks[index + 1], input_ticks[index])
            for index in range(micro)
        ]
    )
    seq_count = lax.axis_size("seq")
    fsdp_count = lax.axis_size("fsdp")
    spread = tuple((reorder(item, seq_count, fsdp_count) for item in totals))
    parts = (
        lax.psum_scatter(spread[0], ("seq", "fsdp"), scatter_dimension=0, tiled=True),
        lax.psum_scatter(spread[1], ("seq", "fsdp"), scatter_dimension=0, tiled=True),
        lax.psum_scatter(spread[2], ("seq", "fsdp"), scatter_dimension=0, tiled=True),
        lax.psum_scatter(spread[3], ("seq", "fsdp"), scatter_dimension=0, tiled=True),
        lax.psum_scatter(spread[4], ("seq", "fsdp"), scatter_dimension=0, tiled=True),
        lax.psum_scatter(spread[5], ("seq", "fsdp"), scatter_dimension=0, tiled=True),
        lax.psum_scatter(spread[6], ("seq", "fsdp"), scatter_dimension=0, tiled=True),
        lax.psum_scatter(spread[7], ("seq", "fsdp"), scatter_dimension=0, tiled=True),
        lax.psum_scatter(spread[8], ("seq", "fsdp"), scatter_dimension=0, tiled=True),
        lax.psum_scatter(spread[9], ("seq", "fsdp"), scatter_dimension=0, tiled=True),
        lax.psum_scatter(spread[10], ("seq", "fsdp"), scatter_dimension=0, tiled=True),
        lax.psum_scatter(spread[11], ("seq", "fsdp"), scatter_dimension=0, tiled=True),
        lax.psum_scatter(spread[12], ("seq", "fsdp"), scatter_dimension=0, tiled=True),
    )
    owned = (
        lax.all_gather(parts[0].astype(jnp.bfloat16), "seq", axis=0, tiled=True).astype(
            jnp.float32
        ),
        lax.all_gather(parts[1].astype(jnp.bfloat16), "seq", axis=0, tiled=True).astype(
            jnp.float32
        ),
        lax.all_gather(parts[2].astype(jnp.bfloat16), "seq", axis=0, tiled=True).astype(
            jnp.float32
        ),
        lax.all_gather(parts[3].astype(jnp.bfloat16), "seq", axis=0, tiled=True).astype(
            jnp.float32
        ),
        lax.all_gather(parts[4].astype(jnp.bfloat16), "seq", axis=0, tiled=True).astype(
            jnp.float32
        ),
        lax.all_gather(parts[5].astype(jnp.bfloat16), "seq", axis=0, tiled=True).astype(
            jnp.float32
        ),
        lax.all_gather(parts[6].astype(jnp.bfloat16), "seq", axis=0, tiled=True).astype(
            jnp.float32
        ),
        lax.all_gather(parts[7].astype(jnp.bfloat16), "seq", axis=0, tiled=True).astype(
            jnp.float32
        ),
        lax.all_gather(parts[8].astype(jnp.bfloat16), "seq", axis=0, tiled=True).astype(
            jnp.float32
        ),
        lax.all_gather(parts[9].astype(jnp.bfloat16), "seq", axis=0, tiled=True).astype(
            jnp.float32
        ),
        lax.all_gather(parts[10].astype(jnp.bfloat16), "seq", axis=0, tiled=True).astype(
            jnp.float32
        ),
        lax.all_gather(parts[11].astype(jnp.bfloat16), "seq", axis=0, tiled=True).astype(
            jnp.float32
        ),
        lax.all_gather(parts[12].astype(jnp.bfloat16), "seq", axis=0, tiled=True).astype(
            jnp.float32
        ),
    )
    return (
        outputs[None, :, None],
        input_grads[None, :, None],
        owned[0][None],
        owned[1][None],
        owned[2][None],
        owned[3][None],
        owned[4][None],
        owned[5][None],
        owned[6][None],
        owned[7][None],
        owned[8][None],
        owned[9][None],
        owned[10][None],
        owned[11][None],
        owned[12][None],
    )


def solution(mesh):
    in_specs = (
        P(None, "fsdp", "seq", None),
        P(None, "fsdp", "seq"),
        P(None, "fsdp", None),
        P(None, "fsdp", "seq", None),
        P("section", "fsdp", None),
        P("section", "fsdp", None),
        P("section", "fsdp", None),
        P("section", "fsdp", None),
        P("section", "fsdp", None),
        P("section", "fsdp", None),
        P("section", "fsdp", None),
        P("section", "fsdp"),
        P("section", "fsdp"),
        P("section", "fsdp"),
        P("section", "fsdp"),
        P("section", "fsdp"),
        P("section", "fsdp"),
    )
    out_specs = (
        P("section", None, "fsdp", "seq", None),
        P("section", None, "fsdp", "seq", None),
        P("section", "fsdp", None),
        P("section", "fsdp", None),
        P("section", "fsdp", None),
        P("section", "fsdp", None),
        P("section", "fsdp", None),
        P("section", "fsdp", None),
        P("section", "fsdp", None),
        P("section", "fsdp"),
        P("section", "fsdp"),
        P("section", "fsdp"),
        P("section", "fsdp"),
        P("section", "fsdp"),
        P("section", "fsdp"),
    )
    return jax.shard_map(
        per_device, mesh=mesh, in_specs=in_specs, out_specs=out_specs, check_vma=False
    )
```

profile of v0, /device:TPU:0, one launch (start us, length us, event | category | flops | bytes accessed | tf_op | source)
XLA Modules:
  0.0 1331.2 jit_solution(7065651824506193178)
XLA Ops:
  13.5 12.0 all-reduce.45
  25.6 13.4 %all_gather.79 = bf16[1,640,256]{2,1,0:T(8,128)(2,1)S(1)} all-gather(bf16[1,160,256]{2,1,0:T(8,128)(2,1)S(1)} %copy-done.228), channel_id=1, replica_groups=mesh['section'=2,'seq'=16,'fsdp'=4] {'fsdp'}, dimensions={1}, use_global_device_ids=true | all-gather | bytes 409600 | tf_op jit(solution)/shard_map/all_gather | solution.py:303
  39.0 12.7 all_gather.81
  54.2 3.4 collective-permute-start
  60.1 4.3 collective-permute-start.1
  66.9 4.3 collective-permute-start.2
  73.8 4.3 collective-permute-start.3
  88.7 15.3 %all-gather.15.cloned.1.call-done = bf16[1,640,2048]{2,1,0:T(8,128)(2,1)} async-done(((bf16[1,160,2048]{2,1,0:T(8,128)(2,1)}), bf16[1,640,2048]{2,1,0:T(8,128)(2,1)}) %all-gather.15.cloned.1.call-update) | async-done | bytes 2621456 | tf_op jit(solution)/shard_map/all_gather | solution.py:312
  104.0 3.3 fusion.46
  107.3 33.7 %all-gather.17.cloned.1.call-done = bf16[1,640,2048]{2,1,0:T(8,128)(2,1)} async-done(((bf16[1,160,2048]{2,1,0:T(8,128)(2,1)}), bf16[1,640,2048]{2,1,0:T(8,128)(2,1)}) %all-gather.17.cloned.1.call-update) | async-done | bytes 2621456 | tf_op jit(solution)/shard_map/all_gather | solution.py:313
  140.9 3.8 fusion.190
  144.7 33.1 %all-gather.19.cloned.1.call-done = bf16[1,2048,640]{2,1,0:T(8,128)(2,1)} async-done(((bf16[1,512,640]{2,1,0:T(8,128)(2,1)}), bf16[1,2048,640]{2,1,0:T(8,128)(2,1)}) %all-gather.19.cloned.1.call-update) | async-done | bytes 2621456 | tf_op jit(solution)/shard_map/all_gather | solution.py:314
  197.0 3.4 collective-permute-start.5
  202.8 4.3 collective-permute-start.6
  209.7 4.3 collective-permute-start.7
  216.5 4.9 collective-permute-start.8
  253.1 4.3 collective-permute-start.10
  259.9 5.3 collective-permute-start.11
  267.8 6.8 collective-permute-start.12
  274.7 3.5 collective-permute-done.12
  278.2 7.0 collective-permute-start.13
  298.7 4.5 collective-permute-done.19
  304.6 7.8 collective-permute-done.20
  316.5 5.4 collective-permute-done.21
  323.8 7.5 collective-permute-done.22
  347.5 6.0 collective-permute-start.15
  357.4 6.0 collective-permute-start.16
  366.5 5.4 collective-permute-start.17
  374.4 4.6 collective-permute-start.18
  403.1 3.2 fusion.229
  419.1 3.9 collective-permute-done.24
  427.9 4.4 collective-permute-done.25
  435.7 6.4 collective-permute-done.26
  443.9 7.7 collective-permute-done.27
  457.4 3.3 fusion.522
  483.6 4.9 collective-permute-done.29
  493.2 5.1 collective-permute-done.30
  502.9 4.9 collective-permute-done.31
  509.6 7.2 collective-permute-done.32
  549.7 7.0 select_add_fusion.2
  556.8 6.4 select_add_fusion.1
  563.3 6.3 select_add_fusion
  570.1 7.0 reshape.2126
  577.1 7.9 copy.174
  584.9 7.3 reshape.2127
  592.3 7.0 reshape.2128
  599.3 7.9 copy.175
  607.1 7.3 reshape.2129
  616.2 8.8 collective-permute-done.35
  626.7 5.3 copy.176
  632.0 3.4 collective-permute-done.36
  637.4 7.7 collective-permute-done.37
  654.0 4.4 reshape.2118
  658.3 4.7 copy.170
  663.1 4.6 reshape.2119
  674.9 434.5 %all-reduce.47 = (bf16[640,1024]{1,0:T(8,128)(2,1)}, bf16[640,256]{1,0:T(8,128)(2,1)S(1)}, bf16[640,256]{1,0:T(8,128)(2,1)S(1)}, bf16[640,2048]{1,0:T(8,128)(2,1...) all-reduce(f32[640,1024]{1,0:T(8,128)} %reshape.2119, ...), channel_id=2, replica_groups=mesh['section'=2,'seq'=16,'fsdp'=4] {'seq','fsdp'}, use_global_device_ids=true, to_apply=%region_84.85.clone | all-reduce | flops 3607552 | bytes 21645312
  1110.2 21.1 %all-gather = bf16[16,10,1024]{2,1,0:T(8,128)(2,1)S(1)} all-gather(bf16[1,10,1024]{2,1,0:T(8,128)(2,1)S(1)} %fusion.447), channel_id=1, replica_groups=mesh['section'=2,'seq'=16,'fsdp'=4] {'seq'}, dimensions={0}, use_global_device_ids=true | all-gather | bytes 348160 | tf_op jit(solution)/shard_map/all_gather | solution.py:413
  1132.2 23.9 %all-gather.1 = bf16[16,10,256]{2,1,0:T(8,128)(2,1)S(1)} all-gather(bf16[1,10,256]{2,1,0:T(8,128)(2,1)S(1)} %fusion.464), channel_id=1, replica_groups=mesh['section'=2,'seq'=16,'fsdp'=4] {'seq'}, dimensions={0}, use_global_device_ids=true | all-gather | bytes 87040 | tf_op jit(solution)/shard_map/all_gather | solution.py:416
  1156.9 20.9 %all-gather.2 = bf16[16,10,256]{2,1,0:T(8,128)(2,1)S(1)} all-gather(bf16[1,10,256]{2,1,0:T(8,128)(2,1)S(1)} %fusion.465), channel_id=1, replica_groups=mesh['section'=2,'seq'=16,'fsdp'=4] {'seq'}, dimensions={0}, use_global_device_ids=true | all-gather | bytes 87040 | tf_op jit(solution)/shard_map/all_gather | solution.py:419
  1179.4 25.0 %all-gather.3 = bf16[16,10,2048]{2,1,0:T(8,128)(2,1)S(1)} all-gather(bf16[1,10,2048]{2,1,0:T(8,128)(2,1)S(1)} %fusion.435), channel_id=1, replica_groups=mesh['section'=2,'seq'=16,'fsdp'=4] {'seq'}, dimensions={0}, use_global_device_ids=true | all-gather | bytes 696320 | tf_op jit(solution)/shard_map/all_gather | solution.py:425
  1206.6 22.8 %all-gather.4 = bf16[16,10,2048]{2,1,0:T(8,128)(2,1)S(1)} all-gather(bf16[1,10,2048]{2,1,0:T(8,128)(2,1)S(1)} %fusion.436), channel_id=1, replica_groups=mesh['section'=2,'seq'=16,'fsdp'=4] {'seq'}, dimensions={0}, use_global_device_ids=true | all-gather | bytes 696320 | tf_op jit(solution)/shard_map/all_gather | solution.py:428
  1232.4 38.1 %all-reduce.44 = (bf16[160]{0:T(256)(128)(2,1)S(1)}, bf16[64]{0:T(256)(128)(2,1)S(1)}, bf16[64]{0:T(256)(128)(2,1)S(1)}, bf16[160]{0:T(256)(128)(2,1)S(1)}, bf16...) all-reduce(bf16[160]{0:T(256)(128)(2,1)S(1)} %dynamic-update-slice., ...), channel_id=1, replica_groups=mesh['section'=2,'seq'=16,'fsdp'=4] {'seq'}, use_global_device_ids=true, to_apply=%add.26 | all-reduce | flops 768 | bytes 3072
  1275.8 20.8 %all_gather.94 = bf16[256,640]{1,0:T(8,128)(2,1)S(1)} all-gather(bf16[16,640]{1,0:T(8,128)(2,1)S(1)} %convert_element_type.789), channel_id=1, replica_groups=mesh['section'=2,'seq'=16,'fsdp'=4] {'seq'}, dimensions={0}, use_global_device_ids=true | all-gather | bytes 348160 | tf_op jit(solution)/shard_map/all_gather | solution.py:422
  1298.4 24.3 %all_gather.97 = bf16[512,640]{1,0:T(8,128)(2,1)S(1)} all-gather(bf16[32,640]{1,0:T(8,128)(2,1)S(1)} %convert_element_type.792), channel_id=1, replica_groups=mesh['section'=2,'seq'=16,'fsdp'=4] {'seq'}, dimensions={0}, use_global_device_ids=true | all-gather | bytes 696320 | tf_op jit(solution)/shard_map/all_gather | solution.py:431
  (1201 shorter events, 286.7 us)
Async XLA Ops:
  7.3 31.8 %copy-start.229 = (bf16[1,160,256]{2,1,0:T(8,128)(2,1)S(1)}, bf16[1,160,256]{2,1,0:T(8,128)(2,1)}, u32[]{:S(2)}) copy-start(bf16[1,160,256]{2,1,0:T(8,128)(2,1)} %param.23) | copy-start | bytes 245764
  7.3 73.5 %all-gather.11.cloned.1.call-start = ((), (), s32[]{:S(2)}) async-start(), calls=%async_computation.2 | async-start | bytes 1638400 | tf_op jit(solution)/shard_map/all_gather | solution.py:302
  8.0 43.8 %copy-start.22 = (bf16[3,1,128,640]{3,2,1,0:T(8,128)(2,1)S(1)}, bf16[3,1,128,640]{3,2,1,0:T(8,128)(2,1)}, u32[]{:S(2)}) copy-start(bf16[3,1,128,640]{3,2,1,0:T(8,128)(2,1)} %param.17) | copy-start | bytes 1474564
  8.0 77.9 %all-gather.13.cloned.1.call-start = ((), (), s32[]{:S(2)}) async-start(), calls=%async_computation.3 | async-start | bytes 1638400 | tf_op jit(solution)/shard_map/all_gather | solution.py:305
  8.8 95.2 %all-gather.15.cloned.1.call-start = ((), (), s32[]{:S(2)}) async-start(), calls=%async_computation.4 | async-start | bytes 3276800 | tf_op jit(solution)/shard_map/all_gather | solution.py:312
  9.5 131.4 %all-gather.17.cloned.1.call-start = ((), (), s32[]{:S(2)}) async-start(), calls=%async_computation.5 | async-start | bytes 3276800 | tf_op jit(solution)/shard_map/all_gather | solution.py:313
  10.1 167.8 %all-gather.19.cloned.1.call-start = ((), (), s32[]{:S(2)}) async-start(), calls=%async_computation.6 | async-start | bytes 3276800 | tf_op jit(solution)/shard_map/all_gather | solution.py:314
  54.2 5.9 collective-permute-start
  57.6 1217.4 %reduce-scatter.3.cloned.1.call-start = ((), (), s32[]{:S(2)}) async-start(), calls=%async_computation.7 | async-start | bytes 2662400 | tf_op jit(solution)/shard_map/reduce_scatter | solution.py:401
  60.1 6.8 collective-permute-start.1
  66.9 6.8 collective-permute-start.2
  73.8 6.8 collective-permute-start.3
  82.7 112.4 %copy-start.15 = (bf16[1024,640]{1,0:T(8,128)(2,1)}, bf16[1024,640]{1,0:T(8,128)(2,1)S(1)}, u32[]{:S(2)}) copy-start(bf16[1024,640]{1,0:T(8,128)(2,1)S(1)} %copy.130) | copy-start | bytes 3932164
  83.4 117.0 %copy-start.25 = (f32[128,4,256]{2,0,1:T(8,128)}, f32[128,4,256]{2,0,1:T(8,128)S(1)}, u32[]{:S(2)}) copy-start(f32[128,4,256]{2,0,1:T(8,128)S(1)} %get-tuple-element.337) | copy-start | bytes 1572868
  85.1 139.5 %copy-start.240 = (f32[4,128]{1,0:T(4,128)}, f32[4,128]{1,0:T(4,128)S(1)}, u32[]{:S(2)}) copy-start(f32[4,128]{1,0:T(4,128)S(1)} %get-tuple-element.338) | copy-start | bytes 6148
  88.6 52.3 %copy-start.53 = (bf16[128,640]{1,0:T(8,128)(2,1)}, bf16[128,640]{1,0:T(8,128)(2,1)S(1)}, u32[]{:S(2)}) copy-start(bf16[128,640]{1,0:T(8,128)(2,1)S(1)} %multiply_convert_fusion.11) | copy-start | bytes 491524
  144.7 35.6 %copy-start.35 = (bf16[128,2048]{1,0:T(8,128)(2,1)}, bf16[128,2048]{1,0:T(8,128)(2,1)S(1)}, u32[]{:S(2)}) copy-start(bf16[128,2048]{1,0:T(8,128)(2,1)S(1)} %get-tuple-element.342) | copy-start | bytes 1572868
  181.0 13.8 %collective-permute-start.4 = (bf16[128,640]{1,0:T(8,128)(2,1)S(1)}, bf16[128,640]{1,0:T(8,128)(2,1)S(1)}, u32[]{:S(2)}, u32[]{:S(2)}) collective-permute-start(bf16[128,640]{1,0:T(8,128)(2,1)S(1)} %add_convert_fusion.3), channel_id=1, source_target_pairs={{0,64},{1,65},{2,66},{3,67},{4,68},{5,69},{6,70},{7,71},{8,72},{9,... | collective-permute-start | bytes 491528 | tf_op jit(solution)/shard_map/ppermute | solution.py:16
  197.0 5.9 collective-permute-start.5
  200.7 92.6 %copy-start.204 = (bf16[128,4,128]{2,0,1:T(8,128)(2,1)}, bf16[128,4,128]{2,0,1:T(8,128)(2,1)S(1)}, u32[]{:S(2)}) copy-start(bf16[128,4,128]{2,0,1:T(8,128)(2,1)S(1)} %get-tuple-element.223) | copy-start | bytes 393220
  200.7 92.6 %copy-start.206 = (bf16[128,4,128]{2,0,1:T(8,128)(2,1)}, bf16[128,4,128]{2,0,1:T(8,128)(2,1)S(1)}, u32[]{:S(2)}) copy-start(bf16[128,4,128]{2,0,1:T(8,128)(2,1)S(1)} %get-tuple-element.224) | copy-start | bytes 393220
  202.8 6.8 collective-permute-start.6
  209.7 6.8 collective-permute-start.7
  216.5 6.8 collective-permute-start.8
  223.5 74.7 %copy-start.158 = (bf16[2,640,256]{2,1,0:T(8,128)(2,1)}, bf16[2,640,256]{2,1,0:T(8,128)(2,1)S(1)}, u32[]{:S(2)}) copy-start(bf16[2,640,256]{2,1,0:T(8,128)(2,1)S(1)} %constant_dynamic-update-slice_fusion.5) | copy-start | bytes 1966084
  234.2 16.6 %collective-permute-start.9 = (bf16[128,640]{1,0:T(8,128)(2,1)S(1)}, bf16[128,640]{1,0:T(8,128)(2,1)S(1)}, u32[]{:S(2)}, u32[]{:S(2)}) collective-permute-start(bf16[128,640]{1,0:T(8,128)(2,1)S(1)} %get-tuple-element.182), channel_id=1, source_target_pairs={{0,64},{1,65},{2,66},{3,67},{4,68},{5,69},{6,70},{7,71},{8,72},{9,... | collective-permute-start | bytes 491528 | tf_op jit(solution)/shard_map/ppermute | solution.py:16
  250.7 38.8 %copy-start.107 = (f32[128,640]{1,0:T(8,128)}, f32[128,640]{1,0:T(8,128)S(1)}, u32[]{:S(2)}) copy-start(f32[128,640]{1,0:T(8,128)S(1)} %get-tuple-element.190) | copy-start | bytes 983044
  253.1 6.8 collective-permute-start.10
  259.9 7.8 collective-permute-start.11
  267.8 10.4 collective-permute-start.12
  278.2 9.4 collective-permute-start.13
  290.4 32.7 %copy-start.315 = (f32[128]{0:T(128)}, f32[128]{0:T(128)S(1)}, u32[]{:S(2)}) copy-start(f32[128]{0:T(128)S(1)} %get-tuple-element.173) | copy-start | bytes 1540
  293.8 9.5 collective-permute-start.19
  303.3 9.1 collective-permute-start.20
  312.4 9.4 collective-permute-start.21
  314.5 24.6 %collective-permute-start.14 = (bf16[128,640]{1,0:T(8,128)(2,1)S(1)}, bf16[128,640]{1,0:T(8,128)(2,1)}, u32[]{:S(2)}, u32[]{:S(2)}) collective-permute-start(bf16[128,640]{1,0:T(8,128)(2,1)S(1)} %get-tuple-element.184), channel_id=1, source_target_pairs={{0,64},{1,65},{2,66},{3,67},{4,68},{5,69},{6,70},{7,71},{8,72},{9,... | collective-permute-start | bytes 491528 | tf_op jit(solution)/shard_map/ppermute | solution.py:16
  321.9 9.4 collective-permute-start.22
  340.3 31.6 %copy-start.335 = (f32[128]{0:T(128)}, f32[128]{0:T(128)S(1)}, u32[]{:S(2)}) copy-start(f32[128]{0:T(128)S(1)} %get-tuple-element.109) | copy-start | bytes 1540
  347.2 31.8 %copy-start.311 = (f32[128]{0:T(128)}, f32[128]{0:T(128)S(1)}, u32[]{:S(2)}) copy-start(f32[128]{0:T(128)S(1)} %get-tuple-element.143) | copy-start | bytes 1540
  347.5 9.8 collective-permute-start.15
  357.4 9.1 collective-permute-start.16
  366.5 7.9 collective-permute-start.17
  374.4 6.8 collective-permute-start.18
  393.7 7.6 collective-permute-start.23
  414.6 8.3 collective-permute-start.24
  423.0 9.3 collective-permute-start.25
  432.3 9.8 collective-permute-start.26
  442.1 9.4 collective-permute-start.27
  463.7 3.9 collective-permute-start.28
  479.1 9.4 collective-permute-start.29
  488.6 9.8 collective-permute-start.30
  498.4 9.4 collective-permute-start.31
  507.8 9.0 collective-permute-start.32
  526.6 3.9 collective-permute-start.33
  542.7 754.8 %reduce-scatter.5.cloned.1.call-start = ((), (), s32[]{:S(2)}) async-start(), calls=%async_computation.8 | async-start | bytes 5324800 | tf_op jit(solution)/shard_map/reduce_scatter | solution.py:404
  547.8 66.7 %collective-permute-start.34 = (bf16[2,128,256]{2,1,0:T(8,128)(2,1)}, bf16[2,128,256]{2,1,0:T(8,128)(2,1)S(1)}, u32[]{:S(2)}, u32[]{:S(2)}) collective-permute-start(bf16[2,128,256]{2,1,0:T(8,128)(2,1)} %fusion.345), channel_id=1, source_target_pairs={{4,0},{8,4},{12,8},{16,12},{20,16},{24,20},{28,24},{32,28},{36,32}... | collective-permute-start | bytes 393224 | tf_op jit(solution)/shard_map/ppermute | solution.py:16
  614.6 10.4 collective-permute-start.35
  625.0 10.4 collective-permute-start.36
  635.5 9.6 collective-permute-start.37
  1229.4 43.4 %copy-start.336 = (f32[128]{0:T(128)S(1)}, f32[128]{0:T(128)}, u32[]{:S(2)}) copy-start(f32[128]{0:T(128)} %copy-done.335) | copy-start | bytes 1540
  1229.4 43.4 %copy-start.90 = (f32[128,640]{1,0:T(8,128)S(1)}, f32[128,640]{1,0:T(8,128)}, u32[]{:S(2)}) copy-start(f32[128,640]{1,0:T(8,128)} %copy-done.89) | copy-start | bytes 983044
  1229.4 43.4 %copy-start.97 = (f32[128,640]{1,0:T(8,128)S(1)}, f32[128,640]{1,0:T(8,128)}, u32[]{:S(2)}) copy-start(f32[128,640]{1,0:T(8,128)} %copy-done.96) | copy-start | bytes 983044
  1230.7 42.3 %copy-start.138 = (f32[1,128,640]{2,1,0:T(8,128)S(1)}, f32[1,128,640]{2,1,0:T(8,128)}, u32[]{:S(2)}) copy-start(f32[1,128,640]{2,1,0:T(8,128)} %get-tuple-element.137) | copy-start | bytes 983044
  1230.7 42.3 %copy-start.139 = (f32[1,128,640]{2,1,0:T(8,128)S(1)}, f32[1,128,640]{2,1,0:T(8,128)}, u32[]{:S(2)}) copy-start(f32[1,128,640]{2,1,0:T(8,128)} %get-tuple-element.139) | copy-start | bytes 983044
  (333 other events, 1394.5 us)
Sparse Core Ops, SparseCore 0:
  9.8 29.6 all-gather.10
  41.2 25.2 all-gather.12
  68.1 35.8 all-gather.14
  105.5 35.4 all-gather.16
  142.4 35.3 all-gather.18
  542.8 365.5 reduce-scatter.2
  911.0 360.4 reduce-scatter.4
where the time goes:
time: 1340 us; the launch traced here: 1330 us
  blocking collectives  670 us (50%)
  waiting for transfers between devices  207 us (15%)
  matrix products  140 us (10%)
  local copies, waits for them, and re-layouts  122 us (9%)
  starting transfers between devices  110 us (8%)
  other arithmetic  57.8 us (4%)
  between operations  23.9 us (2%)
    unnamed x3, blocking collectives  485 us
    ppermute x38, waiting for transfers between devices, shifted(): return lax.ppermute(x, axis, pairs)  122 us
    ppermute x38, starting transfers between devices, shifted(): return lax.ppermute(x, axis, pairs)  110 us
    dot_general x28, matrix products, inner_rows(): lax.dot_general(left, right, (((0,), (0,)), ((), ())), preferred_element_...  71.5 us
    all_gather x1, waiting for transfers between devices, per_device(): lax.all_gather(up_weight, 'fsdp', axis=1, tiled=True)  33.7 us
    all_gather x1, waiting for transfers between devices, per_device(): lax.all_gather(down_weight, 'fsdp', axis=1, tiled=True)  33.1 us
    unnamed x758, local copies, waits for them, and re-layouts  30 us
    dot_general x28, matrix products, against(): lax.dot_general(left, right, (((1,), (1,)), ((), ())), preferred_element_...  29.3 us
  transfers between devices with their start and end apart: 45, of which 33 were waited for; matrix products, arithmetic and copies ran while one was open for 16% of the time, Pallas kernels for 0%

commit v1 on v0

v1 whole, which is shorter than its diff:
```python
import jax
import jax.numpy as jnp
import numpy as np
from jax import lax
from jax.experimental import pallas as pl
from jax.experimental.pallas import tpu as pltpu
from jax.sharding import Mesh, PartitionSpec as P

WINDOW = 512
EPSILON = 1e-06
ROPE_BASE = 10000.0

RING = 4
D = 640
FF = 2048
QH = 4
HD = 256
MICRO = 3
SHARD = 128
TOKENS = MICRO * SHARD
HOPS = WINDOW // SHARD
KEYS = SHARD + WINDOW

ROWS = 256
FFN_COLS = 4096
ATTN_COLS = 1920

FFN_PLAN = ((0, 0, 160, 0, 2048, 0, 0), (1, 0, 160, 0, 2048, 0, 2048)) + tuple(
    (2, 96 * i, min(96, 512 - 96 * i), 0, 640, 160, 640 * i) for i in range(6)
)
ATTN_PLAN = (
    (0, 0, 160, 0, 1024, 0, 0),
    (1, 0, 160, 0, 256, 0, 1024),
    (2, 0, 160, 0, 256, 0, 1280),
) + tuple((3, 96 * i, min(96, 256 - 96 * i), 0, 640, 160, 640 * i) for i in range(3))

FFN_GRAD_PLAN = ((0, 0, 160, 0, 4096, 0, 0),) + tuple(
    (1, 96 * i, min(96, 512 - 96 * i), 0, 640, 160, 640 * i) for i in range(6)
)
ATTN_GRAD_PLAN = ((0, 0, 160, 0, 1536, 0, 0),) + tuple(
    (1, 96 * i, min(96, 256 - 96 * i), 0, 640, 160, 640 * i) for i in range(3)
)


def in_any(count):
    return [pl.BlockSpec(memory_space=pl.ANY)] * count


def run_copies(copies):
    for item in copies:
        item.start()
    for item in copies:
        item.wait()


def pack_shard(arrays, plan, cols):
    def body(*refs):
        sources, out, sems = refs[: len(arrays)], refs[len(arrays)], refs[len(arrays) + 1]
        run_copies(
            [
                pltpu.make_async_copy(
                    sources[a].at[pl.ds(r, n), pl.ds(c, w)],
                    out.at[pl.ds(pr, n), pl.ds(pc, w)],
                    sems.at[i],
                )
                for i, (a, r, n, c, w, pr, pc) in enumerate(plan)
            ]
        )

    return pl.pallas_call(
        body,
        in_specs=in_any(len(arrays)),
        out_specs=pl.BlockSpec(memory_space=pl.ANY),
        out_shape=jax.ShapeDtypeStruct((ROWS, cols), jnp.bfloat16),
        scratch_shapes=[pltpu.SemaphoreType.DMA((len(plan),))],
        name="pack_shard",
    )(*arrays)


def unpack_full(place, pieces, plan, shapes):
    arrays = [item[0] for item in pieces]
    jobs = []
    for index, (_, rel, first, count) in enumerate(pieces):
        for a, r, n, c, w, pr, pc in plan:
            low, high = max(pr, first), min(pr + n, first + count)
            if low < high:
                jobs.append((index, rel, low - first, pc, a, r + low - pr, c, high - low, w))

    def body(place_ref, *refs):
        sources = refs[: len(arrays)]
        outs = refs[len(arrays) : len(arrays) + len(shapes)]
        sems = refs[-1]
        here = place_ref[0]
        copies = []
        for i, (index, rel, sr, sc, a, r, c, n, w) in enumerate(jobs):
            block = lax.rem(here + rel, RING)
            rows = shapes[a][0] // RING
            start = pl.multiple_of(block * rows + r, 32)
            copies.append(
                pltpu.make_async_copy(
                    sources[index].at[pl.ds(sr, n), pl.ds(sc, w)],
                    outs[a].at[pl.ds(start, n), pl.ds(c, w)],
                    sems.at[i],
                )
            )
        run_copies(copies)

    return pl.pallas_call(
        body,
        in_specs=[pl.BlockSpec(memory_space=pltpu.SMEM)] + in_any(len(arrays)),
        out_specs=in_any(len(shapes)),
        out_shape=[jax.ShapeDtypeStruct(shape, jnp.bfloat16) for shape in shapes],
        scratch_shapes=[pltpu.SemaphoreType.DMA((len(jobs),))],
        name="unpack_full",
    )(place, *arrays)


def pack_blocks(place, arrays, plan, cols):
    half = ROWS // 2
    targets = [(0, 0, ROWS), (1, 0, ROWS), (3, 0, ROWS), (2, 0, half), (2, half, half)]
    jobs = []
    for index, (rel, first, count) in enumerate(targets):
        for a, r, n, c, w, pr, pc in plan:
            low, high = max(pr, first), min(pr + n, first + count)
            if low < high:
                jobs.append((index, rel, low - first, pc, a, r + low - pr, c, high - low, w))

    def body(place_ref, *refs):
        sources = refs[: len(arrays)]
        outs = refs[len(arrays) : len(arrays) + len(targets)]
        sems = refs[-1]
        here = place_ref[0]
        copies = []
        for i, (index, rel, sr, sc, a, r, c, n, w) in enumerate(jobs):
            block = lax.rem(here + rel, RING)
            rows = arrays[a].shape[0] // RING
            start = pl.multiple_of(block * rows + r, 32)
            copies.append(
                pltpu.make_async_copy(
                    sources[a].at[pl.ds(start, n), pl.ds(c, w)],
                    outs[index].at[pl.ds(sr, n), pl.ds(sc, w)],
                    sems.at[i],
                )
            )
        run_copies(copies)

    return pl.pallas_call(
        body,
        in_specs=[pl.BlockSpec(memory_space=pltpu.SMEM)] + in_any(len(arrays)),
        out_specs=in_any(len(targets)),
        out_shape=[jax.ShapeDtypeStruct((t[2], cols), jnp.bfloat16) for t in targets],
        scratch_shapes=[pltpu.SemaphoreType.DMA((len(jobs),))],
        name="pack_blocks",
    )(place, *arrays)


def along_z(x, section, by):
    pairs = [(section * RING + i, section * RING + (i + by) % RING) for i in range(RING)]
    return lax.ppermute(x, ("section", "z"), pairs)


def along_seq(x, section, by):
    count = RING * RING
    pairs = [
        (section * count + i, section * count + i + by) for i in range(count) if 0 <= i + by < count
    ]
    return lax.ppermute(x, ("section", "y", "x"), pairs)


def gather_weights(shard, section, place, plan, shapes):
    half = ROWS // 2
    above = along_z(shard, section, -1)
    below = along_z(shard, section, 1)
    first = along_z(below[:half], section, 1)
    second = along_z(above[half:], section, -1)
    pieces = (
        (shard, 0, 0, ROWS),
        (above, 1, 0, ROWS),
        (below, 3, 0, ROWS),
        (first, 2, 0, half),
        (second, 2, half, half),
    )
    return unpack_full(place, pieces, plan, shapes)


def reduce_z(place, section, arrays, plan, cols):
    own, after, before, far_a, far_b = pack_blocks(place, arrays, plan, cols)
    half = ROWS // 2
    got_a = along_z(far_a, section, 1)
    got_b = along_z(far_b, section, -1)
    after = lax.dynamic_update_slice(after, after[:half] + got_a, (0, 0))
    before = lax.dynamic_update_slice(before, before[half:] + got_b, (half, 0))
    left = along_z(after, section, 1)
    right = along_z(before, section, -1)
    return own, left, right


def total_of(parts):
    own, left, right = (item.astype(jnp.float32) for item in parts)
    return own + left + right


def normalize(values, gain):
    return values * lax.rsqrt(jnp.mean(values * values, axis=-1, keepdims=True) + EPSILON) * gain


def product(left, right):
    return jnp.dot(left, right, preferred_element_type=jnp.float32)


def inner_rows(left, right):
    return lax.dot_general(
        left, right, (((0,), (0,)), ((), ())), preferred_element_type=jnp.float32
    ).astype(jnp.bfloat16)


def against(left, right):
    return lax.dot_general(
        left, right, (((1,), (1,)), ((), ())), preferred_element_type=jnp.float32
    )


def turn(values, cosine, sine):
    half = values.shape[-1] // 2
    former = values[..., :half]
    latter = values[..., half:]
    return jnp.concatenate(
        [former * cosine - latter * sine, latter * cosine + former * sine], axis=-1
    )


def batched(spec, left, right):
    return jnp.einsum(spec, left, right, preferred_element_type=jnp.float32)


def forward_layer(inputs, tables, allowed, attn_w, ffn_w, gains, section):
    qkv_w, output_w = attn_w
    gate_up_w, down_w = ffn_w
    pre_g, query_g, key_g, mix_g, ffn_g, out_g = gains
    cosine, sine = tables
    normed = normalize(inputs, pre_g).astype(jnp.bfloat16)
    key_value = product(normed, qkv_w[:, QH * HD :])
    key_raw = key_value[:, :HD]
    values = key_value[:, HD:].astype(jnp.bfloat16)
    key_rot = turn(normalize(key_raw, key_g), cosine, sine).astype(jnp.bfloat16)
    own = jnp.stack([key_rot, values]).reshape(2, MICRO, SHARD, HD)
    pieces = [along_seq(own, section, by) for by in range(HOPS, 0, -1)]
    query_raw = product(normed, qkv_w[:, : QH * HD]).reshape(MICRO, SHARD, QH, HD)
    query_raw = jnp.swapaxes(query_raw, 1, 2)
    query_rot = turn(
        normalize(query_raw, query_g),
        cosine.reshape(MICRO, 1, SHARD, HD // 2),
        sine.reshape(MICRO, 1, SHARD, HD // 2),
    ).astype(jnp.bfloat16)
    joined = jnp.concatenate(pieces + [own], axis=2)
    keys_all, values_all = joined[0], joined[1]
    raw = batched("mhqd,mkd->mhqk", query_rot, keys_all)
    score = jnp.where(allowed[:, None], raw * HD ** (-0.5), -1e30)
    highest = jnp.max(score, axis=-1, keepdims=True)
    expo = jnp.exp(score - highest)
    prob = expo / jnp.sum(expo, axis=-1, keepdims=True)
    mixed = batched("mhqk,mkd->mhqd", prob.astype(jnp.bfloat16), values_all).astype(jnp.bfloat16)
    mixed = jnp.swapaxes(mixed, 1, 2).reshape(TOKENS, QH * HD)
    branch = product(mixed, output_w)
    middle = inputs + normalize(branch, mix_g)
    inner = normalize(middle, ffn_g).astype(jnp.bfloat16)
    gate_up = product(inner, gate_up_w)
    gate_act = gate_up[:, :FF]
    up_act = gate_up[:, FF:]
    hidden = (jax.nn.gelu(gate_act) * up_act).astype(jnp.bfloat16)
    down = product(hidden, down_w)
    result = (middle + normalize(down, out_g)).astype(jnp.bfloat16)
    stored = (
        inputs, normed, query_raw, key_raw, query_rot, keys_all, values_all, prob, mixed, branch,
        middle, inner, gate_act, up_act, hidden, down,
    )
    return result, stored


def norm_back(grad, values, gain):
    scale = lax.rsqrt(jnp.mean(values * values, axis=-1, keepdims=True) + EPSILON)
    unit = values * scale
    weighted = grad * gain
    dv = scale * (weighted - unit * jnp.mean(weighted * unit, axis=-1, keepdims=True))
    return dv, grad * unit


def backward_layer(grad_out, stored, tables, attn_w, ffn_w, gains, section, place, merge):
    (
        inputs, normed, query_raw, key_raw, query_rot, keys_all, values_all, prob, mixed, branch,
        middle, inner, gate_act, up_act, hidden, down,
    ) = stored
    qkv_w, output_w = attn_w
    gate_up_w, down_w = ffn_w
    pre_g, query_g, key_g, mix_g, ffn_g, out_g = gains
    cosine, sine = tables
    d_down, by_out = norm_back(grad_out, down, out_g)
    d_out_g = jnp.sum(by_out, axis=0)
    d_down = d_down.astype(jnp.bfloat16)
    d_hidden = against(d_down, down_w)
    _, pull = jax.vjp(
        lambda gate_in, up_in: jax.nn.gelu(gate_in) * up_in, gate_act, up_act
    )
    d_gate, d_up = pull(d_hidden)
    d_gate_up = jnp.concatenate([d_gate.astype(jnp.bfloat16), d_up.astype(jnp.bfloat16)], axis=1)
    d_inner = against(d_gate_up, gate_up_w)
    d_middle_ffn, by_ffn = norm_back(d_inner, middle, ffn_g)
    d_ffn_g = jnp.sum(by_ffn, axis=0)
    d_middle = grad_out + d_middle_ffn
    d_branch, by_mix = norm_back(d_middle, branch, mix_g)
    d_mix_g = jnp.sum(by_mix, axis=0)
    d_branch = d_branch.astype(jnp.bfloat16)
    d_mixed = against(d_branch, output_w).astype(jnp.bfloat16).reshape(MICRO, SHARD, QH, HD)
    d_mixed = jnp.swapaxes(d_mixed, 1, 2)
    d_prob = batched("mhqd,mkd->mhqk", d_mixed, values_all)
    d_score = (prob * (d_prob - jnp.sum(prob * d_prob, axis=-1, keepdims=True))).astype(
        jnp.bfloat16
    )
    scale = HD ** (-0.5)
    d_keys = batched("mhqk,mhqd->mkd", d_score, query_rot) * scale
    d_values_all = batched("mhqk,mhqd->mkd", prob.astype(jnp.bfloat16), d_mixed)
    d_stacked = jnp.stack([d_keys, d_values_all])
    back = d_stacked[:, :, HOPS * SHARD :]
    for offset in range(HOPS):
        piece = d_stacked[:, :, offset * SHARD : (offset + 1) * SHARD].astype(jnp.bfloat16)
        back = back + along_seq(piece, section, offset - HOPS).astype(jnp.float32)
    back = back.reshape(2, TOKENS, HD)
    grad_ffn = (inner_rows(inner, d_gate_up), inner_rows(hidden, d_down))
    ffn_parts = None if merge else reduce_z(place, section, grad_ffn, FFN_GRAD_PLAN, FFN_COLS)
    d_query_rot = batched("mhqk,mkd->mhqd", d_score, keys_all) * scale
    d_query, by_query = norm_back(
        turn(
            d_query_rot,
            cosine.reshape(MICRO, 1, SHARD, HD // 2),
            -sine.reshape(MICRO, 1, SHARD, HD // 2),
        ),
        query_raw,
        query_g,
    )
    d_query_g = jnp.sum(by_query, axis=(0, 1, 2))
    d_query = jnp.swapaxes(d_query.astype(jnp.bfloat16), 1, 2).reshape(TOKENS, QH * HD)
    d_values = back[1].astype(jnp.bfloat16)
    d_key, by_key = norm_back(turn(back[0], cosine, -sine), key_raw, key_g)
    d_key_g = jnp.sum(by_key, axis=0)
    d_qkv = jnp.concatenate([d_query, d_key.astype(jnp.bfloat16), d_values], axis=1)
    d_normed = against(d_qkv, qkv_w)
    d_inputs_pre, by_pre = norm_back(d_normed, inputs, pre_g)
    d_pre_g = jnp.sum(by_pre, axis=0)
    d_inputs = d_middle + d_inputs_pre
    grad_attn = (inner_rows(normed, d_qkv), inner_rows(mixed, d_branch))
    gain_grads = jnp.concatenate([d_pre_g, d_query_g, d_key_g, d_mix_g, d_ffn_g, d_out_g])
    return d_inputs, grad_ffn, ffn_parts, grad_attn, gain_grads


GAIN_SIZES = (D, HD, HD, D, D, D)


def per_device(
    hidden_in, positions, segments, cotangent,
    query_weight, key_weight, value_weight, output_weight, gate_weight, up_weight, down_weight,
    pre_gain, query_gain, key_gain, mix_gain, ffn_gain, out_gain,
):
    leading = lax.axis_index("section") == 0
    z_index = lax.axis_index("z")
    seq_index = lax.axis_index("y") * RING + lax.axis_index("x")
    place = jnp.reshape(z_index, (1,)).astype(jnp.int32)

    attn_shard = pack_shard(
        (query_weight[0], key_weight[0], value_weight[0], output_weight[0]), ATTN_PLAN, ATTN_COLS
    )
    ffn_shard = pack_shard((gate_weight[0], up_weight[0], down_weight[0]), FFN_PLAN, FFN_COLS)
    full_attn_plan = ATTN_GRAD_PLAN
    full_ffn_plan = FFN_GRAD_PLAN
    attn_shapes = ((D, QH * HD + 2 * HD), (QH * HD, D))
    ffn_shapes = ((D, 2 * FF), (FF, D))
    weights = []
    for section in range(2):
        attn = gather_weights(attn_shard, section, place, full_attn_plan, attn_shapes)
        ffn = gather_weights(ffn_shard, section, place, full_ffn_plan, ffn_shapes)
        weights.append((attn, ffn))

    packed_gains = jnp.concatenate(
        [item[0] for item in (pre_gain, query_gain, key_gain, mix_gain, ffn_gain, out_gain)]
    )
    all_gains = lax.all_gather(packed_gains, "z").astype(jnp.float32)
    gains = []
    start = 0
    for size in GAIN_SIZES:
        part = size // RING
        gains.append(all_gains[:, start : start + part].reshape(size))
        start += part

    exponent = jnp.arange(HD // 2).astype(jnp.float32) * (2.0 / HD)
    freqs = ROPE_BASE ** (-exponent)
    angle = positions[:, 0].reshape(TOKENS).astype(jnp.float32)[:, None] * freqs[None, :]
    tables = (jnp.cos(angle), jnp.sin(angle))

    segment_rows = segments[:, 0]
    anchor = seq_index * SHARD
    padded = jnp.concatenate([jnp.full((MICRO, WINDOW), -1, jnp.int32), segment_rows], axis=1)
    query_seg = lax.dynamic_slice_in_dim(segment_rows, anchor, SHARD, 1)
    key_seg = lax.dynamic_slice_in_dim(padded, anchor, KEYS, 1)
    gap = (jnp.arange(SHARD, dtype=jnp.int32) + WINDOW)[:, None] - jnp.arange(
        KEYS, dtype=jnp.int32
    )[None, :]
    allowed = (gap >= 0) & (gap < WINDOW)
    allowed = allowed[None] & (query_seg[:, :, None] == key_seg[:, None, :])

    first_in = hidden_in[:, 0].reshape(TOKENS, D).astype(jnp.float32)
    first_out, first_kept = forward_layer(first_in, tables, allowed, *weights[0], gains, 0)
    handed = lax.ppermute(first_out, "section", [(0, 1)]).astype(jnp.float32)
    second_out, second_kept = forward_layer(handed, tables, allowed, *weights[1], gains, 1)

    cot = cotangent[:, 0].reshape(TOKENS, D).astype(jnp.float32)
    d_second, ffn_grad1, _, attn_grad1, gain_grad1 = backward_layer(
        cot, second_kept, tables, *weights[1], gains, 1, place, True
    )
    d_first_out = lax.ppermute(d_second.astype(jnp.bfloat16), "section", [(1, 0)])
    ffn_parts1 = reduce_z(place, 1, ffn_grad1, FFN_GRAD_PLAN, FFN_COLS)
    attn_parts1 = reduce_z(place, 1, attn_grad1, ATTN_GRAD_PLAN, ATTN_COLS)
    d_first, _, ffn_parts0, attn_grad0, gain_grad0 = backward_layer(
        d_first_out.astype(jnp.float32), first_kept, tables, *weights[0], gains, 0, place, False
    )
    attn_parts0 = reduce_z(place, 0, attn_grad0, ATTN_GRAD_PLAN, ATTN_COLS)

    def finish(parts0, parts1, cols):
        mine = jnp.where(leading, total_of(parts0), total_of(parts1)).astype(jnp.bfloat16)
        count = RING * RING
        split = mine.reshape(count, ROWS // count, cols)
        moved = lax.all_to_all(split, ("y", "x"), split_axis=0, concat_axis=0, tiled=True)
        summed = jnp.sum(moved.astype(jnp.float32), axis=0).astype(jnp.bfloat16)
        return lax.all_gather(summed, ("y", "x"), axis=0, tiled=True)

    ffn_done = finish(ffn_parts0, ffn_parts1, FFN_COLS)
    attn_done = finish(attn_parts0, attn_parts1, ATTN_COLS)
    gain_total = lax.psum(jnp.where(leading, gain_grad0, gain_grad1), ("y", "x", "z"))

    def restore(packed, plan, which):
        return jnp.concatenate(
            [packed[pr : pr + n, pc : pc + w] for a, r, n, c, w, pr, pc in plan if a == which]
        ).astype(jnp.float32)[None]

    gain_outs = []
    start = 0
    for size in GAIN_SIZES:
        part = size // RING
        gain_outs.append(lax.dynamic_slice(gain_total, (start + z_index * part,), (part,))[None])
        start += size
    outputs = jnp.where(leading, first_out, second_out).reshape(1, MICRO, 1, SHARD, D)
    input_grads = jnp.where(leading, d_first, d_second).reshape(1, MICRO, 1, SHARD, D)
    return (
        outputs,
        input_grads,
        restore(attn_done, ATTN_PLAN, 0),
        restore(attn_done, ATTN_PLAN, 1),
        restore(attn_done, ATTN_PLAN, 2),
        restore(attn_done, ATTN_PLAN, 3),
        restore(ffn_done, FFN_PLAN, 0),
        restore(ffn_done, FFN_PLAN, 1),
        restore(ffn_done, FFN_PLAN, 2),
    ) + tuple(gain_outs)


def solution(mesh):
    grid = Mesh(
        mesh.devices.reshape(2, RING, RING, RING), ("section", "y", "x", "z")
    )
    seq = ("y", "x")
    in_specs = (
        P(None, "z", seq, None),
        P(None, "z", seq),
        P(None, "z", None),
        P(None, "z", seq, None),
    ) + (P("section", "z", None),) * 7 + (P("section", "z"),) * 6
    out_specs = (
        (P("section", None, "z", seq, None),) * 2
        + (P("section", "z", None),) * 7
        + (P("section", "z"),) * 6
    )
    return jax.shard_map(
        per_device, mesh=grid, in_specs=in_specs, out_specs=out_specs, check_vma=False
    )
```

time: 1340 us -> 2290 us (1.71)
  Pallas kernels: 0 us -> 1450 us
  blocking collectives: 670 us -> 398 us
  waiting for transfers between devices: 207 us -> 52.6 us
  local copies, waits for them, and re-layouts: 122 us -> 66 us
  matrix products: 140 us -> 90.5 us
  starting transfers between devices: 110 us -> 144 us
    pallas_call x0 -> x10, Pallas kernels: none -> 1450 us  [the longest x4 680 us: unpack_full(): pl.pallas_call(body, in_specs=[pl.BlockSpec(memory_space=pltpu.SMEM)] + i...]
    unnamed x3 -> x0, blocking collectives: 485 us -> none
    psum x0 -> x1, blocking collectives: none -> 346 us  [per_device(): lax.psum(jnp.where(leading, gain_grad0, gain_grad1), ('y', 'x', 'z'))]
    all_gather x9 -> x2, blocking collectives: 185 us -> 51.8 us  [the longest x1 30.2 us: per_device(): all_gains = lax.all_gather(packed_gains, 'z').astype(jnp.float32)]
    all_gather x5 -> x1, waiting for transfers between devices: 82.2 us -> 0.01 us  [finish(): return lax.all_gather(summed, ('y', 'x'), axis=0, tiled=True)]
    ppermute x38 -> x50, waiting for transfers between devices: 122 us -> 52.5 us  [the longest x32 39 us: along_z(): return lax.ppermute(x, ('section', 'z'), pairs)]
    dot_general x28 -> x8, matrix products: 71.5 us -> 27 us  [inner_rows(): lax.dot_general(left, right, (((0,), (0,)), ((), ())), preferred_element_...]
    reshape x16 -> x3, local copies, waits for them, and re-layouts: 40.5 us -> 7.26 us  [the longest x2 5.28 us: backward_layer(): against(d_branch, output_w).astype(jnp.bfloat16)]
  transfers between devices with their start and end apart: 45 -> 53, of which waited for: 33 -> 7; matrix products, arithmetic and copies ran while one was open for 16% -> 6% of each run, Pallas kernels for 0% -> 62%
where the time goes in v1:
time: 2290 us; the launch traced here: 2280 us
  Pallas kernels  1450 us (63%)
  blocking collectives  398 us (17%)
  starting transfers between devices  144 us (6%)
  matrix products  90.5 us (4%)
  local copies, waits for them, and re-layouts  66 us (3%)
  other arithmetic  65.4 us (3%)
  waiting for transfers between devices  52.6 us (2%)
    pallas_call x4, Pallas kernels, unpack_full(): pl.pallas_call(body, in_specs=[pl.BlockSpec(memory_space=pltpu.SMEM)] + i...  680 us
    pallas_call x4, Pallas kernels, pack_blocks(): pl.pallas_call(body, in_specs=[pl.BlockSpec(memory_space=pltpu.SMEM)] + i...  680 us
    psum x1, blocking collectives, per_device(): lax.psum(jnp.where(leading, gain_grad0, gain_grad1), ('y', 'x', 'z'))  346 us
    ppermute x32, starting transfers between devices, along_z(): return lax.ppermute(x, ('section', 'z'), pairs)  89 us
    pallas_call x2, Pallas kernels, pack_shard(): pl.pallas_call(body, in_specs=in_any(len(arrays)), out_specs=pl.BlockSpec...  86.7 us
  transfers between devices with their start and end apart: 53, of which 7 were waited for; matrix products, arithmetic and copies ran while one was open for 6% of the time, Pallas kernels for 62%

profile of v1, /device:TPU:0, one launch (start us, length us, event | category | flops | bytes accessed | tf_op | source)
XLA Modules:
  0.0 2280.7 jit_solution(4069923049328242931)
XLA Ops:
  7.2 26.0 %pack_shard.2.refs_0_ = bf16[256,1920]{1,0:T(8,128)(2,1)} custom-call(bf16[160,1024]{1,0:T(8,128)(2,1)} %bitcast.343, bf16[160,256]{1,0:T(8,128)(2,1)} %bitcast.352, bf16[160,256]{1,0:T(8,128)(2,1)} %bitcast.353, bf16[256,640]{1,0:T(8,128)(2,1)} %bitcast.344), custom_call_target="tpu_custom_call" | custom-call | tf_op jit(solution)/shard_map/pack_shard/pallas_call | solution.py:70
  33.2 6.2 collective-permute-start
  44.7 60.7 %pack_shard.3.refs_0_ = bf16[256,4096]{1,0:T(8,128)(2,1)} custom-call(bf16[160,2048]{1,0:T(8,128)(2,1)} %bitcast.339, bf16[160,2048]{1,0:T(8,128)(2,1)} %bitcast.340, bf16[512,640]{1,0:T(8,128)(2,1)} %bitcast.341), custom_call_target="tpu_custom_call" | custom-call | tf_op jit(solution)/shard_map/pack_shard/pallas_call | solution.py:70
  105.4 5.1 collective-permute-start.8
  110.8 30.2 %all-gather.1 = bf16[4,1,768]{2,1,0:T(2,128)(2,1)S(1)} all-gather(bf16[1,1,768]{2,1,0:T(2,128)(2,1)S(1)} %reshape.592), channel_id=2, replica_groups=mesh['section'=2,'y'=4,'x'=4,'z'=4] {'z'}, dimensions={0}, use_global_device_ids=true | all-gather | bytes 7680 | tf_op jit(solution)/shard_map/all_gather | solution.py:385
  144.5 4.2 collective-permute-start.2
  150.5 3.0 collective-permute-start.3
  155.9 2.8 collective-permute-start.9
  162.4 100.5 %unpack_full.4 = (bf16[640,1536]{1,0:T(8,128)(2,1)}, bf16[1024,640]{1,0:T(8,128)(2,1)}) custom-call(s32[1]{0:T(128)} %bitcast.6.place_ref, bf16[256,1920]{1,0:T(8,128)(2,1)} %pack_shard.2.refs_0_, bf16[256,1920]{1,0:T(8,128)(2,1)} %collective-permute-done.refs_1_, bf16[256,1920]{1,0:T(8,128)(2,1)} %collective-permute-done.1.refs_2_, ...), custom_call_target="tpu_custom_call" | custom-call | tf_op jit(solution)/shard_map/unpack_full/pallas_call | solution.py:108
  267.2 4.2 collective-permute-start.4
  271.4 5.4 collective-permute-start.5
  276.8 3.7 collective-permute-start.6
  281.8 2.4 copy.82
  284.2 2.2 fusion.31
  298.9 2.1 slice.359
  301.0 2.4 collective-permute-start.10
  304.7 4.6 collective-permute-start.11
  313.4 13.5 collective-permute-start.16
  333.4 239.6 %unpack_full.5 = (bf16[640,4096]{1,0:T(8,128)(2,1)}, bf16[2048,640]{1,0:T(8,128)(2,1)}) custom-call(s32[1]{0:T(128)} %bitcast.6.place_ref, bf16[256,4096]{1,0:T(8,128)(2,1)} %pack_shard.3.refs_0_, bf16[256,4096]{1,0:T(8,128)(2,1)} %collective-permute-done.8.refs_1_, bf16[256,4096]{1,0:T(8,128)(2,1)} %collective-permute-done.9.refs_2_, ...), custom_call_target="tpu_custom_call" | custom-call | tf_op jit(solution)/shard_map/unpack_full/pallas_call | solution.py:108
  573.0 4.7 fusion.178
  585.4 100.5 %unpack_full.6 = (bf16[640,1536]{1,0:T(8,128)(2,1)}, bf16[1024,640]{1,0:T(8,128)(2,1)}) custom-call(s32[1]{0:T(128)} %bitcast.6.place_ref, bf16[256,1920]{1,0:T(8,128)(2,1)} %pack_shard.2.refs_0_, bf16[256,1920]{1,0:T(8,128)(2,1)} %collective-permute-done.13.refs_1_, bf16[256,1920]{1,0:T(8,128)(2,1)} %collective-permute-done.14.refs_2_, ...), custom_call_target="tpu_custom_call" | custom-call | tf_op jit(solution)/shard_map/unpack_full/pallas_call | solution.py:108
  685.9 239.6 %unpack_full.7 = (bf16[640,4096]{1,0:T(8,128)(2,1)}, bf16[2048,640]{1,0:T(8,128)(2,1)}) custom-call(s32[1]{0:T(128)} %bitcast.6.place_ref, bf16[256,4096]{1,0:T(8,128)(2,1)} %pack_shard.3.refs_0_, bf16[256,4096]{1,0:T(8,128)(2,1)} %copy-done.32, bf16[256,4096]{1,0:T(8,128)(2,1)} %copy-done.33, bf16[128,4096]{1,0:T(8,128)(2,1)} %collective-permute-done.23.refs_3_, ...), custom_call_target="tpu_custom_call" | custom-call | tf_op jit(solution)/shard_map/unpack_full/pallas_call | solution.py:108
  952.7 2.7 fusion.179
  960.0 3.9 fusion.17
  964.0 3.3 multiply_reduce_fusion.6
  972.1 2.6 reshape.576
  974.8 3.7 multiply_reduce_fusion.1
  987.2 5.1 convolution_convert_fusion.refs_0_
  992.3 3.2 convolution_convert_fusion.2.refs_1_
  1006.9 239.6 %pack_blocks.7 = (bf16[256,4096]{1,0:T(8,128)(2,1)}, bf16[256,4096]{1,0:T(8,128)(2,1)}, bf16[256,4096]{1,0:T(8,128)(2,1)}, bf16[128,4096]{1,0:T(8,128)(2,1)}, bf16[128,4096]{1,0:T(8,128)(2,1)}) custom-call(s32[1]{0:T(128)} %bitcast.6.place_ref, bf16[640,4096]{1,0:T(8,128)(2,1)} %convolution_convert_fusion.refs_0_, ...), custom_call_target="tpu_custom_call" | custom-call | tf_op jit(solution)/shard_map/pack_blocks/pallas_call | solution.py:147
  1257.5 2.6 convolution_convert_fusion.4.refs_0_
  1260.2 100.5 %pack_blocks.5 = (bf16[256,1920]{1,0:T(8,128)(2,1)}, bf16[256,1920]{1,0:T(8,128)(2,1)}, bf16[256,1920]{1,0:T(8,128)(2,1)}, bf16[128,1920]{1,0:T(8,128)(2,1)}, bf16[128,1920]{1,0:T(8,128)(2,1)}) custom-call(s32[1]{0:T(128)} %bitcast.6.place_ref, bf16[640,1536]{1,0:T(8,128)(2,1)} %convolution_convert_fusion.4.refs_0_, ...), custom_call_target="tpu_custom_call" | custom-call | tf_op jit(solution)/shard_map/pack_blocks/pallas_call | solution.py:147
  1362.4 5.5 fusion.10
  1368.0 6.4 multiply_reduce_fusion.8
  1378.5 2.6 reshape.578
  1381.2 3.4 multiply_reduce_fusion
  1386.4 3.3 convolution_convert_fusion.3.refs_1_
  1398.7 4.9 convolution_convert_fusion.1.refs_0_
  1404.7 239.6 %pack_blocks.6 = (bf16[256,4096]{1,0:T(8,128)(2,1)}, bf16[256,4096]{1,0:T(8,128)(2,1)}, bf16[256,4096]{1,0:T(8,128)(2,1)}, bf16[128,4096]{1,0:T(8,128)(2,1)}, bf16[128,4096]{1,0:T(8,128)(2,1)}) custom-call(s32[1]{0:T(128)} %bitcast.6.place_ref, bf16[640,4096]{1,0:T(8,128)(2,1)} %convolution_convert_fusion.1.refs_0_, ...), custom_call_target="tpu_custom_call" | custom-call | tf_op jit(solution)/shard_map/pack_blocks/pallas_call | solution.py:147
  1644.4 3.3 collective-permute-start.44
  1647.7 2.9 add_dynamic-update-slice_fusion
  1650.7 2.8 collective-permute-start.42
  1655.2 10.8 collective-permute-done.44
  1667.3 8.9 collective-permute-done.42
  1679.6 3.9 collective-permute-start.43
  1689.8 13.5 collective-permute-done.30
  1711.6 7.5 collective-permute-done.43
  1719.1 3.7 select_convert_fusion
  1722.8 11.5 all-to-all-start.1
  1734.4 3.8 convolution_convert_fusion.5.refs_0_
  1738.2 100.5 %pack_blocks.4 = (bf16[256,1920]{1,0:T(8,128)(2,1)}, bf16[256,1920]{1,0:T(8,128)(2,1)}, bf16[256,1920]{1,0:T(8,128)(2,1)}, bf16[128,1920]{1,0:T(8,128)(2,1)}, bf16[128,1920]{1,0:T(8,128)(2,1)}) custom-call(s32[1]{0:T(128)} %bitcast.6.place_ref, bf16[640,1536]{1,0:T(8,128)(2,1)} %convolution_convert_fusion.5.refs_0_, ...), custom_call_target="tpu_custom_call" | custom-call | tf_op jit(solution)/shard_map/pack_blocks/pallas_call | solution.py:147
  1838.7 2.8 collective-permute-start.36
  1841.5 2.1 add_dynamic-update-slice_fusion.4
  1845.3 3.0 collective-permute-start.34
  1848.3 2.1 add_dynamic-update-slice_fusion.5
  1853.9 4.1 collective-permute-start.37
  1863.0 4.0 fusion.71
  1867.1 3.3 collective-permute-done.37
  1870.4 7.2 collective-permute-done.35
  1877.6 3.8 select_convert_fusion.1
  1881.4 7.5 all-to-all-start
  1888.9 346.5 %psum.7 = f32[3072]{0:T(1024)S(1)} all-reduce(f32[3072]{0:T(1024)S(1)} %broadcast_select_fusion), channel_id=1, replica_groups=mesh['section'=2,'y'=4,'x'=4,'z'=4] {'y','x','z'}, use_global_device_ids=true, to_apply=%region_44.45 | all-reduce | flops 3072 | bytes 24576 | tf_op jit(solution)/shard_map/psum | solution.py:436
  2236.7 3.0 fusion.70
  2241.0 21.6 all_gather.14
  (616 shorter events, 182.4 us)
Async XLA Ops:
  33.2 115.4 %collective-permute-start = (bf16[256,1920]{1,0:T(8,128)(2,1)}, bf16[256,1920]{1,0:T(8,128)(2,1)}, u32[]{:S(2)}, u32[]{:S(2)}) collective-permute-start(bf16[256,1920]{1,0:T(8,128)(2,1)} %pack_shard.2.refs_0_), channel_id=1, source_target_pairs={{0,3},{1,0},{2,1},{3,2},{4,7},{5,4},{6,5},{7,6},{8,11},{9,8},{10,9... | collective-permute-start | bytes 2949128 | tf_op jit(solution)/shard_map/ppermute | solution.py:159
  39.4 103.2 %collective-permute-start.1 = (bf16[256,1920]{1,0:T(8,128)(2,1)}, bf16[256,1920]{1,0:T(8,128)(2,1)}, u32[]{:S(2)}, u32[]{:S(2)}) collective-permute-start(bf16[256,1920]{1,0:T(8,128)(2,1)} %pack_shard.2.refs_0_), channel_id=1, source_target_pairs={{0,1},{1,2},{2,3},{3,0},{4,5},{5,6},{6,7},{7,4},{8,9},{9,10},{10,1... | collective-permute-start | bytes 2949128 | tf_op jit(solution)/shard_map/ppermute | solution.py:159
  41.3 119.2 %collective-permute-start.13 = (bf16[256,1920]{1,0:T(8,128)(2,1)}, bf16[256,1920]{1,0:T(8,128)(2,1)}, u32[]{:S(2)}, u32[]{:S(2)}) collective-permute-start(bf16[256,1920]{1,0:T(8,128)(2,1)} %pack_shard.2.refs_0_), channel_id=1, source_target_pairs={{64,67},{65,64},{66,65},{67,66},{68,71},{69,68},{70,69},{71,70},{7... | collective-permute-start | bytes 2949128 | tf_op jit(solution)/shard_map/ppermute | solution.py:159
  43.0 112.8 %collective-permute-start.14 = (bf16[256,1920]{1,0:T(8,128)(2,1)}, bf16[256,1920]{1,0:T(8,128)(2,1)}, u32[]{:S(2)}, u32[]{:S(2)}) collective-permute-start(bf16[256,1920]{1,0:T(8,128)(2,1)} %pack_shard.2.refs_0_), channel_id=1, source_target_pairs={{64,65},{65,66},{66,67},{67,64},{68,69},{69,70},{70,71},{71,68},{7... | collective-permute-start | bytes 2949128 | tf_op jit(solution)/shard_map/ppermute | solution.py:159
  105.4 198.0 %collective-permute-start.8 = (bf16[256,4096]{1,0:T(8,128)(2,1)}, bf16[256,4096]{1,0:T(8,128)(2,1)}, u32[]{:S(2)}, u32[]{:S(2)}) collective-permute-start(bf16[256,4096]{1,0:T(8,128)(2,1)} %pack_shard.3.refs_0_), channel_id=1, source_target_pairs={{0,3},{1,0},{2,1},{3,2},{4,7},{5,4},{6,5},{7,6},{8,11},{9,8},{10,9... | collective-permute-start | bytes 6291464 | tf_op jit(solution)/shard_map/ppermute | solution.py:159
  141.3 786.6 %copy-start.117 = (f32[3,128]{1,0:T(4,128)}, f32[3,128]{1,0:T(4,128)S(1)}, u32[]{:S(2)}) copy-start(f32[3,128]{1,0:T(4,128)S(1)} %convert_reduce_fusion) | copy-start | bytes 4612
  144.5 17.9 collective-permute-start.2
  150.5 11.9 collective-permute-start.3
  153.8 781.5 %copy-start.115 = (f32[640]{0:T(1024)}, f32[640]{0:T(1024)S(1)}, u32[]{:S(2)}) copy-start(f32[640]{0:T(1024)S(1)} %mul.970) | copy-start | bytes 7684
  153.9 773.9 %copy-start.122 = (f32[256]{0:T(256)}, f32[256]{0:T(256)S(1)}, u32[]{:S(2)}) copy-start(f32[256]{0:T(256)S(1)} %mul.997) | copy-start | bytes 3076
  153.9 785.7 %copy-start.119 = (f32[256]{0:T(256)}, f32[256]{0:T(256)S(1)}, u32[]{:S(2)}) copy-start(f32[256]{0:T(256)S(1)} %mul.976) | copy-start | bytes 3076
  154.1 428.7 %copy-start.108 = (f32[640]{0:T(1024)}, f32[640]{0:T(1024)S(1)}, u32[]{:S(2)}) copy-start(f32[640]{0:T(1024)S(1)} %mul.1028) | copy-start | bytes 7684
  155.6 784.4 %copy-start.29 = (f32[3,128,128]{2,1,0:T(8,128)}, f32[3,128,128]{2,1,0:T(8,128)S(1)}, u32[]{:S(2)}) copy-start(f32[3,128,128]{2,1,0:T(8,128)S(1)} %get-tuple-element.194) | copy-start | bytes 589828
  155.9 143.0 %collective-permute-start.9 = (bf16[256,4096]{1,0:T(8,128)(2,1)S(1)}, bf16[256,4096]{1,0:T(8,128)(2,1)}, u32[]{:S(2)}, u32[]{:S(2)}) collective-permute-start(bf16[256,4096]{1,0:T(8,128)(2,1)S(1)} %copy-done.1), channel_id=1, source_target_pairs={{0,1},{1,2},{2,3},{3,0},{4,5},{5,6},{6,7},{7,4},{8,9},{9,10},{10,1... | collective-permute-start | bytes 6291464 | tf_op jit(solution)/shard_map/ppermute | solution.py:159
  267.2 19.6 collective-permute-start.4
  271.4 19.1 collective-permute-start.5
  276.8 15.5 collective-permute-start.6
  286.8 7.4 collective-permute-start.7
  290.5 37.5 %collective-permute-start.21 = (bf16[256,4096]{1,0:T(8,128)(2,1)S(1)}, bf16[256,4096]{1,0:T(8,128)(2,1)S(1)}, u32[]{:S(2)}, u32[]{:S(2)}) collective-permute-start(bf16[256,4096]{1,0:T(8,128)(2,1)S(1)} %copy-done.1), channel_id=1, source_target_pairs={{64,67},{65,64},{66,65},{67,66},{68,71},{69,68},{70,69},{71,70},{7... | collective-permute-start | bytes 6291464 | tf_op jit(solution)/shard_map/ppermute | solution.py:159
  292.3 21.0 collective-permute-start.22
  294.2 291.2 %collective-permute-start.15 = (bf16[128,1920]{1,0:T(8,128)(2,1)}, bf16[128,1920]{1,0:T(8,128)(2,1)}, u32[]{:S(2)}, u32[]{:S(2)}) collective-permute-start(bf16[128,1920]{1,0:T(8,128)(2,1)} %slice.364), channel_id=1, source_target_pairs={{64,65},{65,66},{66,67},{67,64},{68,69},{69,70},{70,71},{71,68},{7... | collective-permute-start | bytes 1474568 | tf_op jit(solution)/shard_map/ppermute | solution.py:159
  301.0 29.8 %collective-permute-start.10 = (bf16[128,4096]{1,0:T(8,128)(2,1)S(1)}, bf16[128,4096]{1,0:T(8,128)(2,1)S(1)}, u32[]{:S(2)}, u32[]{:S(2)}) collective-permute-start(bf16[128,4096]{1,0:T(8,128)(2,1)S(1)} %slice.359), channel_id=1, source_target_pairs={{0,1},{1,2},{2,3},{3,0},{4,5},{5,6},{6,7},{7,4},{8,9},{9,10},{10,1... | collective-permute-start | bytes 3145736 | tf_op jit(solution)/shard_map/ppermute | solution.py:159
  304.7 28.7 %collective-permute-start.11 = (bf16[128,4096]{1,0:T(8,128)(2,1)S(1)}, bf16[128,4096]{1,0:T(8,128)(2,1)}, u32[]{:S(2)}, u32[]{:S(2)}) collective-permute-start(bf16[128,4096]{1,0:T(8,128)(2,1)S(1)} %slice.360), channel_id=1, source_target_pairs={{0,3},{1,0},{2,1},{3,2},{4,7},{5,4},{6,5},{7,6},{8,11},{9,8},{10,9... | collective-permute-start | bytes 3145736 | tf_op jit(solution)/shard_map/ppermute | solution.py:159
  313.4 272.0 %collective-permute-start.16 = (bf16[128,1920]{1,0:T(8,128)(2,1)}, bf16[128,1920]{1,0:T(8,128)(2,1)}, u32[]{:S(2)}, u32[]{:S(2)}) collective-permute-start(bf16[128,1920]{1,0:T(8,128)(2,1)} %slice.365), channel_id=1, source_target_pairs={{64,67},{65,64},{66,65},{67,66},{68,71},{69,68},{70,69},{71,70},{7... | collective-permute-start | bytes 1474568 | tf_op jit(solution)/shard_map/ppermute | solution.py:159
  328.0 357.9 %collective-permute-start.23 = (bf16[128,4096]{1,0:T(8,128)(2,1)}, bf16[128,4096]{1,0:T(8,128)(2,1)}, u32[]{:S(2)}, u32[]{:S(2)}) collective-permute-start(bf16[128,4096]{1,0:T(8,128)(2,1)} %slice.374), channel_id=1, source_target_pairs={{64,65},{65,66},{66,67},{67,64},{68,69},{69,70},{70,71},{71,68},{7... | collective-permute-start | bytes 3145736 | tf_op jit(solution)/shard_map/ppermute | solution.py:159
  331.8 354.2 %collective-permute-start.24 = (bf16[128,4096]{1,0:T(8,128)(2,1)}, bf16[128,4096]{1,0:T(8,128)(2,1)}, u32[]{:S(2)}, u32[]{:S(2)}) collective-permute-start(bf16[128,4096]{1,0:T(8,128)(2,1)} %slice.375), channel_id=1, source_target_pairs={{64,67},{65,64},{66,65},{67,66},{68,71},{69,68},{70,69},{71,70},{7... | collective-permute-start | bytes 3145736 | tf_op jit(solution)/shard_map/ppermute | solution.py:159
  584.0 341.6 %copy-start.53 = (bf16[384,640]{1,0:T(8,128)(2,1)}, bf16[384,640]{1,0:T(8,128)(2,1)S(1)}, u32[]{:S(2)}) copy-start(bf16[384,640]{1,0:T(8,128)(2,1)S(1)} %add_convert_fusion.1) | copy-start | bytes 1474564
  584.0 341.6 %collective-permute-start.12 = (bf16[384,640]{1,0:T(8,128)(2,1)S(1)}, bf16[384,640]{1,0:T(8,128)(2,1)S(1)}, u32[]{:S(2)}, u32[]{:S(2)}) collective-permute-start(bf16[384,640]{1,0:T(8,128)(2,1)S(1)} %add_convert_fusion.1), channel_id=1, source_target_pairs={{0,64},{1,65},{2,66},{3,67},{4,68},{5,69},{6,70},{7,71},{8,72},{9,... | collective-permute-start | bytes 1474568 | tf_op jit(solution)/shard_map/ppermute | solution.py:411
  929.5 11.0 collective-permute-start.17
  930.9 10.9 collective-permute-start.18
  932.4 10.5 collective-permute-start.19
  933.9 10.1 collective-permute-start.20
  997.1 252.2 %collective-permute-start.28 = (bf16[2,3,128,256]{3,2,1,0:T(8,128)(2,1)}, bf16[2,3,128,256]{3,2,1,0:T(8,128)(2,1)}, u32[]{:S(2)}, u32[]{:S(2)}) collective-permute-start(bf16[2,3,128,256]{3,2,1,0:T(8,128)(2,1)} %get-tuple-element.161), channel_id=1, source_target_pairs={{68,64},{72,68},{76,72},{80,76},{84,80},{88,84},{92,88},{96,92},{1... | collective-permute-start | bytes 1179656 | tf_op jit(solution)/shard_map/ppermute | solution.py:167
  998.7 252.4 %collective-permute-start.27 = (bf16[2,3,128,256]{3,2,1,0:T(8,128)(2,1)}, bf16[2,3,128,256]{3,2,1,0:T(8,128)(2,1)}, u32[]{:S(2)}, u32[]{:S(2)}) collective-permute-start(bf16[2,3,128,256]{3,2,1,0:T(8,128)(2,1)} %get-tuple-element.162), channel_id=1, source_target_pairs={{72,64},{76,68},{80,72},{84,76},{88,80},{92,84},{96,88},{100,92},{... | collective-permute-start | bytes 1179656 | tf_op jit(solution)/shard_map/ppermute | solution.py:167
  1000.1 251.0 %collective-permute-start.26 = (bf16[2,3,128,256]{3,2,1,0:T(8,128)(2,1)}, bf16[2,3,128,256]{3,2,1,0:T(8,128)(2,1)}, u32[]{:S(2)}, u32[]{:S(2)}) collective-permute-start(bf16[2,3,128,256]{3,2,1,0:T(8,128)(2,1)} %get-tuple-element.163), channel_id=1, source_target_pairs={{76,64},{80,68},{84,72},{88,76},{92,80},{96,84},{100,88},{104,92},... | collective-permute-start | bytes 1179656 | tf_op jit(solution)/shard_map/ppermute | solution.py:167
  1001.5 249.6 %collective-permute-start.25 = (bf16[2,3,128,256]{3,2,1,0:T(8,128)(2,1)}, bf16[2,3,128,256]{3,2,1,0:T(8,128)(2,1)}, u32[]{:S(2)}, u32[]{:S(2)}) collective-permute-start(bf16[2,3,128,256]{3,2,1,0:T(8,128)(2,1)} %get-tuple-element.160), channel_id=1, source_target_pairs={{80,64},{84,68},{88,72},{92,76},{96,80},{100,84},{104,88},{108,92}... | collective-permute-start | bytes 1179656 | tf_op jit(solution)/shard_map/ppermute | solution.py:167
  1006.9 241.4 %copy-start.110 = (f32[640]{0:T(1024)S(1)}, f32[640]{0:T(1024)}, u32[]{:S(2)}) copy-start(f32[640]{0:T(1024)} %copy-done.108) | copy-start | bytes 7684
  1006.9 241.4 %copy-start.133 = (f32[384]{0:T(512)S(1)}, f32[384]{0:T(512)}, u32[]{:S(2)}) copy-start(f32[384]{0:T(512)} %copy-done.132) | copy-start | bytes 4612
  1246.5 397.9 %collective-permute-start.48 = (bf16[128,4096]{1,0:T(8,128)(2,1)}, bf16[128,4096]{1,0:T(8,128)(2,1)}, u32[]{:S(2)}, u32[]{:S(2)}) collective-permute-start(bf16[128,4096]{1,0:T(8,128)(2,1)} %get-tuple-element.70), channel_id=1, source_target_pairs={{64,67},{65,64},{66,65},{67,66},{68,71},{69,68},{70,69},{71,70},{7... | collective-permute-start | bytes 3145736 | tf_op jit(solution)/shard_map/ppermute | solution.py:159
  1249.4 401.3 %collective-permute-start.46 = (bf16[128,4096]{1,0:T(8,128)(2,1)}, bf16[128,4096]{1,0:T(8,128)(2,1)}, u32[]{:S(2)}, u32[]{:S(2)}) collective-permute-start(bf16[128,4096]{1,0:T(8,128)(2,1)} %get-tuple-element.68), channel_id=1, source_target_pairs={{64,65},{65,66},{66,67},{67,64},{68,69},{69,70},{70,71},{71,68},{7... | collective-permute-start | bytes 3145736 | tf_op jit(solution)/shard_map/ppermute | solution.py:159
  1256.2 104.6 %collective-permute-start.29 = (bf16[384,640]{1,0:T(8,128)(2,1)S(1)}, bf16[384,640]{1,0:T(8,128)(2,1)S(1)}, u32[]{:S(2)}, u32[]{:S(2)}) collective-permute-start(bf16[384,640]{1,0:T(8,128)(2,1)S(1)} %fusion.183), channel_id=1, source_target_pairs={{64,0},{65,1},{66,2},{67,3},{68,4},{69,5},{70,6},{71,7},{72,8},{73... | collective-permute-start | bytes 1474568 | tf_op jit(solution)/shard_map/ppermute | solution.py:418
  1393.3 284.2 %collective-permute-start.33 = (bf16[2,3,128,256]{3,2,1,0:T(8,128)(2,1)}, bf16[2,3,128,256]{3,2,1,0:T(8,128)(2,1)}, u32[]{:S(2)}, u32[]{:S(2)}) collective-permute-start(bf16[2,3,128,256]{3,2,1,0:T(8,128)(2,1)} %get-tuple-element.155), channel_id=1, source_target_pairs={{4,0},{8,4},{12,8},{16,12},{20,16},{24,20},{28,24},{32,28},{36,32}... | collective-permute-start | bytes 1179656 | tf_op jit(solution)/shard_map/ppermute | solution.py:167
  1394.5 285.0 %collective-permute-start.32 = (bf16[2,3,128,256]{3,2,1,0:T(8,128)(2,1)}, bf16[2,3,128,256]{3,2,1,0:T(8,128)(2,1)}, u32[]{:S(2)}, u32[]{:S(2)}) collective-permute-start(bf16[2,3,128,256]{3,2,1,0:T(8,128)(2,1)} %get-tuple-element.156), channel_id=1, source_target_pairs={{8,0},{12,4},{16,8},{20,12},{24,16},{28,20},{32,24},{36,28},{40,32... | collective-permute-start | bytes 1179656 | tf_op jit(solution)/shard_map/ppermute | solution.py:167
  1395.9 288.4 %collective-permute-start.31 = (bf16[2,3,128,256]{3,2,1,0:T(8,128)(2,1)}, bf16[2,3,128,256]{3,2,1,0:T(8,128)(2,1)}, u32[]{:S(2)}, u32[]{:S(2)}) collective-permute-start(bf16[2,3,128,256]{3,2,1,0:T(8,128)(2,1)} %get-tuple-element.157), channel_id=1, source_target_pairs={{12,0},{16,4},{20,8},{24,12},{28,16},{32,20},{36,24},{40,28},{44,3... | collective-permute-start | bytes 1179656 | tf_op jit(solution)/shard_map/ppermute | solution.py:167
  1644.4 21.6 collective-permute-start.44
  1650.7 25.5 %collective-permute-start.42 = (bf16[128,4096]{1,0:T(8,128)(2,1)}, bf16[128,4096]{1,0:T(8,128)(2,1)S(1)}, u32[]{:S(2)}, u32[]{:S(2)}) collective-permute-start(bf16[128,4096]{1,0:T(8,128)(2,1)} %get-tuple-element.63), channel_id=1, source_target_pairs={{0,1},{1,2},{2,3},{3,0},{4,5},{5,6},{6,7},{7,4},{8,9},{9,10},{10,1... | collective-permute-start | bytes 3145736 | tf_op jit(solution)/shard_map/ppermute | solution.py:159
  1666.0 42.7 %collective-permute-start.49 = (bf16[256,4096]{1,0:T(8,128)(2,1)S(1)}, bf16[256,4096]{1,0:T(8,128)(2,1)S(1)}, u32[]{:S(2)}, u32[]{:S(2)}) collective-permute-start(bf16[256,4096]{1,0:T(8,128)(2,1)S(1)} %copy-done.94), channel_id=1, source_target_pairs={{64,67},{65,64},{66,65},{67,66},{68,71},{69,68},{70,69},{71,70},{7... | collective-permute-start | bytes 6291464 | tf_op jit(solution)/shard_map/ppermute | solution.py:159
  1676.2 34.1 %collective-permute-start.47 = (bf16[256,4096]{1,0:T(8,128)(2,1)S(1)}, bf16[256,4096]{1,0:T(8,128)(2,1)S(1)}, u32[]{:S(2)}, u32[]{:S(2)}) collective-permute-start(bf16[256,4096]{1,0:T(8,128)(2,1)S(1)} %add_dynamic-update-slice_fusion.1), channel_id=1, source_target_pairs={{64,65},{65,66},{66,67},{67,64},{68,69},{69,70},{70,71},{71,68},{7... | collective-permute-start | bytes 6291464 | tf_op jit(solution)/shard_map/ppermute | solution.py:159
  1677.5 34.1 %collective-permute-start.45 = (bf16[256,4096]{1,0:T(8,128)(2,1)S(1)}, bf16[256,4096]{1,0:T(8,128)(2,1)S(1)}, u32[]{:S(2)}, u32[]{:S(2)}) collective-permute-start(bf16[256,4096]{1,0:T(8,128)(2,1)S(1)} %add_dynamic-update-slice_fusion.2), channel_id=1, source_target_pairs={{0,3},{1,0},{2,1},{3,2},{4,7},{5,4},{6,5},{7,6},{8,11},{9,8},{10,9... | collective-permute-start | bytes 6291464 | tf_op jit(solution)/shard_map/ppermute | solution.py:159
  1679.6 39.5 %collective-permute-start.43 = (bf16[256,4096]{1,0:T(8,128)(2,1)S(1)}, bf16[256,4096]{1,0:T(8,128)(2,1)S(1)}, u32[]{:S(2)}, u32[]{:S(2)}) collective-permute-start(bf16[256,4096]{1,0:T(8,128)(2,1)S(1)} %add_dynamic-update-slice_fusion.3), channel_id=1, source_target_pairs={{0,1},{1,2},{2,3},{3,0},{4,5},{5,6},{6,7},{7,4},{8,9},{9,10},{10,1... | collective-permute-start | bytes 6291464 | tf_op jit(solution)/shard_map/ppermute | solution.py:159
  1684.3 19.0 collective-permute-start.30
  1703.3 138.2 %collective-permute-start.40 = (bf16[128,1920]{1,0:T(8,128)(2,1)}, bf16[128,1920]{1,0:T(8,128)(2,1)}, u32[]{:S(2)}, u32[]{:S(2)}) collective-permute-start(bf16[128,1920]{1,0:T(8,128)(2,1)} %get-tuple-element.60), channel_id=1, source_target_pairs={{64,67},{65,64},{66,65},{67,66},{68,71},{69,68},{70,69},{71,70},{7... | collective-permute-start | bytes 1474568 | tf_op jit(solution)/shard_map/ppermute | solution.py:159
  1708.7 139.6 %collective-permute-start.38 = (bf16[128,1920]{1,0:T(8,128)(2,1)}, bf16[128,1920]{1,0:T(8,128)(2,1)}, u32[]{:S(2)}, u32[]{:S(2)}) collective-permute-start(bf16[128,1920]{1,0:T(8,128)(2,1)} %get-tuple-element.58), channel_id=1, source_target_pairs={{64,65},{65,66},{66,67},{67,64},{68,69},{69,70},{70,71},{71,68},{7... | collective-permute-start | bytes 1474568 | tf_op jit(solution)/shard_map/ppermute | solution.py:159
  1722.8 139.1 %all-to-all-start.1 = ((bf16[16,16,4096]{2,1,0:T(8,128)(2,1)}), bf16[16,16,4096]{2,1,0:T(8,128)(2,1)S(1)}, u32[]{:S(2)}, u32[]{:S(2)}) async-start(bf16[16,16,4096]{2,1,0:T(8,128)(2,1)} %bitcast.307), calls=%async_computation.1 | async-start | bytes 4194304 | tf_op jit(solution)/shard_map/all_to_all | solution.py:430
  1734.3 530.8 %all-gather.4.cloned.1.call-start = ((), (), s32[]{:S(2)}) async-start(), calls=%async_computation.2 | async-start | bytes 2228224 | tf_op jit(solution)/shard_map/all_gather | solution.py:432
  1838.7 13.3 collective-permute-start.36
  1843.6 23.5 %collective-permute-start.41 = (bf16[256,1920]{1,0:T(8,128)(2,1)}, bf16[256,1920]{1,0:T(8,128)(2,1)}, u32[]{:S(2)}, u32[]{:S(2)}) collective-permute-start(bf16[256,1920]{1,0:T(8,128)(2,1)} %add_dynamic-update-slice_fusion.4), channel_id=1, source_target_pairs={{64,67},{65,64},{66,65},{67,66},{68,71},{69,68},{70,69},{71,70},{7... | collective-permute-start | bytes 2949128 | tf_op jit(solution)/shard_map/ppermute | solution.py:159
  1845.3 12.8 collective-permute-start.34
  1850.4 16.7 collective-permute-start.39
  1853.9 16.5 collective-permute-start.37
  1860.0 17.6 collective-permute-start.35
  1881.4 355.2 %copy-start.6 = (f32[384,640]{1,0:T(8,128)S(1)}, f32[384,640]{1,0:T(8,128)}, u32[]{:S(2)}) copy-start(f32[384,640]{1,0:T(8,128)} %copy-done.4) | copy-start | bytes 2949124
  1881.4 355.2 %copy-start.12 = (f32[384,640]{1,0:T(8,128)S(1)}, f32[384,640]{1,0:T(8,128)}, u32[]{:S(2)}) copy-start(f32[384,640]{1,0:T(8,128)} %copy-done.11) | copy-start | bytes 2949124
  1881.4 358.2 %all-to-all-start = ((bf16[16,16,1920]{2,1,0:T(8,128)(2,1)}), bf16[16,16,1920]{2,1,0:T(8,128)(2,1)}, u32[]{:S(2)}, u32[]{:S(2)}) async-start(bf16[16,16,1920]{2,1,0:T(8,128)(2,1)} %bitcast.310), calls=%async_computation | async-start | bytes 1966080 | tf_op jit(solution)/shard_map/all_to_all | solution.py:430
  (158 other events, 2848.7 us)
Sparse Core Ops, SparseCore 0:
  1863.0 48.2 all-gather.3

commit v2 on v1

--- a/solution.py
+++ b/solution.py
@@ -32,18 +32,29 @@
     (0, 0, 160, 0, 1024, 0, 0),
     (1, 0, 160, 0, 256, 0, 1024),
     (2, 0, 160, 0, 256, 0, 1280),
-) + tuple((3, 96 * i, min(96, 256 - 96 * i), 0, 640, 160, 640 * i) for i in range(3))
+) + tuple((3, 96 * i, min(96, 256 - 96 * i), 0, 640, 160, 640 * i) for i in range(3)) + (
+    (4, 0, 32, 0, 640, 224, 1280),
+)
 
 FFN_GRAD_PLAN = ((0, 0, 160, 0, 4096, 0, 0),) + tuple(
     (1, 96 * i, min(96, 512 - 96 * i), 0, 640, 160, 640 * i) for i in range(6)
 )
-ATTN_GRAD_PLAN = ((0, 0, 160, 0, 1536, 0, 0),) + tuple(
-    (1, 96 * i, min(96, 256 - 96 * i), 0, 640, 160, 640 * i) for i in range(3)
+ATTN_GRAD_PLAN = (
+    ((0, 0, 160, 0, 1536, 0, 0),)
+    + tuple((1, 96 * i, min(96, 256 - 96 * i), 0, 640, 160, 640 * i) for i in range(3))
+    + ((2, 0, 32, 0, 640, 224, 1280),)
 )
 
 
 def in_any(count):
     return [pl.BlockSpec(memory_space=pl.ANY)] * count
+
+
+def in_vmem(count):
+    return [pl.BlockSpec(memory_space=pltpu.VMEM)] * count
+
+
+LIMIT = 24 * 1024 * 1024
 
 
 def run_copies(copies):
@@ -53,9 +64,9 @@
         item.wait()
 
 
-def pack_shard(arrays, plan, cols):
+def pack_shard(arrays, plan, cols, after=()):
     def body(*refs):
-        sources, out, sems = refs[: len(arrays)], refs[len(arrays)], refs[len(arrays) + 1]
+        sources, out, sems = refs[: len(arrays)], refs[-2], refs[-1]
         run_copies(
             [
                 pltpu.make_async_copy(
@@ -69,12 +80,24 @@
 
     return pl.pallas_call(
         body,
-        in_specs=in_any(len(arrays)),
-        out_specs=pl.BlockSpec(memory_space=pl.ANY),
+        in_specs=in_any(len(arrays) + len(after)),
+        out_specs=pl.BlockSpec(memory_space=pltpu.VMEM),
         out_shape=jax.ShapeDtypeStruct((ROWS, cols), jnp.bfloat16),
+        compiler_params=pltpu.CompilerParams(vmem_limit_bytes=LIMIT),
         scratch_shapes=[pltpu.SemaphoreType.DMA((len(plan),))],
         name="pack_shard",
-    )(*arrays)
+    )(*arrays, *after)
+
+
+def ordered(value, *after):
+    return pl.pallas_call(
+        lambda *refs: None,
+        in_specs=in_any(1 + len(after)),
+        out_specs=pl.BlockSpec(memory_space=pl.ANY),
+        out_shape=jax.ShapeDtypeStruct(value.shape, value.dtype),
+        input_output_aliases={0: 0},
+        name="ordered",
+    )(value, *after)
 
 
 def unpack_full(place, pieces, plan, shapes):
@@ -108,7 +131,8 @@
     return pl.pallas_call(
         body,
         in_specs=[pl.BlockSpec(memory_space=pltpu.SMEM)] + in_any(len(arrays)),
-        out_specs=in_any(len(shapes)),
+        out_specs=in_vmem(len(shapes)),
+        compiler_params=pltpu.CompilerParams(vmem_limit_bytes=LIMIT),
         out_shape=[jax.ShapeDtypeStruct(shape, jnp.bfloat16) for shape in shapes],
         scratch_shapes=[pltpu.SemaphoreType.DMA((len(jobs),))],
         name="unpack_full",
@@ -147,7 +171,8 @@
     return pl.pallas_call(
         body,
         in_specs=[pl.BlockSpec(memory_space=pltpu.SMEM)] + in_any(len(arrays)),
-        out_specs=in_any(len(targets)),
+        out_specs=in_vmem(len(targets)),
+        compiler_params=pltpu.CompilerParams(vmem_limit_bytes=LIMIT),
         out_shape=[jax.ShapeDtypeStruct((t[2], cols), jnp.bfloat16) for t in targets],
         scratch_shapes=[pltpu.SemaphoreType.DMA((len(jobs),))],
         name="pack_blocks",
@@ -180,19 +205,20 @@
         (first, 2, 0, half),
         (second, 2, half, half),
     )
-    return unpack_full(place, pieces, plan, shapes)
-
-
-def reduce_z(place, section, arrays, plan, cols):
+    return unpack_full(place, pieces, plan, shapes), (above, below)
+
+
+def reduce_z_begin(place, section, arrays, plan, cols):
     own, after, before, far_a, far_b = pack_blocks(place, arrays, plan, cols)
+    return own, after, before, along_z(far_a, section, 1), along_z(far_b, section, -1)
+
+
+def reduce_z_end(begun, section):
+    own, after, before, got_a, got_b = begun
     half = ROWS // 2
-    got_a = along_z(far_a, section, 1)
-    got_b = along_z(far_b, section, -1)
     after = lax.dynamic_update_slice(after, after[:half] + got_a, (0, 0))
     before = lax.dynamic_update_slice(before, before[half:] + got_b, (half, 0))
-    left = along_z(after, section, 1)
-    right = along_z(before, section, -1)
-    return own, left, right
+    return own, along_z(after, section, 1), along_z(before, section, -1)
 
 
 def total_of(parts):
@@ -285,7 +311,9 @@
     return dv, grad * unit
 
 
-def backward_layer(grad_out, stored, tables, attn_w, ffn_w, gains, section, place, merge):
+def backward_layer(
+    grad_out, stored, tables, attn_w, ffn_w, gains, section, place, other_ffn=None, other_attn=None
+):
     (
         inputs, normed, query_raw, key_raw, query_rot, keys_all, values_all, prob, mixed, branch,
         middle, inner, gate_act, up_act, hidden, down,
@@ -303,6 +331,10 @@
     )
     d_gate, d_up = pull(d_hidden)
     d_gate_up = jnp.concatenate([d_gate.astype(jnp.bfloat16), d_up.astype(jnp.bfloat16)], axis=1)
+    grad_ffn = (inner_rows(inner, d_gate_up), inner_rows(hidden, d_down))
+    ffn_begun = reduce_z_begin(place, section, grad_ffn, FFN_GRAD_PLAN, FFN_COLS)
+    if other_ffn is not None:
+        d_gate_up = ordered(d_gate_up, *other_ffn[1:])
     d_inner = against(d_gate_up, gate_up_w)
     d_middle_ffn, by_ffn = norm_back(d_inner, middle, ffn_g)
     d_ffn_g = jnp.sum(by_ffn, axis=0)
@@ -310,12 +342,16 @@
     d_branch, by_mix = norm_back(d_middle, branch, mix_g)
     d_mix_g = jnp.sum(by_mix, axis=0)
     d_branch = d_branch.astype(jnp.bfloat16)
+    if other_attn is not None:
+        d_branch = ordered(d_branch, *other_attn[1:])
     d_mixed = against(d_branch, output_w).astype(jnp.bfloat16).reshape(MICRO, SHARD, QH, HD)
     d_mixed = jnp.swapaxes(d_mixed, 1, 2)
     d_prob = batched("mhqd,mkd->mhqk", d_mixed, values_all)
     d_score = (prob * (d_prob - jnp.sum(prob * d_prob, axis=-1, keepdims=True))).astype(
         jnp.bfloat16
     )
+    d_score = ordered(d_score, ffn_begun[3], ffn_begun[4])
+    ffn_parts = reduce_z_end(ffn_begun, section)
     scale = HD ** (-0.5)
     d_keys = batched("mhqk,mhqd->mkd", d_score, query_rot) * scale
     d_values_all = batched("mhqk,mhqd->mkd", prob.astype(jnp.bfloat16), d_mixed)
@@ -325,8 +361,6 @@
         piece = d_stacked[:, :, offset * SHARD : (offset + 1) * SHARD].astype(jnp.bfloat16)
         back = back + along_seq(piece, section, offset - HOPS).astype(jnp.float32)
     back = back.reshape(2, TOKENS, HD)
-    grad_ffn = (inner_rows(inner, d_gate_up), inner_rows(hidden, d_down))
-    ffn_parts = None if merge else reduce_z(place, section, grad_ffn, FFN_GRAD_PLAN, FFN_COLS)
     d_query_rot = batched("mhqk,mkd->mhqd", d_score, keys_all) * scale
     d_query, by_query = norm_back(
         turn(
@@ -347,12 +381,25 @@
     d_inputs_pre, by_pre = norm_back(d_normed, inputs, pre_g)
     d_pre_g = jnp.sum(by_pre, axis=0)
     d_inputs = d_middle + d_inputs_pre
-    grad_attn = (inner_rows(normed, d_qkv), inner_rows(mixed, d_branch))
-    gain_grads = jnp.concatenate([d_pre_g, d_query_g, d_key_g, d_mix_g, d_ffn_g, d_out_g])
-    return d_inputs, grad_ffn, ffn_parts, grad_attn, gain_grads
+    wide = jnp.stack([d_pre_g, d_mix_g, d_ffn_g, d_out_g]).reshape(4, RING, D // RING)
+    narrow = jnp.stack([d_query_g, d_key_g]).reshape(2, RING, HD // RING)
+    rows = jnp.concatenate(
+        [
+            jnp.pad(jnp.swapaxes(wide, 0, 1), ((0, 0), (0, 0), (0, D - D // RING))),
+            jnp.pad(jnp.swapaxes(narrow, 0, 1), ((0, 0), (0, 26), (0, D - HD // RING))),
+        ],
+        axis=1,
+    ).astype(jnp.bfloat16)
+    grad_attn = (
+        inner_rows(normed, d_qkv),
+        inner_rows(mixed, d_branch),
+        rows.reshape(RING * 32, D),
+    )
+    return d_inputs, ffn_parts, grad_attn
 
 
 GAIN_SIZES = (D, HD, HD, D, D, D)
+GAIN_ROWS = (0, 4, 5, 1, 2, 3)
 
 
 def per_device(
@@ -365,30 +412,34 @@
     seq_index = lax.axis_index("y") * RING + lax.axis_index("x")
     place = jnp.reshape(z_index, (1,)).astype(jnp.int32)
 
-    attn_shard = pack_shard(
-        (query_weight[0], key_weight[0], value_weight[0], output_weight[0]), ATTN_PLAN, ATTN_COLS
-    )
-    ffn_shard = pack_shard((gate_weight[0], up_weight[0], down_weight[0]), FFN_PLAN, FFN_COLS)
-    full_attn_plan = ATTN_GRAD_PLAN
-    full_ffn_plan = FFN_GRAD_PLAN
-    attn_shapes = ((D, QH * HD + 2 * HD), (QH * HD, D))
+    wide = jnp.concatenate([pre_gain, mix_gain, ffn_gain, out_gain])
+    narrow = jnp.concatenate([query_gain, key_gain])
+    gain_shard = jnp.concatenate(
+        [
+            jnp.pad(wide, ((0, 0), (0, D - D // RING))),
+            jnp.pad(narrow, ((0, 26), (0, D - HD // RING))),
+        ]
+    )
+    attn_arrays = (query_weight[0], key_weight[0], value_weight[0], output_weight[0], gain_shard)
+    ffn_arrays = (gate_weight[0], up_weight[0], down_weight[0])
+    attn_shapes = ((D, QH * HD + 2 * HD), (QH * HD, D), (RING * 32, D))
     ffn_shapes = ((D, 2 * FF), (FF, D))
     weights = []
+    gains = []
+    seen = ()
     for section in range(2):
-        attn = gather_weights(attn_shard, section, place, full_attn_plan, attn_shapes)
-        ffn = gather_weights(ffn_shard, section, place, full_ffn_plan, ffn_shapes)
-        weights.append((attn, ffn))
-
-    packed_gains = jnp.concatenate(
-        [item[0] for item in (pre_gain, query_gain, key_gain, mix_gain, ffn_gain, out_gain)]
-    )
-    all_gains = lax.all_gather(packed_gains, "z").astype(jnp.float32)
-    gains = []
-    start = 0
-    for size in GAIN_SIZES:
-        part = size // RING
-        gains.append(all_gains[:, start : start + part].reshape(size))
-        start += part
+        shard = pack_shard(attn_arrays, ATTN_PLAN, ATTN_COLS, seen)
+        attn, seen = gather_weights(shard, section, place, ATTN_GRAD_PLAN, attn_shapes)
+        shard = pack_shard(ffn_arrays, FFN_PLAN, FFN_COLS, seen)
+        ffn, seen = gather_weights(shard, section, place, FFN_GRAD_PLAN, ffn_shapes)
+        weights.append((attn[:2], ffn))
+        corner = attn[2].reshape(RING, 32, D).astype(jnp.float32)
+        gains.append(
+            [
+                corner[:, row, : size // RING].reshape(size)
+                for row, size in zip(GAIN_ROWS, GAIN_SIZES)
+            ]
+        )
 
     exponent = jnp.arange(HD // 2).astype(jnp.float32) * (2.0 / HD)
     freqs = ROPE_BASE ** (-exponent)
@@ -407,21 +458,25 @@
     allowed = allowed[None] & (query_seg[:, :, None] == key_seg[:, None, :])
 
     first_in = hidden_in[:, 0].reshape(TOKENS, D).astype(jnp.float32)
-    first_out, first_kept = forward_layer(first_in, tables, allowed, *weights[0], gains, 0)
+    first_out, first_kept = forward_layer(first_in, tables, allowed, *weights[0], gains[0], 0)
     handed = lax.ppermute(first_out, "section", [(0, 1)]).astype(jnp.float32)
-    second_out, second_kept = forward_layer(handed, tables, allowed, *weights[1], gains, 1)
+    second_out, second_kept = forward_layer(handed, tables, allowed, *weights[1], gains[1], 1)
 
     cot = cotangent[:, 0].reshape(TOKENS, D).astype(jnp.float32)
-    d_second, ffn_grad1, _, attn_grad1, gain_grad1 = backward_layer(
-        cot, second_kept, tables, *weights[1], gains, 1, place, True
+    d_second, ffn_parts1, attn_grad1 = backward_layer(
+        cot, second_kept, tables, *weights[1], gains[1], 1, place
     )
     d_first_out = lax.ppermute(d_second.astype(jnp.bfloat16), "section", [(1, 0)])
-    ffn_parts1 = reduce_z(place, 1, ffn_grad1, FFN_GRAD_PLAN, FFN_COLS)
-    attn_parts1 = reduce_z(place, 1, attn_grad1, ATTN_GRAD_PLAN, ATTN_COLS)
-    d_first, _, ffn_parts0, attn_grad0, gain_grad0 = backward_layer(
-        d_first_out.astype(jnp.float32), first_kept, tables, *weights[0], gains, 0, place, False
-    )
-    attn_parts0 = reduce_z(place, 0, attn_grad0, ATTN_GRAD_PLAN, ATTN_COLS)
+    attn_parts1 = reduce_z_end(
+        reduce_z_begin(place, 1, attn_grad1, ATTN_GRAD_PLAN, ATTN_COLS), 1
+    )
+    d_first, ffn_parts0, attn_grad0 = backward_layer(
+        d_first_out.astype(jnp.float32), first_kept, tables, *weights[0], gains[0], 0, place,
+        ffn_parts1, attn_parts1,
+    )
+    attn_parts0 = reduce_z_end(
+        reduce_z_begin(place, 0, attn_grad0, ATTN_GRAD_PLAN, ATTN_COLS), 0
+    )
 
     def finish(parts0, parts1, cols):
         mine = jnp.where(leading, total_of(parts0), total_of(parts1)).astype(jnp.bfloat16)
@@ -433,19 +488,16 @@
 
     ffn_done = finish(ffn_parts0, ffn_parts1, FFN_COLS)
     attn_done = finish(attn_parts0, attn_parts1, ATTN_COLS)
-    gain_total = lax.psum(jnp.where(leading, gain_grad0, gain_grad1), ("y", "x", "z"))
 
     def restore(packed, plan, which):
         return jnp.concatenate(
             [packed[pr : pr + n, pc : pc + w] for a, r, n, c, w, pr, pc in plan if a == which]
         ).astype(jnp.float32)[None]
 
-    gain_outs = []
-    start = 0
-    for size in GAIN_SIZES:
-        part = size // RING
-        gain_outs.append(lax.dynamic_slice(gain_total, (start + z_index * part,), (part,))[None])
-        start += size
+    corner = attn_done[224:256, 1280:1920].astype(jnp.float32)
+    gain_outs = [
+        corner[row : row + 1, : size // RING] for row, size in zip(GAIN_ROWS, GAIN_SIZES)
+    ]
     outputs = jnp.where(leading, first_out, second_out).reshape(1, MICRO, 1, SHARD, D)
     input_grads = jnp.where(leading, d_first, d_second).reshape(1, MICRO, 1, SHARD, D)
     return (

time: 2290 us -> 629 us (0.27)
  Pallas kernels: 1450 us -> 20.9 us
  blocking collectives: 398 us -> 22.7 us
  waiting for transfers between devices: 52.6 us -> 119 us
  other arithmetic: 65.4 us -> 106 us
  local copies, waits for them, and re-layouts: 66 us -> 100 us
    pallas_call x4, Pallas kernels: 680 us -> 8.63 us  [pack_blocks(): pl.pallas_call(body, in_specs=[pl.BlockSpec(memory_space=pltpu.SMEM)] + i...]
    pallas_call x4, Pallas kernels: 680 us -> 9.14 us  [unpack_full(): pl.pallas_call(body, in_specs=[pl.BlockSpec(memory_space=pltpu.SMEM)] + i...]
    psum x1 -> x0, blocking collectives: 346 us -> none  [per_device(): lax.psum(jnp.where(leading, gain_grad0, gain_grad1), ('y', 'x', 'z'))]
    pallas_call x2 -> x8, Pallas kernels: 86.7 us -> 3.17 us  [the longest x4 3.17 us: pack_shard(): pl.pallas_call(body, in_specs=in_any(len(arrays) + len(after)), out_specs...]
    all_gather x1 -> x0, blocking collectives: 30.2 us -> none  [per_device(): all_gains = lax.all_gather(packed_gains, 'z').astype(jnp.float32)]
    unnamed x370 -> x396, local copies, waits for them, and re-layouts: 34.4 us -> 59.1 us
    ppermute x32, waiting for transfers between devices: 39 us -> 62.4 us  [along_z(): return lax.ppermute(x, ('section', 'z'), pairs)]
  transfers between devices with their start and end apart: 53 -> 53, of which waited for: 7 -> 16; matrix products, arithmetic and copies ran while one was open for 6% -> 30% of each run, Pallas kernels for 62% -> 2%
where the time goes in v2:
time: 629 us; the launch traced here: 620 us
  starting transfers between devices  139 us (22%)
  waiting for transfers between devices  119 us (19%)
  other arithmetic  106 us (17%)
  local copies, waits for them, and re-layouts  100 us (16%)
  matrix products  94.5 us (15%)
  blocking collectives  22.7 us (4%)
  Pallas kernels  20.9 us (3%)
  between operations  17.3 us (3%)
    ppermute x32, starting transfers between devices, along_z(): return lax.ppermute(x, ('section', 'z'), pairs)  73.7 us
    ppermute x32, waiting for transfers between devices, along_z(): return lax.ppermute(x, ('section', 'z'), pairs)  62.4 us
    unnamed x396, local copies, waits for them, and re-layouts  59.1 us
    ppermute x16, starting transfers between devices, along_seq(): return lax.ppermute(x, ('section', 'y', 'x'), pairs)  33 us
    dot_general x8, matrix products, against(): lax.dot_general(left, right, (((1,), (1,)), ((), ())), preferred_element_...  31 us
    all_to_all x2, starting transfers between devices, finish(): lax.all_to_all(split, ('y', 'x'), split_axis=0, concat_axis=0, tiled=True)  28.9 us
    dot_general x12, matrix products, batched(): return jnp.einsum(spec, left, right, preferred_element_type=jnp.float32)  23.6 us
    ppermute x1, waiting for transfers between devices, per_device(): lax.ppermute(d_second.astype(jnp.bfloat16), 'section', [(1, 0)])  22.9 us
  transfers between devices with their start and end apart: 53, of which 16 were waited for; matrix products, arithmetic and copies ran while one was open for 30% of the time, Pallas kernels for 2%

profile of v2, /device:TPU:0, one launch (start us, length us, event | category | flops | bytes accessed | tf_op | source)
XLA Modules:
  0.0 619.6 jit_solution(4677674191975320373)
XLA Ops:
  12.7 3.9 collective-permute-start.1
  16.6 4.0 collective-permute-start
  21.6 9.2 %collective-permute-done.1.refs_2_.refs_4_ = bf16[256,1920]{1,0:T(8,128)(2,1)S(1)} collective-permute-done((bf16[256,1920]{1,0:T(8,128)(2,1)S(1)}, bf16[256,1920]{1,0:T(8,128)(2,1)S(1)}, u32[]{:S(2)}, u32[]{:S(2)}) %collective-permute-start.1) | collective-permute-done | bytes 983072 | tf_op jit(solution)/shard_map/ppermute | solution.py:184
  34.3 3.8 collective-permute-start.9
  38.1 3.3 collective-permute-start.8
  48.7 4.5 collective-permute-start.3
  55.9 28.2 %collective-permute-done.2.refs_3_ = bf16[128,1920]{1,0:T(8,128)(2,1)} collective-permute-done((bf16[128,1920]{1,0:T(8,128)(2,1)}, bf16[128,1920]{1,0:T(8,128)(2,1)}, u32[]{:S(2)}, u32[]{:S(2)}) %collective-permute-start.2) | collective-permute-done | bytes 491552 | tf_op jit(solution)/shard_map/ppermute | solution.py:184
  105.3 3.9 collective-permute-start.10
  111.6 3.2 collective-permute-start.11
  125.7 2.9 collective-permute-done.11.refs_4_
  128.6 2.9 unpack_full.5
  146.4 4.2 collective-permute-start.7
  150.5 4.7 collective-permute-start.6
  155.2 4.4 collective-permute-start.5
  159.6 3.6 collective-permute-start.4
  164.5 5.7 collective-permute-done.4
  183.7 2.7 fusion.202
  214.3 3.1 fusion.43
  217.4 2.8 reshape.631
  239.1 2.6 unpack_full.7
  241.7 2.7 fusion.203
  248.2 3.7 fusion.21
  251.9 2.8 multiply_reduce_fusion.8
  261.1 4.9 convolution_convert_fusion.1.refs_0_
  268.0 4.7 convolution_bitcast_fusion.1
  272.7 2.8 fusion.89
  280.0 3.2 pack_blocks.4
  286.1 9.8 %multiply_convert_fusion.1.refs_0_ = bf16[3,4,128,640]{3,2,1,0:T(8,128)(2,1)} fusion(f32[3,4,128,640]{3,2,1,0:T(8,128)S(1)} %copy-done.81, f32[3,4,128,640]{3,2,1,0:T(8,128)S(1)} %copy-done.181, f32[3,4,128]{2,1,0:T(4,128)S(1)} %copy-done.185), kind=kOutput, calls=%fused_computation.22 | output fusion | flops 5900415 | bytes 9836544 | tf_op jit(solution)/shard_map/sub | solution.py:350
  297.9 2.7 convolution_multiply_fusion.1
  301.9 2.6 add_dynamic-update-slice_fusion.2
  315.9 2.5 add_dynamic-update-slice_fusion.3
  330.3 3.4 fusion.64
  342.8 22.9 %collective-permute-done.31 = bf16[384,640]{1,0:T(8,128)(2,1)S(1)} collective-permute-done((bf16[384,640]{1,0:T(8,128)(2,1)S(1)}, bf16[384,640]{1,0:T(8,128)(2,1)S(1)}, u32[]{:S(2)}, u32[]{:S(2)}) %collective-permute-start.31) | collective-permute-done | bytes 491552 | tf_op jit(solution)/shard_map/ppermute | solution.py:469
  366.7 5.8 fusion.14
  374.3 3.4 convolution_convert_fusion.refs_0_
  377.7 3.1 pack_blocks.6
  382.1 4.3 collective-permute-start.39
  393.1 6.1 collective-permute-done.39.refs_2_
  400.7 2.8 add_dynamic-update-slice_fusion
  403.5 3.0 collective-permute-done.38.refs_1_
  406.5 2.5 collective-permute-start.49
  409.0 2.8 add_dynamic-update-slice_fusion.1
  411.9 6.5 %multiply_reduce_fusion.6 = (bf16[640]{0:T(1024)(128)(2,1)S(1)}, f32[384]{0:T(512)S(1)}, f32[384,640]{1,0:T(8,128)S(1)}) fusion(f32[384,640]{1,0:T(8,128)} %copy-done.47, f32[384]{0:T(512)S(1)} %add_rsqrt_fusion.8, f32[640]{0:T(1024)S(1)} %mul.1031, bf16[384,4096]{1,0:T(8,128)(2,1)} %ordered.5, bf16[640,4096]{1,0:T(8,128)(2,1)} %copy-done.1), kind=kOutput, calls=%fused_computation.162 | convolution fusion | flops 2014739456 | bytes 10361600 | tf_op jit(solution)/shard_map/dot_general | solution.py:244
  420.3 3.2 convolution_convert_fusion.8
  425.6 4.7 convolution_bitcast_fusion
  432.4 9.6 %multiply_convert_fusion.refs_0_ = bf16[3,4,128,640]{3,2,1,0:T(8,128)(2,1)} fusion(f32[3,4,128,640]{3,2,1,0:T(8,128)S(1)} %fusion.87, f32[3,4,128,640]{3,2,1,0:T(8,128)S(1)} %copy-done.179, f32[3,4,128]{2,1,0:T(4,128)S(1)} %copy-done.183), kind=kOutput, calls=%fused_computation.19 | output fusion | flops 5900415 | bytes 9836544 | tf_op jit(solution)/shard_map/sub | solution.py:350
  442.1 2.7 convolution_multiply_fusion
  460.2 4.3 collective-permute-done.40
  464.5 3.5 collective-permute-start.48
  468.1 4.8 collective-permute-done.41
  478.2 4.1 fusion.78
  482.4 2.7 convolution_convert_fusion.4.refs_0_
  488.9 5.1 collective-permute-done.48
  494.0 7.1 %select_convert_fusion = bf16[256,4096]{1,0:T(8,128)(2,1)} fusion(bf16[256,4096]{1,0:T(8,128)(2,1)} %collective-permute-done.33.refs_2_, bf16[256,4096]{1,0:T(8,128)(2,1)} %collective-permute-done.32.refs_1_, bf16[256,4096]{1,0:T(8,128)(2,1)S(1)} %copy-done.13, bf16[256,4096]{1,0:T(8,128)(2,1)} %collective-permute-done.49, ...), kind=kLoop, calls=%fused_computation.16 | loop fusion | flops 12582912 | bytes 14680065 | tf_op jit(solution)/shard_map/convert_element_type | solution.py:482
  501.1 21.4 %all-to-all-start.1 = ((bf16[16,16,4096]{2,1,0:T(8,128)(2,1)}), bf16[16,16,4096]{2,1,0:T(8,128)(2,1)}, u32[]{:S(2)}, u32[]{:S(2)}) async-start(bf16[16,16,4096]{2,1,0:T(8,128)(2,1)} %bitcast.321), calls=%async_computation.1 | async-start | bytes 4194304 | tf_op jit(solution)/shard_map/all_to_all | solution.py:485
  526.8 5.1 collective-permute-start.47
  531.9 2.7 collective-permute-done.44
  536.7 11.9 %all-to-all-done.1 = bf16[16,16,4096]{2,1,0:T(8,128)(2,1)} async-done(((bf16[16,16,4096]{2,1,0:T(8,128)(2,1)}), bf16[16,16,4096]{2,1,0:T(8,128)(2,1)}, u32[]{:S(2)}, u32[]{:S(2)}) %all-to-all-start.1) | async-done | bytes 2097184 | tf_op jit(solution)/shard_map/all_to_all | solution.py:485
  548.5 2.6 reduce_sum.473
  552.1 3.8 select_convert_fusion.1
  555.9 7.5 %all-to-all-start = ((bf16[16,16,1920]{2,1,0:T(8,128)(2,1)}), bf16[16,16,1920]{2,1,0:T(8,128)(2,1)}, u32[]{:S(2)}, u32[]{:S(2)}) async-start(bf16[16,16,1920]{2,1,0:T(8,128)(2,1)} %bitcast.322), calls=%async_computation | async-start | bytes 1966080 | tf_op jit(solution)/shard_map/all_to_all | solution.py:485
  565.9 2.8 fusion.77
  568.8 7.6 %all-to-all-done = bf16[16,16,1920]{2,1,0:T(8,128)(2,1)} async-done(((bf16[16,16,1920]{2,1,0:T(8,128)(2,1)}), bf16[16,16,1920]{2,1,0:T(8,128)(2,1)}, u32[]{:S(2)}, u32[]{:S(2)}) %all-to-all-start) | async-done | bytes 983072 | tf_op jit(solution)/shard_map/all_to_all | solution.py:485
  577.7 22.7 %all_gather.6 = bf16[256,1920]{1,0:T(8,128)(2,1)S(1)} all-gather(bf16[16,1920]{1,0:T(8,128)(2,1)S(1)} %reduce_sum.472), channel_id=1, replica_groups=mesh['section'=2,'y'=4,'x'=4,'z'=4] {'y','x'}, dimensions={0}, use_global_device_ids=true | all-gather | bytes 1044480 | tf_op jit(solution)/shard_map/all_gather | solution.py:487
  (671 shorter events, 249.9 us)
Async XLA Ops:
  7.2 25.4 %copy-start.10 = (bf16[1,512,640]{2,1,0:T(8,128)(2,1)S(1)}, bf16[1,512,640]{2,1,0:T(8,128)(2,1)}, u32[]{:S(2)}) copy-start(bf16[1,512,640]{2,1,0:T(8,128)(2,1)} %param.27) | copy-start | bytes 1966084
  12.7 18.1 %collective-permute-start.1 = (bf16[256,1920]{1,0:T(8,128)(2,1)S(1)}, bf16[256,1920]{1,0:T(8,128)(2,1)S(1)}, u32[]{:S(2)}, u32[]{:S(2)}) collective-permute-start(bf16[256,1920]{1,0:T(8,128)(2,1)S(1)} %pack_shard.4.refs_0_), channel_id=1, source_target_pairs={{0,1},{1,2},{2,3},{3,0},{4,5},{5,6},{6,7},{7,4},{8,9},{9,10},{10,1... | collective-permute-start | bytes 2949128 | tf_op jit(solution)/shard_map/ppermute | solution.py:184
  16.6 16.0 %collective-permute-start = (bf16[256,1920]{1,0:T(8,128)(2,1)S(1)}, bf16[256,1920]{1,0:T(8,128)(2,1)S(1)}, u32[]{:S(2)}, u32[]{:S(2)}) collective-permute-start(bf16[256,1920]{1,0:T(8,128)(2,1)S(1)} %pack_shard.4.refs_0_), channel_id=1, source_target_pairs={{0,3},{1,0},{2,1},{3,2},{4,7},{5,4},{6,5},{7,6},{8,11},{9,8},{10,9... | collective-permute-start | bytes 2949128 | tf_op jit(solution)/shard_map/ppermute | solution.py:184
  34.3 59.5 %collective-permute-start.9 = (bf16[256,4096]{1,0:T(8,128)(2,1)}, bf16[256,4096]{1,0:T(8,128)(2,1)S(1)}, u32[]{:S(2)}, u32[]{:S(2)}) collective-permute-start(bf16[256,4096]{1,0:T(8,128)(2,1)} %pack_shard.5.refs_0_), channel_id=1, source_target_pairs={{0,1},{1,2},{2,3},{3,0},{4,5},{5,6},{6,7},{7,4},{8,9},{9,10},{10,1... | collective-permute-start | bytes 6291464 | tf_op jit(solution)/shard_map/ppermute | solution.py:184
  38.1 55.7 %collective-permute-start.8 = (bf16[256,4096]{1,0:T(8,128)(2,1)}, bf16[256,4096]{1,0:T(8,128)(2,1)}, u32[]{:S(2)}, u32[]{:S(2)}) collective-permute-start(bf16[256,4096]{1,0:T(8,128)(2,1)} %pack_shard.5.refs_0_), channel_id=1, source_target_pairs={{0,3},{1,0},{2,1},{3,2},{4,7},{5,4},{6,5},{7,6},{8,11},{9,8},{10,9... | collective-permute-start | bytes 6291464 | tf_op jit(solution)/shard_map/ppermute | solution.py:184
  43.4 59.6 %copy-start.152 = (f32[384]{0:T(512)}, f32[384]{0:T(512)S(1)}, u32[]{:S(2)}) copy-start(f32[384]{0:T(512)S(1)} %get-tuple-element.191) | copy-start | bytes 4612
  44.4 39.7 %collective-permute-start.2 = (bf16[128,1920]{1,0:T(8,128)(2,1)}, bf16[128,1920]{1,0:T(8,128)(2,1)}, u32[]{:S(2)}, u32[]{:S(2)}) collective-permute-start(bf16[128,1920]{1,0:T(8,128)(2,1)} %slice.396), channel_id=1, source_target_pairs={{0,1},{1,2},{2,3},{3,0},{4,5},{5,6},{6,7},{7,4},{8,9},{9,10},{10,1... | collective-permute-start | bytes 1474568 | tf_op jit(solution)/shard_map/ppermute | solution.py:184
  48.7 37.8 %collective-permute-start.3 = (bf16[128,1920]{1,0:T(8,128)(2,1)}, bf16[128,1920]{1,0:T(8,128)(2,1)}, u32[]{:S(2)}, u32[]{:S(2)}) collective-permute-start(bf16[128,1920]{1,0:T(8,128)(2,1)} %slice.397), channel_id=1, source_target_pairs={{0,3},{1,0},{2,1},{3,2},{4,7},{5,4},{6,5},{7,6},{8,11},{9,8},{10,9... | collective-permute-start | bytes 1474568 | tf_op jit(solution)/shard_map/ppermute | solution.py:184
  53.3 33.3 %copy-start.166 = (f32[128]{0:T(128)}, f32[128]{0:T(128)S(1)}, u32[]{:S(2)}) copy-start(f32[128]{0:T(128)S(1)} %negate_power_fusion) | copy-start | bytes 1540
  97.0 21.5 %collective-permute-start.14 = (bf16[256,1920]{1,0:T(8,128)(2,1)}, bf16[256,1920]{1,0:T(8,128)(2,1)S(1)}, u32[]{:S(2)}, u32[]{:S(2)}) collective-permute-start(bf16[256,1920]{1,0:T(8,128)(2,1)} %pack_shard.6.refs_0_), channel_id=1, source_target_pairs={{64,65},{65,66},{66,67},{67,64},{68,69},{69,70},{70,71},{71,68},{7... | collective-permute-start | bytes 2949128 | tf_op jit(solution)/shard_map/ppermute | solution.py:184
  97.7 23.1 %collective-permute-start.13 = (bf16[256,1920]{1,0:T(8,128)(2,1)}, bf16[256,1920]{1,0:T(8,128)(2,1)}, u32[]{:S(2)}, u32[]{:S(2)}) collective-permute-start(bf16[256,1920]{1,0:T(8,128)(2,1)} %pack_shard.6.refs_0_), channel_id=1, source_target_pairs={{64,67},{65,64},{66,65},{67,66},{68,71},{69,68},{70,69},{71,70},{7... | collective-permute-start | bytes 2949128 | tf_op jit(solution)/shard_map/ppermute | solution.py:184
  105.3 20.3 %collective-permute-start.10 = (bf16[128,4096]{1,0:T(8,128)(2,1)}, bf16[128,4096]{1,0:T(8,128)(2,1)}, u32[]{:S(2)}, u32[]{:S(2)}) collective-permute-start(bf16[128,4096]{1,0:T(8,128)(2,1)} %slice.411), channel_id=1, source_target_pairs={{0,1},{1,2},{2,3},{3,0},{4,5},{5,6},{6,7},{7,4},{8,9},{9,10},{10,1... | collective-permute-start | bytes 3145736 | tf_op jit(solution)/shard_map/ppermute | solution.py:184
  111.6 17.0 %collective-permute-start.11 = (bf16[128,4096]{1,0:T(8,128)(2,1)}, bf16[128,4096]{1,0:T(8,128)(2,1)}, u32[]{:S(2)}, u32[]{:S(2)}) collective-permute-start(bf16[128,4096]{1,0:T(8,128)(2,1)} %slice.412), channel_id=1, source_target_pairs={{0,3},{1,0},{2,1},{3,2},{4,7},{5,4},{6,5},{7,6},{8,11},{9,8},{10,9... | collective-permute-start | bytes 3145736 | tf_op jit(solution)/shard_map/ppermute | solution.py:184
  119.3 16.1 %collective-permute-start.15 = (bf16[128,1920]{1,0:T(8,128)(2,1)}, bf16[128,1920]{1,0:T(8,128)(2,1)}, u32[]{:S(2)}, u32[]{:S(2)}) collective-permute-start(bf16[128,1920]{1,0:T(8,128)(2,1)} %slice.416), channel_id=1, source_target_pairs={{64,65},{65,66},{66,67},{67,64},{68,69},{69,70},{70,71},{71,68},{7... | collective-permute-start | bytes 1474568 | tf_op jit(solution)/shard_map/ppermute | solution.py:184
  122.6 12.8 %collective-permute-start.16 = (bf16[128,1920]{1,0:T(8,128)(2,1)}, bf16[128,1920]{1,0:T(8,128)(2,1)}, u32[]{:S(2)}, u32[]{:S(2)}) collective-permute-start(bf16[128,1920]{1,0:T(8,128)(2,1)} %slice.417), channel_id=1, source_target_pairs={{64,67},{65,64},{66,65},{67,66},{68,71},{69,68},{70,69},{71,70},{7... | collective-permute-start | bytes 1474568 | tf_op jit(solution)/shard_map/ppermute | solution.py:184
  124.3 67.3 %copy-start.132 = (f32[640]{0:T(1024)}, f32[640]{0:T(1024)S(1)}, u32[]{:S(2)}) copy-start(f32[640]{0:T(1024)S(1)} %mul.1042) | copy-start | bytes 7684
  125.7 38.3 %copy-start.128 = (f32[3,4,128]{2,1,0:T(4,128)}, f32[3,4,128]{2,1,0:T(4,128)S(1)}, u32[]{:S(2)}) copy-start(f32[3,4,128]{2,1,0:T(4,128)S(1)} %add_rsqrt_fusion.1) | copy-start | bytes 18436
  146.4 27.0 %collective-permute-start.7 = (bf16[2,3,128,256]{3,2,1,0:T(8,128)(2,1)}, bf16[2,3,128,256]{3,2,1,0:T(8,128)(2,1)}, u32[]{:S(2)}, u32[]{:S(2)}) collective-permute-start(bf16[2,3,128,256]{3,2,1,0:T(8,128)(2,1)} %pad_maximum_fusion.20), channel_id=1, source_target_pairs={{0,4},{4,8},{8,12},{12,16},{16,20},{20,24},{24,28},{28,32},{32,36}... | collective-permute-start | bytes 1179656 | tf_op jit(solution)/shard_map/ppermute | solution.py:192
  150.5 21.8 %collective-permute-start.6 = (bf16[2,3,128,256]{3,2,1,0:T(8,128)(2,1)}, bf16[2,3,128,256]{3,2,1,0:T(8,128)(2,1)}, u32[]{:S(2)}, u32[]{:S(2)}) collective-permute-start(bf16[2,3,128,256]{3,2,1,0:T(8,128)(2,1)} %pad_maximum_fusion.20), channel_id=1, source_target_pairs={{0,8},{4,12},{8,16},{12,20},{16,24},{20,28},{24,32},{28,36},{32,40... | collective-permute-start | bytes 1179656 | tf_op jit(solution)/shard_map/ppermute | solution.py:192
  155.2 16.1 %collective-permute-start.5 = (bf16[2,3,128,256]{3,2,1,0:T(8,128)(2,1)}, bf16[2,3,128,256]{3,2,1,0:T(8,128)(2,1)}, u32[]{:S(2)}, u32[]{:S(2)}) collective-permute-start(bf16[2,3,128,256]{3,2,1,0:T(8,128)(2,1)} %pad_maximum_fusion.20), channel_id=1, source_target_pairs={{0,12},{4,16},{8,20},{12,24},{16,28},{20,32},{24,36},{28,40},{32,4... | collective-permute-start | bytes 1179656 | tf_op jit(solution)/shard_map/ppermute | solution.py:192
  159.6 10.6 %collective-permute-start.4 = (bf16[2,3,128,256]{3,2,1,0:T(8,128)(2,1)}, bf16[2,3,128,256]{3,2,1,0:T(8,128)(2,1)}, u32[]{:S(2)}, u32[]{:S(2)}) collective-permute-start(bf16[2,3,128,256]{3,2,1,0:T(8,128)(2,1)} %pad_maximum_fusion.20), channel_id=1, source_target_pairs={{0,16},{4,20},{8,24},{12,28},{16,32},{20,36},{24,40},{28,44},{32,4... | collective-permute-start | bytes 1179656 | tf_op jit(solution)/shard_map/ppermute | solution.py:192
  192.7 11.1 %collective-permute-start.12 = (bf16[384,640]{1,0:T(8,128)(2,1)}, bf16[384,640]{1,0:T(8,128)(2,1)}, u32[]{:S(2)}, u32[]{:S(2)}) collective-permute-start(bf16[384,640]{1,0:T(8,128)(2,1)} %add_convert_fusion.1), channel_id=1, source_target_pairs={{0,64},{1,65},{2,66},{3,67},{4,68},{5,69},{6,70},{7,71},{8,72},{9,... | collective-permute-start | bytes 1474568 | tf_op jit(solution)/shard_map/ppermute | solution.py:462
  198.3 31.4 %collective-permute-start.22 = (bf16[256,4096]{1,0:T(8,128)(2,1)S(1)}, bf16[256,4096]{1,0:T(8,128)(2,1)}, u32[]{:S(2)}, u32[]{:S(2)}) collective-permute-start(bf16[256,4096]{1,0:T(8,128)(2,1)S(1)} %pack_shard.7.refs_0_), channel_id=1, source_target_pairs={{64,65},{65,66},{66,67},{67,64},{68,69},{69,70},{70,71},{71,68},{7... | collective-permute-start | bytes 6291464 | tf_op jit(solution)/shard_map/ppermute | solution.py:184
  200.2 32.2 %collective-permute-start.21 = (bf16[256,4096]{1,0:T(8,128)(2,1)S(1)}, bf16[256,4096]{1,0:T(8,128)(2,1)}, u32[]{:S(2)}, u32[]{:S(2)}) collective-permute-start(bf16[256,4096]{1,0:T(8,128)(2,1)S(1)} %pack_shard.7.refs_0_), channel_id=1, source_target_pairs={{64,67},{65,64},{66,65},{67,66},{68,71},{69,68},{70,69},{71,70},{7... | collective-permute-start | bytes 6291464 | tf_op jit(solution)/shard_map/ppermute | solution.py:184
  203.4 44.1 %copy-start.130 = (f32[640]{0:T(1024)}, f32[640]{0:T(1024)S(1)}, u32[]{:S(2)}) copy-start(f32[640]{0:T(1024)S(1)} %mul.1092) | copy-start | bytes 7684
  209.6 16.2 %collective-permute-start.20 = (bf16[2,3,128,256]{3,2,1,0:T(8,128)(2,1)}, bf16[2,3,128,256]{3,2,1,0:T(8,128)(2,1)}, u32[]{:S(2)}, u32[]{:S(2)}) collective-permute-start(bf16[2,3,128,256]{3,2,1,0:T(8,128)(2,1)} %pad_maximum_fusion.21), channel_id=1, source_target_pairs={{64,68},{68,72},{72,76},{76,80},{80,84},{84,88},{88,92},{92,96},{9... | collective-permute-start | bytes 1179656 | tf_op jit(solution)/shard_map/ppermute | solution.py:192
  211.0 13.8 %collective-permute-start.19 = (bf16[2,3,128,256]{3,2,1,0:T(8,128)(2,1)}, bf16[2,3,128,256]{3,2,1,0:T(8,128)(2,1)}, u32[]{:S(2)}, u32[]{:S(2)}) collective-permute-start(bf16[2,3,128,256]{3,2,1,0:T(8,128)(2,1)} %pad_maximum_fusion.21), channel_id=1, source_target_pairs={{64,72},{68,76},{72,80},{76,84},{80,88},{84,92},{88,96},{92,100},{... | collective-permute-start | bytes 1179656 | tf_op jit(solution)/shard_map/ppermute | solution.py:192
  212.4 10.0 %collective-permute-start.17 = (bf16[2,3,128,256]{3,2,1,0:T(8,128)(2,1)}, bf16[2,3,128,256]{3,2,1,0:T(8,128)(2,1)}, u32[]{:S(2)}, u32[]{:S(2)}) collective-permute-start(bf16[2,3,128,256]{3,2,1,0:T(8,128)(2,1)} %pad_maximum_fusion.21), channel_id=1, source_target_pairs={{64,80},{68,84},{72,88},{76,92},{80,96},{84,100},{88,104},{92,108}... | collective-permute-start | bytes 1179656 | tf_op jit(solution)/shard_map/ppermute | solution.py:192
  222.5 2.3 collective-permute-start.18
  231.7 7.3 %collective-permute-start.23 = (bf16[128,4096]{1,0:T(8,128)(2,1)S(1)}, bf16[128,4096]{1,0:T(8,128)(2,1)S(1)}, u32[]{:S(2)}, u32[]{:S(2)}) collective-permute-start(bf16[128,4096]{1,0:T(8,128)(2,1)S(1)} %slice.431), channel_id=1, source_target_pairs={{64,65},{65,66},{66,67},{67,64},{68,69},{69,70},{70,71},{71,68},{7... | collective-permute-start | bytes 3145736 | tf_op jit(solution)/shard_map/ppermute | solution.py:184
  233.8 5.2 collective-permute-start.24
  284.5 11.4 %collective-permute-start.25 = (bf16[128,4096]{1,0:T(8,128)(2,1)S(1)}, bf16[128,4096]{1,0:T(8,128)(2,1)S(1)}, u32[]{:S(2)}, u32[]{:S(2)}) collective-permute-start(bf16[128,4096]{1,0:T(8,128)(2,1)S(1)} %get-tuple-element.55), channel_id=1, source_target_pairs={{64,65},{65,66},{66,67},{67,64},{68,69},{69,70},{70,71},{71,68},{7... | collective-permute-start | bytes 3145736 | tf_op jit(solution)/shard_map/ppermute | solution.py:184
  285.4 10.6 %collective-permute-start.26 = (bf16[128,4096]{1,0:T(8,128)(2,1)S(1)}, bf16[128,4096]{1,0:T(8,128)(2,1)S(1)}, u32[]{:S(2)}, u32[]{:S(2)}) collective-permute-start(bf16[128,4096]{1,0:T(8,128)(2,1)S(1)} %get-tuple-element.56), channel_id=1, source_target_pairs={{64,67},{65,64},{66,65},{67,66},{68,71},{69,68},{70,69},{71,70},{7... | collective-permute-start | bytes 3145736 | tf_op jit(solution)/shard_map/ppermute | solution.py:184
  304.5 107.3 %collective-permute-start.33 = (bf16[256,4096]{1,0:T(8,128)(2,1)}, bf16[256,4096]{1,0:T(8,128)(2,1)}, u32[]{:S(2)}, u32[]{:S(2)}) collective-permute-start(bf16[256,4096]{1,0:T(8,128)(2,1)} %add_dynamic-update-slice_fusion.2), channel_id=1, source_target_pairs={{64,67},{65,64},{66,65},{67,66},{68,71},{69,68},{70,69},{71,70},{7... | collective-permute-start | bytes 6291464 | tf_op jit(solution)/shard_map/ppermute | solution.py:184
  308.1 15.6 %collective-permute-start.27 = (bf16[2,3,128,256]{3,2,1,0:T(8,128)(2,1)}, bf16[2,3,128,256]{3,2,1,0:T(8,128)(2,1)}, u32[]{:S(2)}, u32[]{:S(2)}) collective-permute-start(bf16[2,3,128,256]{3,2,1,0:T(8,128)(2,1)} %get-tuple-element.161), channel_id=1, source_target_pairs={{80,64},{84,68},{88,72},{92,76},{96,80},{100,84},{104,88},{108,92}... | collective-permute-start | bytes 1179656 | tf_op jit(solution)/shard_map/ppermute | solution.py:192
  309.6 16.3 %collective-permute-start.30 = (bf16[2,3,128,256]{3,2,1,0:T(8,128)(2,1)}, bf16[2,3,128,256]{3,2,1,0:T(8,128)(2,1)}, u32[]{:S(2)}, u32[]{:S(2)}) collective-permute-start(bf16[2,3,128,256]{3,2,1,0:T(8,128)(2,1)} %get-tuple-element.162), channel_id=1, source_target_pairs={{68,64},{72,68},{76,72},{80,76},{84,80},{88,84},{92,88},{96,92},{1... | collective-permute-start | bytes 1179656 | tf_op jit(solution)/shard_map/ppermute | solution.py:192
  311.0 14.9 %collective-permute-start.29 = (bf16[2,3,128,256]{3,2,1,0:T(8,128)(2,1)}, bf16[2,3,128,256]{3,2,1,0:T(8,128)(2,1)}, u32[]{:S(2)}, u32[]{:S(2)}) collective-permute-start(bf16[2,3,128,256]{3,2,1,0:T(8,128)(2,1)} %get-tuple-element.163), channel_id=1, source_target_pairs={{72,64},{76,68},{80,72},{84,76},{88,80},{92,84},{96,88},{100,92},{... | collective-permute-start | bytes 1179656 | tf_op jit(solution)/shard_map/ppermute | solution.py:192
  312.4 13.5 %collective-permute-start.28 = (bf16[2,3,128,256]{3,2,1,0:T(8,128)(2,1)}, bf16[2,3,128,256]{3,2,1,0:T(8,128)(2,1)}, u32[]{:S(2)}, u32[]{:S(2)}) collective-permute-start(bf16[2,3,128,256]{3,2,1,0:T(8,128)(2,1)} %get-tuple-element.164), channel_id=1, source_target_pairs={{76,64},{80,68},{84,72},{88,76},{92,80},{96,84},{100,88},{104,92},... | collective-permute-start | bytes 1179656 | tf_op jit(solution)/shard_map/ppermute | solution.py:192
  323.7 88.1 %collective-permute-start.32 = (bf16[256,4096]{1,0:T(8,128)(2,1)}, bf16[256,4096]{1,0:T(8,128)(2,1)}, u32[]{:S(2)}, u32[]{:S(2)}) collective-permute-start(bf16[256,4096]{1,0:T(8,128)(2,1)} %add_dynamic-update-slice_fusion.3), channel_id=1, source_target_pairs={{64,65},{65,66},{66,67},{67,64},{68,69},{69,70},{70,71},{71,68},{7... | collective-permute-start | bytes 6291464 | tf_op jit(solution)/shard_map/ppermute | solution.py:184
  335.6 30.0 %collective-permute-start.31 = (bf16[384,640]{1,0:T(8,128)(2,1)S(1)}, bf16[384,640]{1,0:T(8,128)(2,1)S(1)}, u32[]{:S(2)}, u32[]{:S(2)}) collective-permute-start(bf16[384,640]{1,0:T(8,128)(2,1)S(1)} %fusion.207), channel_id=1, source_target_pairs={{64,0},{65,1},{66,2},{67,3},{68,4},{69,5},{70,6},{71,7},{72,8},{73... | collective-permute-start | bytes 1474568 | tf_op jit(solution)/shard_map/ppermute | solution.py:469
  339.6 26.1 %copy-start.63 = (f32[384,640]{1,0:T(8,128)S(1)}, f32[384,640]{1,0:T(8,128)}, u32[]{:S(2)}) copy-start(f32[384,640]{1,0:T(8,128)} %copy-done.62) | copy-start | bytes 2949124
  339.6 26.1 %copy-start.133 = (f32[640]{0:T(1024)S(1)}, f32[640]{0:T(1024)}, u32[]{:S(2)}) copy-start(f32[640]{0:T(1024)} %copy-done.132) | copy-start | bytes 7684
  339.6 26.1 %copy-start.150 = (f32[384]{0:T(512)S(1)}, f32[384]{0:T(512)}, u32[]{:S(2)}) copy-start(f32[384]{0:T(512)} %copy-done.149) | copy-start | bytes 4612
  341.2 25.5 %copy-start.35 = (bf16[2048,640]{1,0:T(8,128)(2,1)S(1)}, bf16[2048,640]{1,0:T(8,128)(2,1)}, u32[]{:S(2)}) copy-start(bf16[2048,640]{1,0:T(8,128)(2,1)} %copy-done.33) | copy-start | bytes 7864324
  341.2 47.1 %collective-permute-start.34 = (bf16[128,1920]{1,0:T(8,128)(2,1)S(1)}, bf16[128,1920]{1,0:T(8,128)(2,1)S(1)}, u32[]{:S(2)}, u32[]{:S(2)}) collective-permute-start(bf16[128,1920]{1,0:T(8,128)(2,1)S(1)} %get-tuple-element.60), channel_id=1, source_target_pairs={{64,65},{65,66},{66,67},{67,64},{68,69},{69,70},{70,71},{71,68},{7... | collective-permute-start | bytes 1474568 | tf_op jit(solution)/shard_map/ppermute | solution.py:184
  342.1 48.4 %collective-permute-start.36 = (bf16[128,1920]{1,0:T(8,128)(2,1)S(1)}, bf16[128,1920]{1,0:T(8,128)(2,1)S(1)}, u32[]{:S(2)}, u32[]{:S(2)}) collective-permute-start(bf16[128,1920]{1,0:T(8,128)(2,1)S(1)} %get-tuple-element.62), channel_id=1, source_target_pairs={{64,67},{65,64},{66,65},{67,66},{68,71},{69,68},{70,69},{71,70},{7... | collective-permute-start | bytes 1474568 | tf_op jit(solution)/shard_map/ppermute | solution.py:184
  382.1 17.0 %collective-permute-start.39 = (bf16[128,4096]{1,0:T(8,128)(2,1)}, bf16[128,4096]{1,0:T(8,128)(2,1)}, u32[]{:S(2)}, u32[]{:S(2)}) collective-permute-start(bf16[128,4096]{1,0:T(8,128)(2,1)} %get-tuple-element.64), channel_id=1, source_target_pairs={{0,3},{1,0},{2,1},{3,2},{4,7},{5,4},{6,5},{7,6},{8,11},{9,8},{10,9... | collective-permute-start | bytes 3145736 | tf_op jit(solution)/shard_map/ppermute | solution.py:184
  388.3 18.2 %collective-permute-start.38 = (bf16[128,4096]{1,0:T(8,128)(2,1)}, bf16[128,4096]{1,0:T(8,128)(2,1)}, u32[]{:S(2)}, u32[]{:S(2)}) collective-permute-start(bf16[128,4096]{1,0:T(8,128)(2,1)} %get-tuple-element.63), channel_id=1, source_target_pairs={{0,1},{1,2},{2,3},{3,0},{4,5},{5,6},{6,7},{7,4},{8,9},{9,10},{10,1... | collective-permute-start | bytes 3145736 | tf_op jit(solution)/shard_map/ppermute | solution.py:184
  391.5 28.8 %collective-permute-start.37 = (bf16[256,1920]{1,0:T(8,128)(2,1)S(1)}, bf16[256,1920]{1,0:T(8,128)(2,1)}, u32[]{:S(2)}, u32[]{:S(2)}) collective-permute-start(bf16[256,1920]{1,0:T(8,128)(2,1)S(1)} %add_dynamic-update-slice_fusion.6), channel_id=1, source_target_pairs={{64,67},{65,64},{66,65},{67,66},{68,71},{69,68},{70,69},{71,70},{7... | collective-permute-start | bytes 2949128 | tf_op jit(solution)/shard_map/ppermute | solution.py:184
  399.1 21.1 %collective-permute-start.35 = (bf16[256,1920]{1,0:T(8,128)(2,1)}, bf16[256,1920]{1,0:T(8,128)(2,1)}, u32[]{:S(2)}, u32[]{:S(2)}) collective-permute-start(bf16[256,1920]{1,0:T(8,128)(2,1)} %copy-done.30), channel_id=1, source_target_pairs={{64,65},{65,66},{66,67},{67,64},{68,69},{69,70},{70,71},{71,68},{7... | collective-permute-start | bytes 2949128 | tf_op jit(solution)/shard_map/ppermute | solution.py:184
  406.5 82.3 %collective-permute-start.49 = (bf16[256,4096]{1,0:T(8,128)(2,1)}, bf16[256,4096]{1,0:T(8,128)(2,1)}, u32[]{:S(2)}, u32[]{:S(2)}) collective-permute-start(bf16[256,4096]{1,0:T(8,128)(2,1)} %add_dynamic-update-slice_fusion), channel_id=1, source_target_pairs={{0,3},{1,0},{2,1},{3,2},{4,7},{5,4},{6,5},{7,6},{8,11},{9,8},{10,9... | collective-permute-start | bytes 6291464 | tf_op jit(solution)/shard_map/ppermute | solution.py:184
  450.2 14.3 %collective-permute-start.40 = (bf16[2,3,128,256]{3,2,1,0:T(8,128)(2,1)}, bf16[2,3,128,256]{3,2,1,0:T(8,128)(2,1)}, u32[]{:S(2)}, u32[]{:S(2)}) collective-permute-start(bf16[2,3,128,256]{3,2,1,0:T(8,128)(2,1)} %get-tuple-element.155), channel_id=1, source_target_pairs={{16,0},{20,4},{24,8},{28,12},{32,16},{36,20},{40,24},{44,28},{48,3... | collective-permute-start | bytes 1179656 | tf_op jit(solution)/shard_map/ppermute | solution.py:192
  451.5 16.6 %collective-permute-start.43 = (bf16[2,3,128,256]{3,2,1,0:T(8,128)(2,1)}, bf16[2,3,128,256]{3,2,1,0:T(8,128)(2,1)}, u32[]{:S(2)}, u32[]{:S(2)}) collective-permute-start(bf16[2,3,128,256]{3,2,1,0:T(8,128)(2,1)} %get-tuple-element.156), channel_id=1, source_target_pairs={{4,0},{8,4},{12,8},{16,12},{20,16},{24,20},{28,24},{32,28},{36,32}... | collective-permute-start | bytes 1179656 | tf_op jit(solution)/shard_map/ppermute | solution.py:192
  452.8 15.3 %collective-permute-start.42 = (bf16[2,3,128,256]{3,2,1,0:T(8,128)(2,1)}, bf16[2,3,128,256]{3,2,1,0:T(8,128)(2,1)}, u32[]{:S(2)}, u32[]{:S(2)}) collective-permute-start(bf16[2,3,128,256]{3,2,1,0:T(8,128)(2,1)} %get-tuple-element.157), channel_id=1, source_target_pairs={{8,0},{12,4},{16,8},{20,12},{24,16},{28,20},{32,24},{36,28},{40,32... | collective-permute-start | bytes 1179656 | tf_op jit(solution)/shard_map/ppermute | solution.py:192
  454.1 18.8 %collective-permute-start.41 = (bf16[2,3,128,256]{3,2,1,0:T(8,128)(2,1)}, bf16[2,3,128,256]{3,2,1,0:T(8,128)(2,1)}, u32[]{:S(2)}, u32[]{:S(2)}) collective-permute-start(bf16[2,3,128,256]{3,2,1,0:T(8,128)(2,1)} %get-tuple-element.158), channel_id=1, source_target_pairs={{12,0},{16,4},{20,8},{24,12},{28,16},{32,20},{36,24},{40,28},{44,3... | collective-permute-start | bytes 1179656 | tf_op jit(solution)/shard_map/ppermute | solution.py:192
  464.5 29.4 %collective-permute-start.48 = (bf16[256,4096]{1,0:T(8,128)(2,1)}, bf16[256,4096]{1,0:T(8,128)(2,1)}, u32[]{:S(2)}, u32[]{:S(2)}) collective-permute-start(bf16[256,4096]{1,0:T(8,128)(2,1)} %add_dynamic-update-slice_fusion.1), channel_id=1, source_target_pairs={{0,1},{1,2},{2,3},{3,0},{4,5},{5,6},{6,7},{7,4},{8,9},{9,10},{10,1... | collective-permute-start | bytes 6291464 | tf_op jit(solution)/shard_map/ppermute | solution.py:184
  486.9 37.8 %collective-permute-start.46 = (bf16[128,1920]{1,0:T(8,128)(2,1)}, bf16[128,1920]{1,0:T(8,128)(2,1)}, u32[]{:S(2)}, u32[]{:S(2)}) collective-permute-start(bf16[128,1920]{1,0:T(8,128)(2,1)} %get-tuple-element.69), channel_id=1, source_target_pairs={{0,3},{1,0},{2,1},{3,2},{4,7},{5,4},{6,5},{7,6},{8,11},{9,8},{10,9... | collective-permute-start | bytes 1474568 | tf_op jit(solution)/shard_map/ppermute | solution.py:184
  501.1 33.5 %copy-start.32 = (bf16[256,1920]{1,0:T(8,128)(2,1)S(1)}, bf16[256,1920]{1,0:T(8,128)(2,1)}, u32[]{:S(2)}) copy-start(bf16[256,1920]{1,0:T(8,128)(2,1)} %copy-done.31) | copy-start | bytes 2949124
  501.1 47.4 %all-to-all-start.1 = ((bf16[16,16,4096]{2,1,0:T(8,128)(2,1)}), bf16[16,16,4096]{2,1,0:T(8,128)(2,1)}, u32[]{:S(2)}, u32[]{:S(2)}) async-start(bf16[16,16,4096]{2,1,0:T(8,128)(2,1)} %bitcast.321), calls=%async_computation.1 | async-start | bytes 4194304 | tf_op jit(solution)/shard_map/all_to_all | solution.py:485
  522.5 81.5 %all-gather.2.cloned.1.call-start = ((), (), s32[]{:S(2)}) async-start(), calls=%async_computation.2 | async-start | bytes 2228224 | tf_op jit(solution)/shard_map/all_gather | solution.py:487
  522.6 11.9 %collective-permute-start.44 = (bf16[128,1920]{1,0:T(8,128)(2,1)S(1)}, bf16[128,1920]{1,0:T(8,128)(2,1)S(1)}, u32[]{:S(2)}, u32[]{:S(2)}) collective-permute-start(bf16[128,1920]{1,0:T(8,128)(2,1)S(1)} %copy-done.44), channel_id=1, source_target_pairs={{0,1},{1,2},{2,3},{3,0},{4,5},{5,6},{6,7},{7,4},{8,9},{9,10},{10,1... | collective-permute-start | bytes 1474568 | tf_op jit(solution)/shard_map/ppermute | solution.py:184
  526.8 24.3 %collective-permute-start.47 = (bf16[256,1920]{1,0:T(8,128)(2,1)}, bf16[256,1920]{1,0:T(8,128)(2,1)}, u32[]{:S(2)}, u32[]{:S(2)}) collective-permute-start(bf16[256,1920]{1,0:T(8,128)(2,1)} %add_dynamic-update-slice_fusion.4), channel_id=1, source_target_pairs={{0,3},{1,0},{2,1},{3,2},{4,7},{5,4},{6,5},{7,6},{8,11},{9,8},{10,9... | collective-permute-start | bytes 2949128 | tf_op jit(solution)/shard_map/ppermute | solution.py:184
  534.7 17.3 %collective-permute-start.45 = (bf16[256,1920]{1,0:T(8,128)(2,1)S(1)}, bf16[256,1920]{1,0:T(8,128)(2,1)}, u32[]{:S(2)}, u32[]{:S(2)}) collective-permute-start(bf16[256,1920]{1,0:T(8,128)(2,1)S(1)} %add_dynamic-update-slice_fusion.5), channel_id=1, source_target_pairs={{0,1},{1,2},{2,3},{3,0},{4,5},{5,6},{6,7},{7,4},{8,9},{9,10},{10,1... | collective-permute-start | bytes 2949128 | tf_op jit(solution)/shard_map/ppermute | solution.py:184
  555.9 20.5 %all-to-all-start = ((bf16[16,16,1920]{2,1,0:T(8,128)(2,1)}), bf16[16,16,1920]{2,1,0:T(8,128)(2,1)}, u32[]{:S(2)}, u32[]{:S(2)}) async-start(bf16[16,16,1920]{2,1,0:T(8,128)(2,1)} %bitcast.322), calls=%async_computation | async-start | bytes 1966080 | tf_op jit(solution)/shard_map/all_to_all | solution.py:485
  (177 other events, 1021.3 us)
Sparse Core Ops, SparseCore 0:
  551.3 42.3 all-gather.1

commit v3 on v2

--- a/solution.py
+++ b/solution.py
@@ -100,7 +100,7 @@
     )(value, *after)
 
 
-def unpack_full(place, pieces, plan, shapes):
+def unpack_full(place, pieces, plan, shapes, after=()):
     arrays = [item[0] for item in pieces]
     jobs = []
     for index, (_, rel, first, count) in enumerate(pieces):
@@ -111,7 +111,7 @@
 
     def body(place_ref, *refs):
         sources = refs[: len(arrays)]
-        outs = refs[len(arrays) : len(arrays) + len(shapes)]
+        outs = refs[-1 - len(shapes) : -1]
         sems = refs[-1]
         here = place_ref[0]
         copies = []
@@ -130,13 +130,13 @@
 
     return pl.pallas_call(
         body,
-        in_specs=[pl.BlockSpec(memory_space=pltpu.SMEM)] + in_any(len(arrays)),
+        in_specs=[pl.BlockSpec(memory_space=pltpu.SMEM)] + in_any(len(arrays) + len(after)),
         out_specs=in_vmem(len(shapes)),
         compiler_params=pltpu.CompilerParams(vmem_limit_bytes=LIMIT),
         out_shape=[jax.ShapeDtypeStruct(shape, jnp.bfloat16) for shape in shapes],
         scratch_shapes=[pltpu.SemaphoreType.DMA((len(jobs),))],
         name="unpack_full",
-    )(place, *arrays)
+    )(place, *arrays, *after)
 
 
 def pack_blocks(place, arrays, plan, cols):
@@ -179,9 +179,8 @@
     )(place, *arrays)
 
 
-def along_z(x, section, by):
-    pairs = [(section * RING + i, section * RING + (i + by) % RING) for i in range(RING)]
-    return lax.ppermute(x, ("section", "z"), pairs)
+def along_z(x, by):
+    return lax.ppermute(x, "z", [(i, (i + by) % RING) for i in range(RING)])
 
 
 def along_seq(x, section, by):
@@ -192,33 +191,49 @@
     return lax.ppermute(x, ("section", "y", "x"), pairs)
 
 
-def gather_weights(shard, section, place, plan, shapes):
+def gather_weights(shard):
     half = ROWS // 2
-    above = along_z(shard, section, -1)
-    below = along_z(shard, section, 1)
-    first = along_z(below[:half], section, 1)
-    second = along_z(above[half:], section, -1)
-    pieces = (
+    above = along_z(shard, -1)
+    below = along_z(shard, 1)
+    first = along_z(below[:half], 1)
+    second = along_z(above[half:], -1)
+    return (
         (shard, 0, 0, ROWS),
         (above, 1, 0, ROWS),
         (below, 3, 0, ROWS),
         (first, 2, 0, half),
         (second, 2, half, half),
     )
-    return unpack_full(place, pieces, plan, shapes), (above, below)
-
-
-def reduce_z_begin(place, section, arrays, plan, cols):
+
+
+def reduce_z_begin(place, arrays, plan, cols):
     own, after, before, far_a, far_b = pack_blocks(place, arrays, plan, cols)
-    return own, after, before, along_z(far_a, section, 1), along_z(far_b, section, -1)
-
-
-def reduce_z_end(begun, section):
+    return own, after, before, along_z(far_a, 1), along_z(far_b, -1)
+
+
+def reduce_z_end(begun):
     own, after, before, got_a, got_b = begun
     half = ROWS // 2
     after = lax.dynamic_update_slice(after, after[:half] + got_a, (0, 0))
     before = lax.dynamic_update_slice(before, before[half:] + got_b, (half, 0))
-    return own, along_z(after, section, 1), along_z(before, section, -1)
+    return own, along_z(after, 1), along_z(before, -1)
+
+
+def unpack_grads(packed, plan, shapes):
+    def body(source, *outs):
+        for a, r, n, c, w, pr, pc in plan:
+            outs[a][pl.ds(r, n), pl.ds(c, w)] = source[pl.ds(pr, n), pl.ds(pc, w)].astype(
+                jnp.float32
+            )
+
+    return pl.pallas_call(
+        body,
+        in_specs=in_vmem(1),
+        out_specs=in_vmem(len(shapes)),
+        out_shape=[jax.ShapeDtypeStruct(shape, jnp.float32) for shape in shapes],
+        compiler_params=pltpu.CompilerParams(vmem_limit_bytes=LIMIT),
+        name="unpack_grads",
+    )(packed)
 
 
 def total_of(parts):
@@ -259,9 +274,8 @@
     return jnp.einsum(spec, left, right, preferred_element_type=jnp.float32)
 
 
-def forward_layer(inputs, tables, allowed, attn_w, ffn_w, gains, section):
+def forward_layer(inputs, tables, allowed, attn_w, gains, section, ffn_weights):
     qkv_w, output_w = attn_w
-    gate_up_w, down_w = ffn_w
     pre_g, query_g, key_g, mix_g, ffn_g, out_g = gains
     cosine, sine = tables
     normed = normalize(inputs, pre_g).astype(jnp.bfloat16)
@@ -287,6 +301,7 @@
     prob = expo / jnp.sum(expo, axis=-1, keepdims=True)
     mixed = batched("mhqk,mkd->mhqd", prob.astype(jnp.bfloat16), values_all).astype(jnp.bfloat16)
     mixed = jnp.swapaxes(mixed, 1, 2).reshape(TOKENS, QH * HD)
+    mixed, (gate_up_w, down_w) = ffn_weights(mixed)
     branch = product(mixed, output_w)
     middle = inputs + normalize(branch, mix_g)
     inner = normalize(middle, ffn_g).astype(jnp.bfloat16)
@@ -303,6 +318,10 @@
     return result, stored
 
 
+ATTN_SHAPES = ((D, QH * HD + 2 * HD), (QH * HD, D), (RING * 32, D))
+FFN_SHAPES = ((D, 2 * FF), (FF, D))
+
+
 def norm_back(grad, values, gain):
     scale = lax.rsqrt(jnp.mean(values * values, axis=-1, keepdims=True) + EPSILON)
     unit = values * scale
@@ -312,8 +331,12 @@
 
 
 def backward_layer(
-    grad_out, stored, tables, attn_w, ffn_w, gains, section, place, other_ffn=None, other_attn=None
+    grad_out, stored, tables, attn_w, ffn_w, gains, section, place=None, leading=None, other=None
 ):
+    def chosen(name, mine):
+        return jnp.where(leading, mine, other[name])
+
+    kept = {}
     (
         inputs, normed, query_raw, key_raw, query_rot, keys_all, values_all, prob, mixed, branch,
         middle, inner, gate_act, up_act, hidden, down,
@@ -331,10 +354,14 @@
     )
     d_gate, d_up = pull(d_hidden)
     d_gate_up = jnp.concatenate([d_gate.astype(jnp.bfloat16), d_up.astype(jnp.bfloat16)], axis=1)
-    grad_ffn = (inner_rows(inner, d_gate_up), inner_rows(hidden, d_down))
-    ffn_begun = reduce_z_begin(place, section, grad_ffn, FFN_GRAD_PLAN, FFN_COLS)
-    if other_ffn is not None:
-        d_gate_up = ordered(d_gate_up, *other_ffn[1:])
+    kept.update(inner=inner, d_gate_up=d_gate_up, hidden=hidden, d_down=d_down)
+    if other is not None:
+        picked = {name: chosen(name, kept[name]) for name in kept}
+        grad_ffn = (
+            inner_rows(picked["inner"], picked["d_gate_up"]),
+            inner_rows(picked["hidden"], picked["d_down"]),
+        )
+        ffn_begun = reduce_z_begin(place, grad_ffn, FFN_GRAD_PLAN, FFN_COLS)
     d_inner = against(d_gate_up, gate_up_w)
     d_middle_ffn, by_ffn = norm_back(d_inner, middle, ffn_g)
     d_ffn_g = jnp.sum(by_ffn, axis=0)
@@ -342,16 +369,15 @@
     d_branch, by_mix = norm_back(d_middle, branch, mix_g)
     d_mix_g = jnp.sum(by_mix, axis=0)
     d_branch = d_branch.astype(jnp.bfloat16)
-    if other_attn is not None:
-        d_branch = ordered(d_branch, *other_attn[1:])
-    d_mixed = against(d_branch, output_w).astype(jnp.bfloat16).reshape(MICRO, SHARD, QH, HD)
-    d_mixed = jnp.swapaxes(d_mixed, 1, 2)
+    d_mixed = against(d_branch, output_w).astype(jnp.bfloat16)
+    if other is not None:
+        d_mixed = ordered(d_mixed, ffn_begun[3], ffn_begun[4])
+        ffn_parts = reduce_z_end(ffn_begun)
+    d_mixed = jnp.swapaxes(d_mixed.reshape(MICRO, SHARD, QH, HD), 1, 2)
     d_prob = batched("mhqd,mkd->mhqk", d_mixed, values_all)
     d_score = (prob * (d_prob - jnp.sum(prob * d_prob, axis=-1, keepdims=True))).astype(
         jnp.bfloat16
     )
-    d_score = ordered(d_score, ffn_begun[3], ffn_begun[4])
-    ffn_parts = reduce_z_end(ffn_begun, section)
     scale = HD ** (-0.5)
     d_keys = batched("mhqk,mhqd->mkd", d_score, query_rot) * scale
     d_values_all = batched("mhqk,mhqd->mkd", prob.astype(jnp.bfloat16), d_mixed)
@@ -377,6 +403,8 @@
     d_key, by_key = norm_back(turn(back[0], cosine, -sine), key_raw, key_g)
     d_key_g = jnp.sum(by_key, axis=0)
     d_qkv = jnp.concatenate([d_query, d_key.astype(jnp.bfloat16), d_values], axis=1)
+    if other is not None:
+        d_qkv = ordered(d_qkv, *ffn_parts[1:])
     d_normed = against(d_qkv, qkv_w)
     d_inputs_pre, by_pre = norm_back(d_normed, inputs, pre_g)
     d_pre_g = jnp.sum(by_pre, axis=0)
@@ -390,12 +418,20 @@
         ],
         axis=1,
     ).astype(jnp.bfloat16)
+    last = dict(
+        normed=normed, d_qkv=d_qkv, mixed=mixed, d_branch=d_branch, rows=rows.reshape(RING * 32, D)
+    )
+    kept.update(last)
+    if other is None:
+        return d_inputs, kept
+    picked = {name: chosen(name, last[name]) for name in last}
     grad_attn = (
-        inner_rows(normed, d_qkv),
-        inner_rows(mixed, d_branch),
-        rows.reshape(RING * 32, D),
-    )
-    return d_inputs, ffn_parts, grad_attn
+        inner_rows(picked["normed"], picked["d_qkv"]),
+        inner_rows(picked["mixed"], picked["d_branch"]),
+        picked["rows"],
+    )
+    attn_parts = reduce_z_end(reduce_z_begin(place, grad_attn, ATTN_GRAD_PLAN, ATTN_COLS))
+    return d_inputs, ffn_parts, attn_parts
 
 
 GAIN_SIZES = (D, HD, HD, D, D, D)
@@ -422,24 +458,25 @@
     )
     attn_arrays = (query_weight[0], key_weight[0], value_weight[0], output_weight[0], gain_shard)
     ffn_arrays = (gate_weight[0], up_weight[0], down_weight[0])
-    attn_shapes = ((D, QH * HD + 2 * HD), (QH * HD, D), (RING * 32, D))
-    ffn_shapes = ((D, 2 * FF), (FF, D))
-    weights = []
-    gains = []
-    seen = ()
-    for section in range(2):
-        shard = pack_shard(attn_arrays, ATTN_PLAN, ATTN_COLS, seen)
-        attn, seen = gather_weights(shard, section, place, ATTN_GRAD_PLAN, attn_shapes)
-        shard = pack_shard(ffn_arrays, FFN_PLAN, FFN_COLS, seen)
-        ffn, seen = gather_weights(shard, section, place, FFN_GRAD_PLAN, ffn_shapes)
-        weights.append((attn[:2], ffn))
-        corner = attn[2].reshape(RING, 32, D).astype(jnp.float32)
-        gains.append(
-            [
-                corner[:, row, : size // RING].reshape(size)
-                for row, size in zip(GAIN_ROWS, GAIN_SIZES)
-            ]
-        )
+    attn_pieces = gather_weights(pack_shard(attn_arrays, ATTN_PLAN, ATTN_COLS))
+    ffn_shard = pack_shard(
+        ffn_arrays, FFN_PLAN, FFN_COLS, (attn_pieces[3][0], attn_pieces[4][0])
+    )
+    ffn_pieces = gather_weights(ffn_shard)
+    qkv_w, output_w, corner = unpack_full(
+        place, attn_pieces, ATTN_GRAD_PLAN, ATTN_SHAPES, (ffn_shard,)
+    )
+    attn_w = (qkv_w, output_w)
+    corner = corner.reshape(RING, 32, D).astype(jnp.float32)
+    gains = [
+        corner[:, row, : size // RING].reshape(size) for row, size in zip(GAIN_ROWS, GAIN_SIZES)
+    ]
+    ffn_w = []
+
+    def await_ffn(mixed):
+        mixed = ordered(mixed, ffn_pieces[1][0], ffn_pieces[2][0])
+        ffn_w.extend(unpack_full(place, ffn_pieces, FFN_GRAD_PLAN, FFN_SHAPES, (mixed,)))
+        return mixed, ffn_w
 
     exponent = jnp.arange(HD // 2).astype(jnp.float32) * (2.0 / HD)
     freqs = ROPE_BASE ** (-exponent)
@@ -458,59 +495,49 @@
     allowed = allowed[None] & (query_seg[:, :, None] == key_seg[:, None, :])
 
     first_in = hidden_in[:, 0].reshape(TOKENS, D).astype(jnp.float32)
-    first_out, first_kept = forward_layer(first_in, tables, allowed, *weights[0], gains[0], 0)
+    first_out, first_kept = forward_layer(
+        first_in, tables, allowed, attn_w, gains, 0, await_ffn
+    )
     handed = lax.ppermute(first_out, "section", [(0, 1)]).astype(jnp.float32)
-    second_out, second_kept = forward_layer(handed, tables, allowed, *weights[1], gains[1], 1)
+    second_out, second_kept = forward_layer(
+        handed, tables, allowed, attn_w, gains, 1, lambda mixed: (mixed, ffn_w)
+    )
 
     cot = cotangent[:, 0].reshape(TOKENS, D).astype(jnp.float32)
-    d_second, ffn_parts1, attn_grad1 = backward_layer(
-        cot, second_kept, tables, *weights[1], gains[1], 1, place
-    )
+    d_second, left = backward_layer(cot, second_kept, tables, attn_w, ffn_w, gains, 1)
     d_first_out = lax.ppermute(d_second.astype(jnp.bfloat16), "section", [(1, 0)])
-    attn_parts1 = reduce_z_end(
-        reduce_z_begin(place, 1, attn_grad1, ATTN_GRAD_PLAN, ATTN_COLS), 1
-    )
-    d_first, ffn_parts0, attn_grad0 = backward_layer(
-        d_first_out.astype(jnp.float32), first_kept, tables, *weights[0], gains[0], 0, place,
-        ffn_parts1, attn_parts1,
-    )
-    attn_parts0 = reduce_z_end(
-        reduce_z_begin(place, 0, attn_grad0, ATTN_GRAD_PLAN, ATTN_COLS), 0
-    )
-
-    def finish(parts0, parts1, cols):
-        mine = jnp.where(leading, total_of(parts0), total_of(parts1)).astype(jnp.bfloat16)
+    d_first, ffn_parts, attn_parts = backward_layer(
+        d_first_out.astype(jnp.float32), first_kept, tables, attn_w, ffn_w, gains, 0,
+        place, leading, left,
+    )
+
+    def finish(parts, cols):
+        mine = total_of(parts).astype(jnp.bfloat16)
         count = RING * RING
         split = mine.reshape(count, ROWS // count, cols)
         moved = lax.all_to_all(split, ("y", "x"), split_axis=0, concat_axis=0, tiled=True)
         summed = jnp.sum(moved.astype(jnp.float32), axis=0).astype(jnp.bfloat16)
         return lax.all_gather(summed, ("y", "x"), axis=0, tiled=True)
 
-    ffn_done = finish(ffn_parts0, ffn_parts1, FFN_COLS)
-    attn_done = finish(attn_parts0, attn_parts1, ATTN_COLS)
-
-    def restore(packed, plan, which):
-        return jnp.concatenate(
-            [packed[pr : pr + n, pc : pc + w] for a, r, n, c, w, pr, pc in plan if a == which]
-        ).astype(jnp.float32)[None]
-
-    corner = attn_done[224:256, 1280:1920].astype(jnp.float32)
+    ffn_done = finish(ffn_parts, FFN_COLS)
+    attn_done = finish(attn_parts, ATTN_COLS)
+
+    ffn_outs = unpack_grads(ffn_done, FFN_PLAN, ((160, FF), (160, FF), (512, D)))
+    attn_outs = unpack_grads(
+        attn_done, ATTN_PLAN, ((160, QH * HD), (160, HD), (160, HD), (256, D), (32, D))
+    )
     gain_outs = [
-        corner[row : row + 1, : size // RING] for row, size in zip(GAIN_ROWS, GAIN_SIZES)
+        attn_outs[4][row : row + 1, : size // RING] for row, size in zip(GAIN_ROWS, GAIN_SIZES)
     ]
     outputs = jnp.where(leading, first_out, second_out).reshape(1, MICRO, 1, SHARD, D)
     input_grads = jnp.where(leading, d_first, d_second).reshape(1, MICRO, 1, SHARD, D)
     return (
         outputs,
         input_grads,
-        restore(attn_done, ATTN_PLAN, 0),
-        restore(attn_done, ATTN_PLAN, 1),
-        restore(attn_done, ATTN_PLAN, 2),
-        restore(attn_done, ATTN_PLAN, 3),
-        restore(ffn_done, FFN_PLAN, 0),
-        restore(ffn_done, FFN_PLAN, 1),
-        restore(ffn_done, FFN_PLAN, 2),
-    ) + tuple(gain_outs)
+        *(item[None] for item in attn_outs[:4]),
+        *(item[None] for item in ffn_outs),
+        *gain_outs,
+    )
 
 
 def solution(mesh):

time: 629 us -> 518 us (0.82)
  starting transfers between devices: 139 us -> 84.3 us
  waiting for transfers between devices: 119 us -> 171 us
  other arithmetic: 106 us -> 62.9 us
  local copies, waits for them, and re-layouts: 100 us -> 66.1 us
  matrix products: 94.5 us -> 71.1 us
  Pallas kernels: 20.9 us -> 13.6 us
    ppermute x32 -> x16, starting transfers between devices: 73.7 us -> 29.2 us  [along_z(): return lax.ppermute(x, 'z', [(i, (i + by) % RING) for i in range(RING)])]
    ppermute x32 -> x16, waiting for transfers between devices: 62.4 us -> 101 us  [along_z(): return lax.ppermute(x, 'z', [(i, (i + by) % RING) for i in range(RING)])]
    sub x2 -> x0, other arithmetic: 19.4 us -> none  [backward_layer(): d_prob - jnp.sum(prob * d_prob, axis=-1, keepdims=True)]
    unnamed x396 -> x281, local copies, waits for them, and re-layouts: 59.1 us -> 41.1 us
    dot_general x8 -> x4, matrix products: 21.3 us -> 11.3 us  [inner_rows(): lax.dot_general(left, right, (((0,), (0,)), ((), ())), preferred_element_...]
    ppermute x16, waiting for transfers between devices: 14.8 us -> 24 us  [along_seq(): return lax.ppermute(x, ('section', 'y', 'x'), pairs)]
    all_to_all x2, starting transfers between devices: 28.9 us -> 21.5 us  [finish(): lax.all_to_all(split, ('y', 'x'), split_axis=0, concat_axis=0, tiled=True)]
    dot_general x12, matrix products: 23.6 us -> 16.3 us  [batched(): return jnp.einsum(spec, left, right, preferred_element_type=jnp.float32)]
  transfers between devices with their start and end apart: 53 -> 37, of which waited for: 16 -> 20; matrix products, arithmetic and copies ran while one was open for 30% -> 17% of each run, Pallas kernels for 2% -> 1%
where the time goes in v3:
time: 518 us; the launch traced here: 508 us
  waiting for transfers between devices  171 us (33%)
  starting transfers between devices  84.3 us (16%)
  matrix products  71.1 us (14%)
  local copies, waits for them, and re-layouts  66.1 us (13%)
  other arithmetic  62.9 us (12%)
  blocking collectives  23 us (4%)
  between operations  16.4 us (3%)
  Pallas kernels  13.6 us (3%)
    ppermute x16, waiting for transfers between devices, along_z(): return lax.ppermute(x, 'z', [(i, (i + by) % RING) for i in range(RING)])  101 us
    unnamed x281, local copies, waits for them, and re-layouts  41.1 us
    ppermute x16, starting transfers between devices, along_seq(): return lax.ppermute(x, ('section', 'y', 'x'), pairs)  30.4 us
    ppermute x16, starting transfers between devices, along_z(): return lax.ppermute(x, 'z', [(i, (i + by) % RING) for i in range(RING)])  29.2 us
    all_to_all x2, waiting for transfers between devices, finish(): lax.all_to_all(split, ('y', 'x'), split_axis=0, concat_axis=0, tiled=True)  26.1 us
    dot_general x8, matrix products, against(): lax.dot_general(left, right, (((1,), (1,)), ((), ())), preferred_element_...  24.7 us
    ppermute x16, waiting for transfers between devices, along_seq(): return lax.ppermute(x, ('section', 'y', 'x'), pairs)  24 us
    all_gather x1, blocking collectives, finish(): return lax.all_gather(summed, ('y', 'x'), axis=0, tiled=True)  23 us
  transfers between devices with their start and end apart: 37, of which 20 were waited for; matrix products, arithmetic and copies ran while one was open for 17% of the time, Pallas kernels for 1%

profile of v3, /device:TPU:0, one launch (start us, length us, event | category | flops | bytes accessed | tf_op | source)
XLA Modules:
  0.0 508.0 jit_solution(1892373036500498557)
XLA Ops:
  12.6 4.2 collective-permute-start
  18.2 22.9 %collective-permute-done.1.refs_2_ = bf16[256,1920]{1,0:T(8,128)(2,1)S(1)} collective-permute-done((bf16[256,1920]{1,0:T(8,128)(2,1)S(1)}, bf16[256,1920]{1,0:T(8,128)(2,1)S(1)}, u32[]{:S(2)}, u32[]{:S(2)}) %collective-permute-start.1) | collective-permute-done | bytes 983072 | tf_op jit(solution)/shard_map/ppermute | solution.py:183
  42.9 3.2 collective-permute-start.3
  48.7 6.6 %collective-permute-done.2.refs_3_ = bf16[128,1920]{1,0:T(8,128)(2,1)} collective-permute-done((bf16[128,1920]{1,0:T(8,128)(2,1)}, bf16[128,1920]{1,0:T(8,128)(2,1)}, u32[]{:S(2)}, u32[]{:S(2)}) %collective-permute-start.2) | collective-permute-done | bytes 491552 | tf_op jit(solution)/shard_map/ppermute | solution.py:183
  70.0 4.2 collective-permute-start.4
  74.2 5.4 %collective-permute-start.5 = (bf16[2,3,128,256]{3,2,1,0:T(8,128)(2,1)}, bf16[2,3,128,256]{3,2,1,0:T(8,128)(2,1)}, u32[]{:S(2)}, u32[]{:S(2)}) collective-permute-start(bf16[2,3,128,256]{3,2,1,0:T(8,128)(2,1)} %pad_maximum_fusion.20), channel_id=1, source_target_pairs={{0,12},{4,16},{8,20},{12,24},{16,28},{20,32},{24,36},{28,40},{32,4... | collective-permute-start | bytes 1179656 | tf_op jit(solution)/shard_map/ppermute | solution.py:191
  79.6 3.8 collective-permute-start.6
  84.6 3.7 collective-permute-start.8
  88.3 2.4 copy.76
  90.7 3.4 fusion.33
  96.0 2.8 collective-permute-start.7
  107.9 23.7 %collective-permute-done.9.refs_2_ = bf16[256,4096]{1,0:T(8,128)(2,1)} collective-permute-done((bf16[256,4096]{1,0:T(8,128)(2,1)S(1)}, bf16[256,4096]{1,0:T(8,128)(2,1)}, u32[]{:S(2)}, u32[]{:S(2)}) %collective-permute-start.9) | collective-permute-done | bytes 2097184 | tf_op jit(solution)/shard_map/ppermute | solution.py:183
  131.6 2.3 slice.289
  133.9 2.3 slice.290
  136.2 3.4 collective-permute-start.11
  143.5 2.0 multiply_reduce_fusion.19
  145.9 4.3 collective-permute-done.10.refs_3_
  150.2 2.0 collective-permute-done.11.refs_4_
  152.3 3.1 unpack_full.3
  155.4 2.7 fusion.199
  173.9 2.0 fusion.49
  175.9 2.9 reshape.501
  187.6 1.9 fusion.210
  189.5 1.9 copy-done.65
  194.9 2.7 fusion.200
  201.7 3.7 fusion.17
  205.4 2.8 multiply_reduce_fusion.6
  212.6 2.6 reshape.504
  215.2 3.7 multiply_reduce_fusion.1
  236.3 17.6 %collective-permute-done.21 = bf16[384,640]{1,0:T(8,128)(2,1)S(1)} collective-permute-done((bf16[384,640]{1,0:T(8,128)(2,1)S(1)}, bf16[384,640]{1,0:T(8,128)(2,1)S(1)}, u32[]{:S(2)}, u32[]{:S(2)}) %collective-permute-start.21) | collective-permute-done | bytes 491552 | tf_op jit(solution)/shard_map/ppermute | solution.py:508
  254.7 6.8 %fusion.10 = (bf16[384,2048]{1,0:T(8,128)(2,1)S(1)}, bf16[384,2048]{1,0:T(8,128)(2,1)S(1)}) fusion(f32[384,4096]{1,0:T(8,128)} %copy-done.27, bf16[384,640]{1,0:T(8,128)(2,1)S(1)} %fusion.57, bf16[2048,640]{1,0:T(8,128)(2,1)} %copy-done.19), kind=kOutput, calls=%fused_computation.32 | convolution fusion | flops 1025507328 | bytes 12550144 | tf_op jit(solution)/shard_map/dot_general | solution.py:259
  261.6 3.6 multiply_reduce_fusion.8
  265.2 4.3 convolution_convert_fusion.refs_0_
  271.4 3.7 pack_blocks.2
  275.2 3.8 collective-permute-start.23
  279.2 3.4 multiply_reduce_fusion.9
  282.7 1.8 multiply_convert_fusion.8
  286.3 2.1 convolution_convert_fusion.3.refs_1_
  288.3 14.4 %collective-permute-done.22.refs_1_ = bf16[128,4096]{1,0:T(8,128)(2,1)} collective-permute-done((bf16[128,4096]{1,0:T(8,128)(2,1)}, bf16[128,4096]{1,0:T(8,128)(2,1)}, u32[]{:S(2)}, u32[]{:S(2)}) %collective-permute-start.22) | collective-permute-done | bytes 1048608 | tf_op jit(solution)/shard_map/ppermute | solution.py:183
  302.7 2.1 reshape.506
  304.9 3.5 multiply_reduce_fusion
  313.7 2.8 add_dynamic-update-slice_fusion.1
  317.6 2.8 add_dynamic-update-slice_fusion
  320.4 2.1 collective-permute-start.29
  328.9 8.5 %collective-permute-done.27 = bf16[2,3,128,256]{3,2,1,0:T(8,128)(2,1)S(1)} collective-permute-done((bf16[2,3,128,256]{3,2,1,0:T(8,128)(2,1)S(1)}, bf16[2,3,128,256]{3,2,1,0:T(8,128)(2,1)S(1)}, u32[]{:S(2)}, u32[]{:S(2)}) %collective-permute-start.27) | collective-permute-done | bytes 393248 | tf_op jit(solution)/shard_map/ppermute | solution.py:191
  341.7 4.6 collective-permute-done.25
  346.3 9.0 %collective-permute-done.24 = bf16[2,3,128,256]{3,2,1,0:T(8,128)(2,1)} collective-permute-done((bf16[2,3,128,256]{3,2,1,0:T(8,128)(2,1)}, bf16[2,3,128,256]{3,2,1,0:T(8,128)(2,1)}, u32[]{:S(2)}, u32[]{:S(2)}) %collective-permute-start.24) | collective-permute-done | bytes 393248 | tf_op jit(solution)/shard_map/ppermute | solution.py:191
  359.9 5.3 %collective-permute-done.28.refs_1_ = bf16[256,4096]{1,0:T(8,128)(2,1)} collective-permute-done((bf16[256,4096]{1,0:T(8,128)(2,1)}, bf16[256,4096]{1,0:T(8,128)(2,1)}, u32[]{:S(2)}, u32[]{:S(2)}) %collective-permute-start.28) | collective-permute-done | bytes 2097184 | tf_op jit(solution)/shard_map/ppermute | solution.py:183
  365.2 2.1 collective-permute-done.29.refs_2_
  367.3 4.7 add_convert_fusion
  372.0 13.5 %all-to-all-start.1 = ((bf16[16,16,4096]{2,1,0:T(8,128)(2,1)}), bf16[16,16,4096]{2,1,0:T(8,128)(2,1)}, u32[]{:S(2)}, u32[]{:S(2)}) async-start(bf16[16,16,4096]{2,1,0:T(8,128)(2,1)} %bitcast.263), calls=%async_computation.1 | async-start | bytes 4194304 | tf_op jit(solution)/shard_map/all_to_all | solution.py:518
  389.8 3.4 fusion.77
  393.4 3.1 convolution_convert_fusion.2.refs_0_
  397.9 3.7 collective-permute-start.32
  401.6 12.9 %all-to-all-done.1 = bf16[16,16,4096]{2,1,0:T(8,128)(2,1)} async-done(((bf16[16,16,4096]{2,1,0:T(8,128)(2,1)}), bf16[16,16,4096]{2,1,0:T(8,128)(2,1)}, u32[]{:S(2)}, u32[]{:S(2)}) %all-to-all-start.1) | async-done | bytes 2097184 | tf_op jit(solution)/shard_map/all_to_all | solution.py:518
  414.5 2.6 reduce_sum.473
  418.4 3.8 collective-permute-start.33
  423.5 15.1 %collective-permute-done.33 = bf16[256,1920]{1,0:T(8,128)(2,1)S(1)} collective-permute-done((bf16[256,1920]{1,0:T(8,128)(2,1)S(1)}, bf16[256,1920]{1,0:T(8,128)(2,1)S(1)}, u32[]{:S(2)}, u32[]{:S(2)}) %collective-permute-start.33) | collective-permute-done | bytes 983072 | tf_op jit(solution)/shard_map/ppermute | solution.py:183
  438.6 4.7 collective-permute-done.31
  444.6 8.0 %all-to-all-start = ((bf16[16,16,1920]{2,1,0:T(8,128)(2,1)}), bf16[16,16,1920]{2,1,0:T(8,128)(2,1)}, u32[]{:S(2)}, u32[]{:S(2)}) async-start(bf16[16,16,1920]{2,1,0:T(8,128)(2,1)} %bitcast.264), calls=%async_computation | async-start | bytes 1966080 | tf_op jit(solution)/shard_map/all_to_all | solution.py:518
  454.6 2.7 fusion.76
  457.3 13.2 %all-to-all-done = bf16[16,16,1920]{2,1,0:T(8,128)(2,1)} async-done(((bf16[16,16,1920]{2,1,0:T(8,128)(2,1)}), bf16[16,16,1920]{2,1,0:T(8,128)(2,1)}, u32[]{:S(2)}, u32[]{:S(2)}) %all-to-all-start) | async-done | bytes 983072 | tf_op jit(solution)/shard_map/all_to_all | solution.py:518
  471.9 23.0 %all_gather.6.source = bf16[256,1920]{1,0:T(8,128)(2,1)S(1)} all-gather(bf16[16,1920]{1,0:T(8,128)(2,1)S(1)} %reduce_sum.472), channel_id=1, replica_groups=mesh['section'=2,'y'=4,'x'=4,'z'=4] {'y','x'}, dimensions={0}, use_global_device_ids=true | all-gather | bytes 1044480 | tf_op jit(solution)/shard_map/all_gather | solution.py:520
  498.8 2.1 unpack_grads.3
  (487 shorter events, 138.0 us)
Async XLA Ops:
  7.2 9.6 %copy-start.119 = (s32[3,1,2048]{2,1,0:T(1,128)S(1)}, s32[3,1,2048]{2,1,0:T(1,128)}, u32[]{:S(2)}) copy-start(s32[3,1,2048]{2,1,0:T(1,128)} %param.19) | copy-start | bytes 73732
  7.2 9.6 %copy-start.122 = (s32[3,1,128]{2,1,0:T(1,128)S(1)}, s32[3,1,128]{2,1,0:T(1,128)}, u32[]{:S(2)}) copy-start(s32[3,1,128]{2,1,0:T(1,128)} %param.18) | copy-start | bytes 4612
  12.6 29.5 %collective-permute-start = (bf16[256,1920]{1,0:T(8,128)(2,1)S(1)}, bf16[256,1920]{1,0:T(8,128)(2,1)S(1)}, u32[]{:S(2)}, u32[]{:S(2)}) collective-permute-start(bf16[256,1920]{1,0:T(8,128)(2,1)S(1)} %pack_shard.2.refs_0_), channel_id=1, source_target_pairs={{0,3},{1,0},{2,1},{3,2},{4,7},{5,4},{6,5},{7,6},{8,11},{9,8},{10,9... | collective-permute-start | bytes 2949128 | tf_op jit(solution)/shard_map/ppermute | solution.py:183
  16.7 24.4 %collective-permute-start.1 = (bf16[256,1920]{1,0:T(8,128)(2,1)S(1)}, bf16[256,1920]{1,0:T(8,128)(2,1)S(1)}, u32[]{:S(2)}, u32[]{:S(2)}) collective-permute-start(bf16[256,1920]{1,0:T(8,128)(2,1)S(1)} %pack_shard.2.refs_0_), channel_id=1, source_target_pairs={{0,1},{1,2},{2,3},{3,0},{4,5},{5,6},{6,7},{7,4},{8,9},{9,10},{10,1... | collective-permute-start | bytes 2949128 | tf_op jit(solution)/shard_map/ppermute | solution.py:183
  18.1 46.3 %copy-start.120 = (f32[384]{0:T(512)}, f32[384]{0:T(512)S(1)}, u32[]{:S(2)}) copy-start(f32[384]{0:T(512)S(1)} %get-tuple-element.165) | copy-start | bytes 4612
  41.2 14.3 %copy-start.4 = (bf16[256,1920]{1,0:T(8,128)(2,1)}, bf16[256,1920]{1,0:T(8,128)(2,1)S(1)}, u32[]{:S(2)}) copy-start(bf16[256,1920]{1,0:T(8,128)(2,1)S(1)} %collective-permute-done.1.refs_2_) | copy-start | bytes 2949124
  42.0 13.3 %collective-permute-start.2 = (bf16[128,1920]{1,0:T(8,128)(2,1)}, bf16[128,1920]{1,0:T(8,128)(2,1)}, u32[]{:S(2)}, u32[]{:S(2)}) collective-permute-start(bf16[128,1920]{1,0:T(8,128)(2,1)} %slice.274), channel_id=1, source_target_pairs={{0,1},{1,2},{2,3},{3,0},{4,5},{5,6},{6,7},{7,4},{8,9},{9,10},{10,1... | collective-permute-start | bytes 1474568 | tf_op jit(solution)/shard_map/ppermute | solution.py:183
  42.0 13.4 %copy-start.2 = (bf16[256,1920]{1,0:T(8,128)(2,1)}, bf16[256,1920]{1,0:T(8,128)(2,1)S(1)}, u32[]{:S(2)}) copy-start(bf16[256,1920]{1,0:T(8,128)(2,1)S(1)} %collective-permute-done.refs_1_) | copy-start | bytes 2949124
  42.9 12.6 %collective-permute-start.3 = (bf16[128,1920]{1,0:T(8,128)(2,1)}, bf16[128,1920]{1,0:T(8,128)(2,1)}, u32[]{:S(2)}, u32[]{:S(2)}) collective-permute-start(bf16[128,1920]{1,0:T(8,128)(2,1)} %slice.275), channel_id=1, source_target_pairs={{0,3},{1,0},{2,1},{3,2},{4,7},{5,4},{6,5},{7,6},{8,11},{9,8},{10,9... | collective-permute-start | bytes 1474568 | tf_op jit(solution)/shard_map/ppermute | solution.py:183
  68.0 16.7 %copy-start.44 = (f32[384,512]{1,0:T(8,128)}, f32[384,512]{1,0:T(8,128)S(1)}, u32[]{:S(2)}) copy-start(f32[384,512]{1,0:T(8,128)S(1)} %fusion.113) | copy-start | bytes 2359300
  68.0 15.4 %copy-start.82 = (bf16[384,256]{1,0:T(8,128)(2,1)}, bf16[384,256]{1,0:T(8,128)(2,1)S(1)}, u32[]{:S(2)}) copy-start(bf16[384,256]{1,0:T(8,128)(2,1)S(1)} %slice.470) | copy-start | bytes 589828
  68.2 15.2 %copy-start.8 = (bf16[640,1536]{1,0:T(8,128)(2,1)S(1)}, bf16[640,1536]{1,0:T(8,128)(2,1)}, u32[]{:S(2)}) copy-start(bf16[640,1536]{1,0:T(8,128)(2,1)} %copy-done.7) | copy-start | bytes 5898244
  68.3 16.4 %copy-start.117 = (f32[384]{0:T(512)}, f32[384]{0:T(512)S(1)}, u32[]{:S(2)}) copy-start(f32[384]{0:T(512)S(1)} %add_rsqrt_fusion.10) | copy-start | bytes 4612
  69.2 14.2 %copy-start.100 = (bf16[384,128]{1,0:T(8,128)(2,1)}, bf16[384,128]{1,0:T(8,128)(2,1)S(1)}, u32[]{:S(2)}) copy-start(bf16[384,128]{1,0:T(8,128)(2,1)S(1)} %get-tuple-element.154) | copy-start | bytes 294916
  70.0 26.0 %collective-permute-start.4 = (bf16[2,3,128,256]{3,2,1,0:T(8,128)(2,1)}, bf16[2,3,128,256]{3,2,1,0:T(8,128)(2,1)}, u32[]{:S(2)}, u32[]{:S(2)}) collective-permute-start(bf16[2,3,128,256]{3,2,1,0:T(8,128)(2,1)} %pad_maximum_fusion.20), channel_id=1, source_target_pairs={{0,16},{4,20},{8,24},{12,28},{16,32},{20,36},{24,40},{28,44},{32,4... | collective-permute-start | bytes 1179656 | tf_op jit(solution)/shard_map/ppermute | solution.py:191
  74.2 26.3 %collective-permute-start.5 = (bf16[2,3,128,256]{3,2,1,0:T(8,128)(2,1)}, bf16[2,3,128,256]{3,2,1,0:T(8,128)(2,1)}, u32[]{:S(2)}, u32[]{:S(2)}) collective-permute-start(bf16[2,3,128,256]{3,2,1,0:T(8,128)(2,1)} %pad_maximum_fusion.20), channel_id=1, source_target_pairs={{0,12},{4,16},{8,20},{12,24},{16,28},{20,32},{24,36},{28,40},{32,4... | collective-permute-start | bytes 1179656 | tf_op jit(solution)/shard_map/ppermute | solution.py:191
  79.6 22.0 %collective-permute-start.6 = (bf16[2,3,128,256]{3,2,1,0:T(8,128)(2,1)}, bf16[2,3,128,256]{3,2,1,0:T(8,128)(2,1)}, u32[]{:S(2)}, u32[]{:S(2)}) collective-permute-start(bf16[2,3,128,256]{3,2,1,0:T(8,128)(2,1)} %pad_maximum_fusion.20), channel_id=1, source_target_pairs={{0,8},{4,12},{8,16},{12,20},{16,24},{20,28},{24,32},{28,36},{32,40... | collective-permute-start | bytes 1179656 | tf_op jit(solution)/shard_map/ppermute | solution.py:191
  84.6 49.3 %collective-permute-start.8 = (bf16[256,4096]{1,0:T(8,128)(2,1)S(1)}, bf16[256,4096]{1,0:T(8,128)(2,1)}, u32[]{:S(2)}, u32[]{:S(2)}) collective-permute-start(bf16[256,4096]{1,0:T(8,128)(2,1)S(1)} %pack_shard.3.refs_5_.refs_0_), channel_id=1, source_target_pairs={{0,3},{1,0},{2,1},{3,2},{4,7},{5,4},{6,5},{7,6},{8,11},{9,8},{10,9... | collective-permute-start | bytes 6291464 | tf_op jit(solution)/shard_map/ppermute | solution.py:183
  88.3 43.3 %collective-permute-start.9 = (bf16[256,4096]{1,0:T(8,128)(2,1)S(1)}, bf16[256,4096]{1,0:T(8,128)(2,1)}, u32[]{:S(2)}, u32[]{:S(2)}) collective-permute-start(bf16[256,4096]{1,0:T(8,128)(2,1)S(1)} %pack_shard.3.refs_5_.refs_0_), channel_id=1, source_target_pairs={{0,1},{1,2},{2,3},{3,0},{4,5},{5,6},{6,7},{7,4},{8,9},{9,10},{10,1... | collective-permute-start | bytes 6291464 | tf_op jit(solution)/shard_map/ppermute | solution.py:183
  96.0 7.7 %collective-permute-start.7 = (bf16[2,3,128,256]{3,2,1,0:T(8,128)(2,1)}, bf16[2,3,128,256]{3,2,1,0:T(8,128)(2,1)}, u32[]{:S(2)}, u32[]{:S(2)}) collective-permute-start(bf16[2,3,128,256]{3,2,1,0:T(8,128)(2,1)} %pad_maximum_fusion.20), channel_id=1, source_target_pairs={{0,4},{4,8},{8,12},{12,16},{16,20},{20,24},{24,28},{28,32},{32,36}... | collective-permute-start | bytes 1179656 | tf_op jit(solution)/shard_map/ppermute | solution.py:191
  104.8 34.9 %copy-start.96 = (bf16[2,3,640,256]{3,2,1,0:T(8,128)(2,1)}, bf16[2,3,640,256]{3,2,1,0:T(8,128)(2,1)S(1)}, u32[]{:S(2)}) copy-start(bf16[2,3,640,256]{3,2,1,0:T(8,128)(2,1)S(1)} %constant_dynamic-update-slice_fusion) | copy-start | bytes 5898244
  107.9 31.7 %copy-start.63 = (f32[3,4,128,640]{3,2,1,0:T(8,128)}, f32[3,4,128,640]{3,2,1,0:T(8,128)S(1)}, u32[]{:S(2)}) copy-start(f32[3,4,128,640]{3,2,1,0:T(8,128)S(1)} %get-tuple-element.169) | copy-start | bytes 11796484
  107.9 31.7 %copy-start.123 = (f32[3,4,128]{2,1,0:T(4,128)}, f32[3,4,128]{2,1,0:T(4,128)S(1)}, u32[]{:S(2)}) copy-start(f32[3,4,128]{2,1,0:T(4,128)S(1)} %get-tuple-element.168) | copy-start | bytes 18436
  133.9 16.3 %collective-permute-start.10 = (bf16[128,4096]{1,0:T(8,128)(2,1)}, bf16[128,4096]{1,0:T(8,128)(2,1)}, u32[]{:S(2)}, u32[]{:S(2)}) collective-permute-start(bf16[128,4096]{1,0:T(8,128)(2,1)} %slice.289), channel_id=1, source_target_pairs={{0,1},{1,2},{2,3},{3,0},{4,5},{5,6},{6,7},{7,4},{8,9},{9,10},{10,1... | collective-permute-start | bytes 3145736 | tf_op jit(solution)/shard_map/ppermute | solution.py:183
  136.2 16.1 %collective-permute-start.11 = (bf16[128,4096]{1,0:T(8,128)(2,1)}, bf16[128,4096]{1,0:T(8,128)(2,1)}, u32[]{:S(2)}, u32[]{:S(2)}) collective-permute-start(bf16[128,4096]{1,0:T(8,128)(2,1)} %slice.290), channel_id=1, source_target_pairs={{0,3},{1,0},{2,1},{3,2},{4,7},{5,4},{6,5},{7,6},{8,11},{9,8},{10,9... | collective-permute-start | bytes 3145736 | tf_op jit(solution)/shard_map/ppermute | solution.py:183
  145.5 9.9 %copy-start.38 = (f32[384,640]{1,0:T(8,128)}, f32[384,640]{1,0:T(8,128)S(1)}, u32[]{:S(2)}) copy-start(f32[384,640]{1,0:T(8,128)S(1)} %get-tuple-element.171) | copy-start | bytes 2949124
  145.9 15.3 %copy-start.29 = (f32[384,640]{1,0:T(8,128)}, f32[384,640]{1,0:T(8,128)S(1)}, u32[]{:S(2)}) copy-start(f32[384,640]{1,0:T(8,128)S(1)} %get-tuple-element.126) | copy-start | bytes 2949124
  161.4 3.0 collective-permute-start.12
  164.5 228.9 %copy-start.51 = (bf16[384,640]{1,0:T(8,128)(2,1)}, bf16[384,640]{1,0:T(8,128)(2,1)S(1)}, u32[]{:S(2)}) copy-start(bf16[384,640]{1,0:T(8,128)(2,1)S(1)} %collective-permute-done.12) | copy-start | bytes 1474564
  167.8 14.0 %collective-permute-start.13 = (bf16[2,3,128,256]{3,2,1,0:T(8,128)(2,1)}, bf16[2,3,128,256]{3,2,1,0:T(8,128)(2,1)}, u32[]{:S(2)}, u32[]{:S(2)}) collective-permute-start(bf16[2,3,128,256]{3,2,1,0:T(8,128)(2,1)} %pad_maximum_fusion.21), channel_id=1, source_target_pairs={{64,80},{68,84},{72,88},{76,92},{80,96},{84,100},{88,104},{92,108}... | collective-permute-start | bytes 1179656 | tf_op jit(solution)/shard_map/ppermute | solution.py:191
  169.2 13.9 %collective-permute-start.14 = (bf16[2,3,128,256]{3,2,1,0:T(8,128)(2,1)}, bf16[2,3,128,256]{3,2,1,0:T(8,128)(2,1)}, u32[]{:S(2)}, u32[]{:S(2)}) collective-permute-start(bf16[2,3,128,256]{3,2,1,0:T(8,128)(2,1)} %pad_maximum_fusion.21), channel_id=1, source_target_pairs={{64,76},{68,80},{72,84},{76,88},{80,92},{84,96},{88,100},{92,104},... | collective-permute-start | bytes 1179656 | tf_op jit(solution)/shard_map/ppermute | solution.py:191
  170.7 13.6 %collective-permute-start.15 = (bf16[2,3,128,256]{3,2,1,0:T(8,128)(2,1)}, bf16[2,3,128,256]{3,2,1,0:T(8,128)(2,1)}, u32[]{:S(2)}, u32[]{:S(2)}) collective-permute-start(bf16[2,3,128,256]{3,2,1,0:T(8,128)(2,1)} %pad_maximum_fusion.21), channel_id=1, source_target_pairs={{64,72},{68,76},{72,80},{76,84},{80,88},{84,92},{88,96},{92,100},{... | collective-permute-start | bytes 1179656 | tf_op jit(solution)/shard_map/ppermute | solution.py:191
  172.1 13.2 %collective-permute-start.16 = (bf16[2,3,128,256]{3,2,1,0:T(8,128)(2,1)}, bf16[2,3,128,256]{3,2,1,0:T(8,128)(2,1)}, u32[]{:S(2)}, u32[]{:S(2)}) collective-permute-start(bf16[2,3,128,256]{3,2,1,0:T(8,128)(2,1)} %pad_maximum_fusion.21), channel_id=1, source_target_pairs={{64,68},{68,72},{72,76},{76,80},{80,84},{84,88},{88,92},{92,96},{9... | collective-permute-start | bytes 1179656 | tf_op jit(solution)/shard_map/ppermute | solution.py:191
  194.9 13.3 %copy-start.31 = (f32[384,640]{1,0:T(8,128)}, f32[384,640]{1,0:T(8,128)S(1)}, u32[]{:S(2)}) copy-start(f32[384,640]{1,0:T(8,128)S(1)} %get-tuple-element.124) | copy-start | bytes 2949124
  224.4 5.9 %collective-permute-start.20 = (bf16[2,3,128,256]{3,2,1,0:T(8,128)(2,1)S(1)}, bf16[2,3,128,256]{3,2,1,0:T(8,128)(2,1)S(1)}, u32[]{:S(2)}, u32[]{:S(2)}) collective-permute-start(bf16[2,3,128,256]{3,2,1,0:T(8,128)(2,1)S(1)} %get-tuple-element.140), channel_id=1, source_target_pairs={{68,64},{72,68},{76,72},{80,76},{84,80},{88,84},{92,88},{96,92},{1... | collective-permute-start | bytes 1179656 | tf_op jit(solution)/shard_map/ppermute | solution.py:191
  225.2 5.1 collective-permute-start.19
  225.9 4.4 collective-permute-start.18
  226.6 3.7 collective-permute-start.17
  233.5 20.4 %copy-start.41 = (f32[384,640]{1,0:T(8,128)S(1)}, f32[384,640]{1,0:T(8,128)}, u32[]{:S(2)}) copy-start(f32[384,640]{1,0:T(8,128)} %copy-done.40) | copy-start | bytes 2949124
  234.5 19.5 %collective-permute-start.21 = (bf16[384,640]{1,0:T(8,128)(2,1)S(1)}, bf16[384,640]{1,0:T(8,128)(2,1)S(1)}, u32[]{:S(2)}, u32[]{:S(2)}) collective-permute-start(bf16[384,640]{1,0:T(8,128)(2,1)S(1)} %fusion.204), channel_id=1, source_target_pairs={{64,0},{65,1},{66,2},{67,3},{68,4},{69,5},{70,6},{71,7},{72,8},{73... | collective-permute-start | bytes 1474568 | tf_op jit(solution)/shard_map/ppermute | solution.py:508
  275.2 27.6 %collective-permute-start.22 = (bf16[128,4096]{1,0:T(8,128)(2,1)}, bf16[128,4096]{1,0:T(8,128)(2,1)}, u32[]{:S(2)}, u32[]{:S(2)}) collective-permute-start(bf16[128,4096]{1,0:T(8,128)(2,1)} %get-tuple-element.43), channel_id=1, source_target_pairs={{0,1},{1,2},{2,3},{3,0},{4,5},{5,6},{6,7},{7,4},{8,9},{9,10},{10,1... | collective-permute-start | bytes 3145736 | tf_op jit(solution)/shard_map/ppermute | solution.py:183
  275.2 27.5 %collective-permute-start.23 = (bf16[128,4096]{1,0:T(8,128)(2,1)}, bf16[128,4096]{1,0:T(8,128)(2,1)}, u32[]{:S(2)}, u32[]{:S(2)}) collective-permute-start(bf16[128,4096]{1,0:T(8,128)(2,1)} %get-tuple-element.44), channel_id=1, source_target_pairs={{0,3},{1,0},{2,1},{3,2},{4,7},{5,4},{6,5},{7,6},{8,11},{9,8},{10,9... | collective-permute-start | bytes 3145736 | tf_op jit(solution)/shard_map/ppermute | solution.py:183
  288.3 16.5 %copy-start.124 = (f32[3,4,128]{2,1,0:T(4,128)S(1)}, f32[3,4,128]{2,1,0:T(4,128)}, u32[]{:S(2)}) copy-start(f32[3,4,128]{2,1,0:T(4,128)} %copy-done.123) | copy-start | bytes 18436
  309.7 12.9 %copy-start.46 = (f32[1,3,640,256]{3,2,1,0:T(8,128)}, f32[1,3,640,256]{3,2,1,0:T(8,128)S(1)}, u32[]{:S(2)}) copy-start(f32[1,3,640,256]{3,2,1,0:T(8,128)S(1)} %convolution_bitcast_fusion) | copy-start | bytes 5898244
  312.9 9.6 %copy-start.28 = (f32[1,3,640,256]{3,2,1,0:T(8,128)}, f32[1,3,640,256]{3,2,1,0:T(8,128)S(1)}, u32[]{:S(2)}) copy-start(f32[1,3,640,256]{3,2,1,0:T(8,128)S(1)} %fusion.24) | copy-start | bytes 5898244
  316.5 48.7 %collective-permute-start.28 = (bf16[256,4096]{1,0:T(8,128)(2,1)}, bf16[256,4096]{1,0:T(8,128)(2,1)}, u32[]{:S(2)}, u32[]{:S(2)}) collective-permute-start(bf16[256,4096]{1,0:T(8,128)(2,1)} %add_dynamic-update-slice_fusion.1), channel_id=1, source_target_pairs={{0,1},{1,2},{2,3},{3,0},{4,5},{5,6},{6,7},{7,4},{8,9},{9,10},{10,1... | collective-permute-start | bytes 6291464 | tf_op jit(solution)/shard_map/ppermute | solution.py:183
  320.4 46.9 %collective-permute-start.29 = (bf16[256,4096]{1,0:T(8,128)(2,1)}, bf16[256,4096]{1,0:T(8,128)(2,1)}, u32[]{:S(2)}, u32[]{:S(2)}) collective-permute-start(bf16[256,4096]{1,0:T(8,128)(2,1)} %add_dynamic-update-slice_fusion), channel_id=1, source_target_pairs={{0,3},{1,0},{2,1},{3,2},{4,7},{5,4},{6,5},{7,6},{8,11},{9,8},{10,9... | collective-permute-start | bytes 6291464 | tf_op jit(solution)/shard_map/ppermute | solution.py:183
  324.0 13.5 %collective-permute-start.27 = (bf16[2,3,128,256]{3,2,1,0:T(8,128)(2,1)S(1)}, bf16[2,3,128,256]{3,2,1,0:T(8,128)(2,1)S(1)}, u32[]{:S(2)}, u32[]{:S(2)}) collective-permute-start(bf16[2,3,128,256]{3,2,1,0:T(8,128)(2,1)S(1)} %get-tuple-element.134), channel_id=1, source_target_pairs={{4,0},{8,4},{12,8},{16,12},{20,16},{24,20},{28,24},{32,28},{36,32}... | collective-permute-start | bytes 1179656 | tf_op jit(solution)/shard_map/ppermute | solution.py:191
  325.4 16.3 %collective-permute-start.26 = (bf16[2,3,128,256]{3,2,1,0:T(8,128)(2,1)}, bf16[2,3,128,256]{3,2,1,0:T(8,128)(2,1)}, u32[]{:S(2)}, u32[]{:S(2)}) collective-permute-start(bf16[2,3,128,256]{3,2,1,0:T(8,128)(2,1)} %get-tuple-element.135), channel_id=1, source_target_pairs={{8,0},{12,4},{16,8},{20,12},{24,16},{28,20},{32,24},{36,28},{40,32... | collective-permute-start | bytes 1179656 | tf_op jit(solution)/shard_map/ppermute | solution.py:191
  326.7 19.7 %collective-permute-start.25 = (bf16[2,3,128,256]{3,2,1,0:T(8,128)(2,1)}, bf16[2,3,128,256]{3,2,1,0:T(8,128)(2,1)}, u32[]{:S(2)}, u32[]{:S(2)}) collective-permute-start(bf16[2,3,128,256]{3,2,1,0:T(8,128)(2,1)} %get-tuple-element.136), channel_id=1, source_target_pairs={{12,0},{16,4},{20,8},{24,12},{28,16},{32,20},{36,24},{40,28},{44,3... | collective-permute-start | bytes 1179656 | tf_op jit(solution)/shard_map/ppermute | solution.py:191
  337.4 17.9 %collective-permute-start.24 = (bf16[2,3,128,256]{3,2,1,0:T(8,128)(2,1)}, bf16[2,3,128,256]{3,2,1,0:T(8,128)(2,1)}, u32[]{:S(2)}, u32[]{:S(2)}) collective-permute-start(bf16[2,3,128,256]{3,2,1,0:T(8,128)(2,1)} %get-tuple-element.133), channel_id=1, source_target_pairs={{16,0},{20,4},{24,8},{28,12},{32,16},{36,20},{40,24},{44,28},{48,3... | collective-permute-start | bytes 1179656 | tf_op jit(solution)/shard_map/ppermute | solution.py:191
  341.0 18.6 %copy-start.45 = (f32[384,512]{1,0:T(8,128)S(1)}, f32[384,512]{1,0:T(8,128)}, u32[]{:S(2)}) copy-start(f32[384,512]{1,0:T(8,128)} %copy-done.44) | copy-start | bytes 2359300
  341.0 18.6 %copy-start.118 = (f32[384]{0:T(512)S(1)}, f32[384]{0:T(512)}, u32[]{:S(2)}) copy-start(f32[384]{0:T(512)} %copy-done.117) | copy-start | bytes 4612
  372.0 14.8 %copy-start.87 = (f32[384,128]{1,0:T(8,128)S(1)}, f32[384,128]{1,0:T(8,128)}, u32[]{:S(2)}) copy-start(f32[384,128]{1,0:T(8,128)} %copy-done.86) | copy-start | bytes 589828
  372.0 14.8 %copy-start.89 = (f32[384,128]{1,0:T(8,128)S(1)}, f32[384,128]{1,0:T(8,128)}, u32[]{:S(2)}) copy-start(f32[384,128]{1,0:T(8,128)} %copy-done.88) | copy-start | bytes 589828
  372.0 15.0 %copy-start.75 = (bf16[48,8,4,256]{3,1,2,0:T(8,128)(2,1)S(1)}, bf16[48,8,4,256]{3,1,2,0:T(8,128)(2,1)}, u32[]{:S(2)}) copy-start(bf16[48,8,4,256]{3,1,2,0:T(8,128)(2,1)} %copy.83) | copy-start | bytes 2359300
  372.0 42.5 %all-to-all-start.1 = ((bf16[16,16,4096]{2,1,0:T(8,128)(2,1)}), bf16[16,16,4096]{2,1,0:T(8,128)(2,1)}, u32[]{:S(2)}, u32[]{:S(2)}) async-start(bf16[16,16,4096]{2,1,0:T(8,128)(2,1)} %bitcast.263), calls=%async_computation.1 | async-start | bytes 4194304 | tf_op jit(solution)/shard_map/all_to_all | solution.py:518
  385.5 111.7 %all-gather.2.cloned.1.call-start = ((), (), s32[]{:S(2)}) async-start(), calls=%async_computation.2 | async-start | bytes 2228224 | tf_op jit(solution)/shard_map/all_gather | solution.py:520
  397.9 19.2 %collective-permute-start.32 = (bf16[128,1920]{1,0:T(8,128)(2,1)}, bf16[128,1920]{1,0:T(8,128)(2,1)}, u32[]{:S(2)}, u32[]{:S(2)}) collective-permute-start(bf16[128,1920]{1,0:T(8,128)(2,1)} %get-tuple-element.51), channel_id=1, source_target_pairs={{0,3},{1,0},{2,1},{3,2},{4,7},{5,4},{6,5},{7,6},{8,11},{9,8},{10,9... | collective-permute-start | bytes 1474568 | tf_op jit(solution)/shard_map/ppermute | solution.py:183
  401.6 20.5 %collective-permute-start.30 = (bf16[128,1920]{1,0:T(8,128)(2,1)S(1)}, bf16[128,1920]{1,0:T(8,128)(2,1)}, u32[]{:S(2)}, u32[]{:S(2)}) collective-permute-start(bf16[128,1920]{1,0:T(8,128)(2,1)S(1)} %get-tuple-element.49), channel_id=1, source_target_pairs={{0,1},{1,2},{2,3},{3,0},{4,5},{5,6},{6,7},{7,4},{8,9},{9,10},{10,1... | collective-permute-start | bytes 1474568 | tf_op jit(solution)/shard_map/ppermute | solution.py:183
  418.4 20.2 %collective-permute-start.33 = (bf16[256,1920]{1,0:T(8,128)(2,1)S(1)}, bf16[256,1920]{1,0:T(8,128)(2,1)S(1)}, u32[]{:S(2)}, u32[]{:S(2)}) collective-permute-start(bf16[256,1920]{1,0:T(8,128)(2,1)S(1)} %add_dynamic-update-slice_fusion.2), channel_id=1, source_target_pairs={{0,3},{1,0},{2,1},{3,2},{4,7},{5,4},{6,5},{7,6},{8,11},{9,8},{10,9... | collective-permute-start | bytes 2949128 | tf_op jit(solution)/shard_map/ppermute | solution.py:183
  423.4 19.9 %collective-permute-start.31 = (bf16[256,1920]{1,0:T(8,128)(2,1)S(1)}, bf16[256,1920]{1,0:T(8,128)(2,1)S(1)}, u32[]{:S(2)}, u32[]{:S(2)}) collective-permute-start(bf16[256,1920]{1,0:T(8,128)(2,1)S(1)} %add_dynamic-update-slice_fusion.3), channel_id=1, source_target_pairs={{0,1},{1,2},{2,3},{3,0},{4,5},{5,6},{6,7},{7,4},{8,9},{9,10},{10,1... | collective-permute-start | bytes 2949128 | tf_op jit(solution)/shard_map/ppermute | solution.py:183
  443.3 10.4 %copy-start.62 = (f32[384,640]{1,0:T(8,128)S(1)}, f32[384,640]{1,0:T(8,128)}, u32[]{:S(2)}) copy-start(f32[384,640]{1,0:T(8,128)} %copy-done.61) | copy-start | bytes 2949124
  444.6 26.0 %all-to-all-start = ((bf16[16,16,1920]{2,1,0:T(8,128)(2,1)}), bf16[16,16,1920]{2,1,0:T(8,128)(2,1)}, u32[]{:S(2)}, u32[]{:S(2)}) async-start(bf16[16,16,1920]{2,1,0:T(8,128)(2,1)} %bitcast.264), calls=%async_computation | async-start | bytes 1966080 | tf_op jit(solution)/shard_map/all_to_all | solution.py:518
  (106 other events, 309.3 us)
Sparse Core Ops, SparseCore 0:
  417.3 50.9 all-gather.1
